TPU v7x, 32 devices: a whole 2x2x4 slice. The times are simulated.
32 devices in a mesh: kv: 2 (over x), seq: 4 (over z), vocab: 4 (over y, core).
Axes of the slice: x: 2, y: 2, z: 4, core: 2. Of those that a mesh axis runs over, the one named last changes fastest.
Arguments:
- hidden_state: bfloat16 [48, 4, 3584], P('kv', 'vocab', 'seq'), may hold values from -6 to 6
- input_projection: bfloat16 [3584, 8, 1024], P('seq', 'kv'), may hold values from -0.09375 to 0.09375
- output_projection: bfloat16 [8, 512, 3584], P('kv', None, 'seq'), may hold values from -0.09375 to 0.09375
- norm_pre_attention: float32 [3584], P('seq'), may hold values from 0.1 to 1.9
- norm_post_attention: float32 [3584], P('seq'), may hold values from 0.1 to 1.9
- norm_pre_feedforward: float32 [3584], P('seq'), may hold values from 0.1 to 1.9
- norm_post_feedforward: float32 [3584], P('seq'), may hold values from 0.1 to 1.9
- norm_final: float32 [3584], P('seq'), may hold values from 0.1 to 1.9
- cache_keys: bfloat16 [4, 8192, 8, 256], P('vocab', 'seq', 'kv')
- cache_values: bfloat16 [4, 8192, 8, 256], P('vocab', 'seq', 'kv')
- cache_length: int32 [4], P('vocab'), may hold values from 1 to 8187, as said below
- ancestors: int32 [4, 48, 48], P('vocab'), may hold values from 0 to 1, as said below
- accepted_path: int32 [4, 5], P('vocab'), may hold values from 0 to 47, as said below
- gate_up_weight: bfloat16 [3584, 2, 14336], P('seq', None, ('kv', 'vocab')), may hold values from -0.09375 to 0.09375
- down_weight: bfloat16 [14336, 3584], P(('kv', 'vocab'), 'seq'), may hold values from -0.046875 to 0.046875
- draft_weight: bfloat16 [4, 3584, 3584], P(None, 'seq', ('kv', 'vocab')), may hold values from -0.09375 to 0.09375
- draft_bias: float32 [4, 3584], P(None, ('kv', 'vocab')), may hold values from -3 to 3
- vocab_weight: bfloat16 [16384, 3584], P(('kv', 'seq', 'vocab'))
- candidate_tokens: int32 [5, 48, 4, 8], replicated, may hold values from 0 to 16383
Outputs:
- keys_updated: bfloat16 [4, 8192, 8, 256], P('vocab', 'seq', 'kv')
- values_updated: bfloat16 [4, 8192, 8, 256], P('vocab', 'seq', 'kv')
- log_normalizer: float32 [5, 48, 4], replicated
- candidate_logits: float32 [5, 48, 4, 8], replicated
Inputs may be any that keep to these rules, and one draw needn't show every extreme that they name: The first cache_length[k] slots of tenant k's cache are filled; in every draw some tenant holds exactly 8187. ancestors[k, t, u] is 1 exactly when u is t or an ancestor of t in tenant k's tree; node 0 is the root and every parent has a lower index than its child. accepted_path[k] lists 5 nodes of tenant k's tree from the root down, each the parent of the next; the last of them is node 47.
All inputs are finite; a program needn't handle non-finite values.
Results may differ from a plain program's by a relative error of at most 0.02.
Values may be sent and summed in bfloat16 or wider, within the bound.
No kernel may reach another device: no remote copies, remote signals or barrier semaphores. Data moves between devices by JAX's collectives and lax.ppermute only.
A program may use at most 128 MiB of HBM per device.

v0:
```python
import jax
import jax.numpy as jnp
from jax import lax
from jax.sharding import PartitionSpec as P

MODEL_WIDTH = 3584
HEAD_SIZE = 256
CAND = 8


EPSILON = 1e-06
SCORE_CAP = 50.0
LOGIT_CAP = 30.0


def apply_rotary(vectors, token_positions):
    half_dim = vectors.shape[-1] // 2
    frequency = 10000.0 ** (-2.0 * jnp.arange(half_dim, dtype=jnp.float32) / vectors.shape[-1])
    angles = token_positions.astype(jnp.float32)[..., None] * frequency
    cosine = jnp.cos(angles)
    sine_part = jnp.sin(angles)
    first_half = vectors[..., :half_dim]
    second_half = vectors[..., half_dim:]
    return jnp.concatenate(
        [
            first_half * cosine - second_half * sine_part,
            second_half * cosine + first_half * sine_part,
        ],
        axis=-1,
    )


def capped_weight(scores):
    return jnp.exp(SCORE_CAP * jnp.tanh(scores * 0.0625 / SCORE_CAP))


def row_inverse(values):
    totals = lax.psum(jnp.sum(values * values, axis=-1), "seq")
    return lax.rsqrt(totals / MODEL_WIDTH + EPSILON)[:, None]


def gated_units(gate_up, squares):
    inverse = lax.rsqrt(squares / MODEL_WIDTH + EPSILON)[:, None]
    return (
        jax.nn.gelu(gate_up[:, 0] * inverse, approximate=True) * (gate_up[:, 1] * inverse)
    ).astype(jnp.bfloat16)


def local(
    hidden_state,
    input_projection,
    output_projection,
    norm_pre_attention,
    norm_post_attention,
    norm_pre_feedforward,
    norm_post_feedforward,
    norm_final,
    cache_keys,
    cache_values,
    cache_length,
    ancestors,
    accepted_path,
    gate_up_weight,
    down_weight,
    draft_weight,
    draft_bias,
    vocab_weight,
    candidate_tokens,
):
    tok_block = hidden_state.shape[0]
    kv_count = lax.axis_size("kv")
    tenants = lax.axis_size("vocab")
    tree_size = tok_block * kv_count
    own_state = hidden_state[:, 0, :]
    tenant_state = lax.all_gather(own_state, "kv", axis=0, tiled=True)
    tenant_float = tenant_state.astype(jnp.float32)
    scaled_input = (tenant_float * norm_pre_attention).astype(jnp.bfloat16)
    projected_rows = jnp.einsum(
        "td,dhc->thc", scaled_input, input_projection, preferred_element_type=jnp.float32
    )
    projected_rows, squares = lax.psum(
        (projected_rows, jnp.sum(tenant_float * tenant_float, axis=-1)), "seq"
    )
    projected_rows = projected_rows * lax.rsqrt(squares / MODEL_WIDTH + EPSILON)[:, None, None]
    head_count = projected_rows.shape[1]
    depths = jnp.sum(ancestors[0], axis=-1) - 1
    length = cache_length[0]
    token_positions = length + depths
    query_rows = apply_rotary(
        projected_rows[:, :, : 2 * HEAD_SIZE].reshape(tree_size, head_count, 2, HEAD_SIZE),
        token_positions[:, None, None],
    ).astype(jnp.bfloat16)
    new_keys = apply_rotary(
        projected_rows[:, :, 2 * HEAD_SIZE : 3 * HEAD_SIZE], token_positions[:, None]
    ).astype(jnp.bfloat16)
    new_values = projected_rows[:, :, 3 * HEAD_SIZE :].astype(jnp.bfloat16)
    block_size = cache_keys.shape[1]
    block_start = lax.axis_index("seq") * block_size
    cache_cells = block_start + jnp.arange(block_size, dtype=jnp.int32)
    scores = jnp.einsum(
        "thgc,shc->thgs", query_rows, cache_keys[0], preferred_element_type=jnp.float32
    )
    weights = jnp.where((cache_cells < length)[None, None, None, :], capped_weight(scores), 0.0)
    numerator = jnp.einsum(
        "thgs,shc->thgc",
        weights.astype(jnp.bfloat16),
        cache_values[0],
        preferred_element_type=jnp.float32,
    )
    numerator, denominator = lax.psum((numerator, jnp.sum(weights, axis=-1)), "seq")
    tree_scores = jnp.einsum(
        "thgc,uhc->thgu", query_rows, new_keys, preferred_element_type=jnp.float32
    )
    tree_weights = jnp.where(ancestors[0][:, None, None, :] > 0, capped_weight(tree_scores), 0.0)
    numerator = numerator + jnp.einsum(
        "thgu,uhc->thgc",
        tree_weights.astype(jnp.bfloat16),
        new_values,
        preferred_element_type=jnp.float32,
    )
    denominator = denominator + jnp.sum(tree_weights, axis=-1)
    attended = (
        (numerator / denominator[..., None])
        .astype(jnp.bfloat16)
        .reshape(tree_size, head_count * 2 * HEAD_SIZE)
    )
    out_matrix = output_projection.reshape(head_count * 2 * HEAD_SIZE, output_projection.shape[2])
    attention_out = lax.psum_scatter(
        jnp.dot(attended, out_matrix, preferred_element_type=jnp.float32),
        "kv",
        scatter_dimension=0,
        tiled=True,
    )
    first_sum = (
        own_state.astype(jnp.float32)
        + attention_out * row_inverse(attention_out) * norm_post_attention
    ).astype(jnp.bfloat16)
    all_state = lax.all_gather(first_sum, ("kv", "vocab"), axis=0, tiled=True)
    all_float = all_state.astype(jnp.float32)
    scaled_ffn = (all_float * norm_pre_feedforward).astype(jnp.bfloat16)
    gate_up = jnp.einsum(
        "td,dcf->tcf", scaled_ffn, gate_up_weight, preferred_element_type=jnp.float32
    )
    ffn_squares = jnp.sum(all_float * all_float, axis=-1)
    gate_up, ffn_squares = lax.psum((gate_up, ffn_squares), "seq")
    activated = gated_units(gate_up, ffn_squares)
    ffn_out = lax.psum_scatter(
        jnp.dot(activated, down_weight, preferred_element_type=jnp.float32),
        ("kv", "vocab"),
        scatter_dimension=0,
        tiled=True,
    )
    first_float = first_sum.astype(jnp.float32)
    second_sum = (first_float + ffn_out * row_inverse(ffn_out) * norm_post_feedforward).astype(
        jnp.bfloat16
    )
    second_float = second_sum.astype(jnp.float32)
    normed = (second_float * row_inverse(second_float) * norm_final).astype(jnp.bfloat16)
    gathered = lax.all_gather(normed, ("kv", "vocab"), axis=0, tiled=True)
    lifted = jnp.einsum("td,ndc->tnc", gathered, draft_weight, preferred_element_type=jnp.float32)
    lifted = lax.psum(lifted.astype(jnp.bfloat16), "seq").astype(jnp.float32)
    branch = jax.nn.silu(lifted + draft_bias).astype(jnp.bfloat16)
    row_count = gathered.shape[0]
    vocab_rows = vocab_weight.shape[0]
    draft_count = branch.shape[1]
    columns = vocab_weight
    base_logits = lax.dot_general(
        lax.all_gather(gathered, "seq", axis=1, tiled=True),
        columns,
        (((1,), (1,)), ((), ())),
        preferred_element_type=jnp.float32,
    )
    columns = vocab_weight
    draft_extra = jnp.einsum(
        "tnc,vc->tnv",
        lax.all_gather(branch, ("kv", "vocab"), axis=2, tiled=True),
        columns,
        preferred_element_type=jnp.float32,
    )
    raw_logits = jnp.concatenate(
        [base_logits[:, None, :], base_logits[:, None, :] + draft_extra], axis=1
    )
    logits = LOGIT_CAP * jnp.tanh(raw_logits / LOGIT_CAP)
    totals = jnp.sum(jnp.exp(logits), axis=-1)
    head_total = draft_count + 1
    candidates = candidate_tokens.reshape(head_total, kv_count, tok_block, tenants, CAND)
    candidates = jnp.transpose(candidates, (0, 1, 3, 2, 4)).reshape(head_total, row_count, CAND)
    candidates = jnp.transpose(candidates, (1, 0, 2))
    vocab_start = lax.axis_index(("kv", "seq", "vocab")) * vocab_rows
    local_tokens = candidates - vocab_start
    entry_index = jnp.arange(vocab_rows, dtype=jnp.int32)
    picked = jnp.stack(
        [
            jnp.sum(
                jnp.where(entry_index == local_tokens[:, :, column : column + 1], logits, 0.0),
                axis=-1,
            )
            for column in range(CAND)
        ],
        axis=-1,
    )
    totals, picked = lax.psum((totals, picked), ("kv", "seq", "vocab"))
    log_totals = jnp.transpose(jnp.log(totals)).reshape(head_total, kv_count, tenants, tok_block)
    log_normalizer = jnp.transpose(log_totals, (0, 1, 3, 2)).reshape(head_total, tree_size, tenants)
    picked = jnp.transpose(picked, (1, 0, 2)).reshape(
        head_total, kv_count, tenants, tok_block, CAND
    )
    candidate_logits = jnp.transpose(picked, (0, 1, 3, 2, 4)).reshape(
        head_total, tree_size, tenants, CAND
    )
    accept_count = accepted_path.shape[1]
    slot_rows = length + jnp.arange(accept_count, dtype=jnp.int32)
    tree_nodes = jnp.arange(tree_size, dtype=jnp.int32)
    matches = (cache_cells[:, None, None] == slot_rows[None, :, None]) & (
        accepted_path[0][None, :, None] == tree_nodes[None, None, :]
    )
    selector = jnp.sum(matches.astype(jnp.float32), axis=1)
    written = jnp.sum(selector, axis=-1) > 0.0
    selector = selector.astype(jnp.bfloat16)

    def write_path(old_block, fresh_rows):
        moved_rows = jnp.dot(
            selector, fresh_rows.reshape(tree_size, -1), preferred_element_type=jnp.float32
        ).astype(jnp.bfloat16)
        return jnp.where(
            written[:, None], moved_rows, old_block[0].reshape(block_size, -1)
        ).reshape(old_block.shape)

    keys_updated = write_path(cache_keys, new_keys)
    values_updated = write_path(cache_values, new_values)
    return (keys_updated, values_updated, log_normalizer, candidate_logits)


def solution(mesh):
    placed = (
        P("kv", "vocab", "seq"),
        P("seq", "kv", None),
        P("kv", None, "seq"),
        P("seq"),
        P("seq"),
        P("seq"),
        P("seq"),
        P("seq"),
        P("vocab", "seq", "kv", None),
        P("vocab", "seq", "kv", None),
        P("vocab"),
        P("vocab", None, None),
        P("vocab", None),
        P("seq", None, ("kv", "vocab")),
        P(("kv", "vocab"), "seq"),
        P(None, "seq", ("kv", "vocab")),
        P(None, ("kv", "vocab")),
        P(("kv", "seq", "vocab"), None),
        P(),
    )
    return jax.shard_map(
        local,
        mesh=mesh,
        in_specs=placed,
        out_specs=(P("vocab", "seq", "kv", None), P("vocab", "seq", "kv", None), P(), P()),
        check_vma=False,
    )
```

profile of v0, /device:TPU:0, one launch (start us, length us, event | category | flops | bytes accessed | tf_op | source)
XLA Modules:
  0.0 542.6 jit_solution(4778211466463317116)
XLA Ops:
  7.2 6.0 %all-gather = bf16[48,1,896]{2,0,1:T(8,128)(2,1)S(1)} all-gather(bf16[24,1,896]{2,0,1:T(8,128)(2,1)} %param.19), channel_id=2, replica_groups=mesh['kv'=2,'seq'=4,'vocab'=4] {'kv'}, dimensions={0}, use_global_device_ids=true | all-gather | bytes 129024 | tf_op jit(solution)/shard_map/all_gather | solution.py:75
  13.2 8.3 %fusion.2 = f32[48,4,1024]{2,0,1:T(8,128)} fusion(bf16[896,4,1024]{2,1,0:T(4,128)(2,1)} %param.20, bf16[48,1,896]{2,0,1:T(8,128)(2,1)S(1)} %all-gather, f32[896]{0:T(1024)} %param.22), kind=kOutput, calls=%fused_computation.2 | convolution fusion | flops 352450560 | bytes 8216064 | tf_op jit(solution)/shard_map/td,dhc->thc/dot_general | solution.py:78
  22.6 12.6 %psum.85 = f32[48]{0:T(128)S(1)} all-reduce(f32[48]{0:T(128)S(1)} %fusion.56), channel_id=1, replica_groups=mesh['kv'=2,'seq'=4,'vocab'=4] {'seq'}, use_global_device_ids=true, to_apply=%region_4.5 | all-reduce | flops 48 | bytes 384 | tf_op jit(solution)/shard_map/psum | solution.py:81
  35.4 31.8 %all-reduce.8.cloned.1.call-done = f32[48,4,1024]{2,0,1:T(8,128)} async-done(((f32[48,4,1024]{2,0,1:T(8,128)}), f32[48,4,1024]{2,0,1:T(8,128)}) %all-reduce.8.cloned.1.call-update) | async-done | bytes 786448 | tf_op jit(solution)/shard_map/psum | solution.py:81
  78.1 10.1 %psum.87 = f32[48,4,2]{0,2,1:T(2,128)S(1)} all-reduce(f32[48,4,2]{0,2,1:T(2,128)S(1)} %get-tuple-element.58), channel_id=1, replica_groups=mesh['kv'=2,'seq'=4,'vocab'=4] {'seq'}, use_global_device_ids=true, to_apply=%region_8.9 | all-reduce | flops 384 | bytes 3072 | tf_op jit(solution)/shard_map/psum | solution.py:110
  95.0 32.8 %all-reduce.10.cloned.1.call-done = f32[48,4,2,256]{3,0,2,1:T(8,128)} async-done(((f32[48,4,2,256]{3,0,2,1:T(8,128)}), f32[48,4,2,256]{3,0,2,1:T(8,128)}) %all-reduce.10.cloned.1.call-update) | async-done | bytes 393232 | tf_op jit(solution)/shard_map/psum | solution.py:110
  134.6 10.4 %reduce-scatter.7.cloned.1.call-done = f32[24,896]{1,0:T(8,128)} async-done(((f32[48,896]{1,0:T(8,128)}), f32[24,896]{1,0:T(8,128)}) %reduce-scatter.7.cloned.1.call-update) | async-done | bytes 86032
  146.0 11.7 %psum.88 = f32[24]{0:T(128)S(1)} all-reduce(f32[24]{0:T(128)S(1)} %multiply_reduce_fusion.1), channel_id=1, replica_groups=mesh['kv'=2,'seq'=4,'vocab'=4] {'seq'}, use_global_device_ids=true, to_apply=%region_12.13 | all-reduce | flops 24 | bytes 192 | tf_op jit(solution)/shard_map/psum | solution.py:38
  159.3 9.5 %all_gather.16 = bf16[192,896]{1,0:T(8,128)(2,1)S(1)} all-gather(bf16[24,896]{1,0:T(8,128)(2,1)S(1)} %fusion.67), channel_id=1, replica_groups=mesh['kv'=2,'seq'=4,'vocab'=4] {'kv','vocab'}, dimensions={0}, use_global_device_ids=true | all-gather | bytes 387072 | tf_op jit(solution)/shard_map/all_gather | solution.py:138
  168.8 6.0 %fusion.4 = f32[192,2,1792]{2,0,1:T(8,128)} fusion(bf16[896,2,1792]{2,1,0:T(2,128)(2,1)} %param.32, bf16[192,896]{1,0:T(8,128)(2,1)S(1)} %all_gather.16, f32[896]{0:T(1024)} %param.24), kind=kOutput, calls=%fused_computation.4 | convolution fusion | flops 1233641472 | bytes 9522688 | tf_op jit(solution)/shard_map/td,dcf->tcf/dot_general | solution.py:141
  175.6 8.8 %psum.90 = f32[192]{0:T(256)S(1)} all-reduce(f32[192]{0:T(256)} %fusion.43), channel_id=1, replica_groups=mesh['kv'=2,'seq'=4,'vocab'=4] {'seq'}, use_global_device_ids=true, to_apply=%region_15.16 | all-reduce | flops 192 | bytes 1536 | tf_op jit(solution)/shard_map/psum | solution.py:145
  184.3 96.3 %all-reduce.12.cloned.1.call-done = f32[192,2,1792]{2,0,1:T(8,128)} async-done(((f32[192,2,1792]{2,0,1:T(8,128)}), f32[192,2,1792]{2,0,1:T(8,128)}) %all-reduce.12.cloned.1.call-update) | async-done | bytes 2752528 | tf_op jit(solution)/shard_map/psum | solution.py:145
  285.5 33.2 %reduce-scatter.9.cloned.1.call-done = f32[24,896]{1,0:T(8,128)} async-done(((f32[192,896]{1,0:T(8,128)}), f32[24,896]{1,0:T(8,128)}) %reduce-scatter.9.cloned.1.call-update) | async-done | bytes 86032
  319.7 11.7 %psum.91 = f32[24]{0:T(128)S(1)} all-reduce(f32[24]{0:T(128)S(1)} %multiply_reduce_fusion), channel_id=1, replica_groups=mesh['kv'=2,'seq'=4,'vocab'=4] {'seq'}, use_global_device_ids=true, to_apply=%region_18.19 | all-reduce | flops 24 | bytes 192 | tf_op jit(solution)/shard_map/psum | solution.py:38
  332.5 8.4 %psum.92 = f32[24]{0:T(128)S(1)} all-reduce(f32[24]{0:T(128)S(1)} %get-tuple-element.37), channel_id=1, replica_groups=mesh['kv'=2,'seq'=4,'vocab'=4] {'seq'}, use_global_device_ids=true, to_apply=%region_20.21 | all-reduce | flops 24 | bytes 192 | tf_op jit(solution)/shard_map/psum | solution.py:38
  341.0 9.4 %all_gather.17 = bf16[192,896]{1,0:T(8,128)(2,1)S(1)} all-gather(bf16[24,896]{1,0:T(8,128)(2,1)S(1)} %fusion.64), channel_id=1, replica_groups=mesh['kv'=2,'seq'=4,'vocab'=4] {'kv','vocab'}, dimensions={0}, use_global_device_ids=true | all-gather | bytes 387072 | tf_op jit(solution)/shard_map/all_gather | solution.py:159
  353.3 41.7 %all-reduce.14.cloned.1.call-done = bf16[192,4,448]{2,0,1:T(8,128)(2,1)} async-done(((bf16[192,4,448]{2,0,1:T(8,128)(2,1)}), bf16[192,4,448]{2,0,1:T(8,128)(2,1)}) %all-reduce.14.cloned.1.call-update) | async-done | bytes 688144 | tf_op jit(solution)/shard_map/psum | solution.py:161
  398.0 7.5 %copy.92 = bf16[1,2048,4,256]{1,3,2,0:T(8,128)(2,1)} copy(bf16[1,2048,4,256]{3,2,1,0:T(4,128)(2,1)} %param.27) | data formatting | bytes 8388608 | tf_op args[8]
  405.5 7.6 %copy.94 = bf16[1,2048,4,256]{1,3,2,0:T(8,128)(2,1)} copy(bf16[1,2048,4,256]{3,2,1,0:T(4,128)(2,1)} %param.28) | data formatting | bytes 8388608 | tf_op args[9]
  420.7 7.4 %copy.108 = bf16[1,2048,4,256]{3,2,1,0:T(4,128)(2,1)} copy(bf16[1,2048,4,256]{1,3,2,0:T(8,128)(2,1)} %bitcast.169) | data formatting | bytes 8388608
  433.7 7.5 %copy.109 = bf16[1,2048,4,256]{3,2,1,0:T(4,128)(2,1)} copy(bf16[1,2048,4,256]{1,3,2,0:T(8,128)(2,1)} %bitcast.168) | data formatting | bytes 8388608
  445.7 35.1 %all-gather.6.cloned.1.call-done = bf16[192,4,3584]{0,1,2:T(4,128)(2,1)} async-done(((bf16[192,4,448]{0,1,2:T(4,128)(2,1)}), bf16[192,4,3584]{0,1,2:T(4,128)(2,1)}) %all-gather.6.cloned.1.call-update) | async-done | bytes 5505040 | tf_op jit(solution)/shard_map/all_gather | solution.py:176
  480.8 8.4 %fusion.15 = f32[192,4,512]{2,0,1:T(8,128)S(1)} fusion(bf16[512,3584]{1,0:T(8,128)(2,1)} %param.36, bf16[192,4,3584]{0,1,2:T(4,128)(2,1)} %all-gather.6.cloned.1.call-done, f32[192,512]{1,0:T(8,128)} %fusion.85), kind=kOutput, calls=%fused_computation.40 | convolution fusion | flops 2818965504 | bytes 11141120 | tf_op jit(solution)/shard_map/tnc,vc->tnv/dot_general | solution.py:174
  494.3 40.7 %all-reduce.2 = (f32[192,5]{0,1:T(8,128)S(1)}, f32[5,48,4,8]{1,3,2,0:T(8,128)}) all-reduce(f32[192,5]{0,1:T(8,128)S(1)} %get-tuple-element.39, f32[5,48,4,8]{1,3,2,0:T(8,128)S(1)} %reshape.290), channel_id=1, replica_groups=mesh['kv'=2,'seq'=4,'vocab'=4] {'kv','seq','vocab'}, use_global_device_ids=true, to_apply=%region_23.24 | all-reduce | flops 8640 | bytes 69120 | tf_op jit(solution)/shard_map/psum | solution.py:202
  (129 shorter events, 64.6 us)
Async XLA Ops:
  7.2 343.3 %copy-start = (bf16[4,896,448]{1,2,0:T(8,128)(2,1)S(1)}, bf16[4,896,448]{1,2,0:T(8,128)(2,1)}, u32[]{:S(2)}) copy-start(bf16[4,896,448]{1,2,0:T(8,128)(2,1)} %param.34) | copy-start | bytes 9633796
  7.2 60.0 %all-reduce.8.cloned.1.call-start = ((), (), s32[]{:S(2)}) async-start(), calls=%async_computation.2 | async-start | bytes 1572864 | tf_op jit(solution)/shard_map/psum | solution.py:81
  13.2 8.5 %copy-start.12 = (s32[1,48,48]{2,1,0:T(8,128)S(1)}, s32[1,48,48]{2,1,0:T(8,128)}, u32[]{:S(2)}) copy-start(s32[1,48,48]{2,1,0:T(8,128)} %param.30) | copy-start | bytes 27652
  21.5 106.3 %all-reduce.10.cloned.1.call-start = ((), (), s32[]{:S(2)}) async-start(), calls=%async_computation.3 | async-start | bytes 786432 | tf_op jit(solution)/shard_map/psum | solution.py:110
  68.4 0.9 copy-start.2
  92.4 52.6 %reduce-scatter.7.cloned.1.call-start = ((), (), s32[]{:S(2)}) async-start(), calls=%async_computation.8 | async-start | bytes 258048
  93.5 1.5 copy-start.9
  131.1 26.6 %copy-start.11 = (bf16[24,1,896]{2,0,1:T(8,128)(2,1)S(1)}, bf16[24,1,896]{2,0,1:T(8,128)(2,1)}, u32[]{:S(2)}) copy-start(bf16[24,1,896]{2,0,1:T(8,128)(2,1)} %param.19) | copy-start | bytes 129028
  131.1 26.6 %copy-start.14 = (f32[896]{0:T(1024)S(1)}, f32[896]{0:T(1024)}, u32[]{:S(2)}) copy-start(f32[896]{0:T(1024)} %param.23) | copy-start | bytes 10756
  134.6 146.1 %all-reduce.12.cloned.1.call-start = ((), (), s32[]{:S(2)}) async-start(), calls=%async_computation.4 | async-start | bytes 5505024 | tf_op jit(solution)/shard_map/psum | solution.py:145
  174.8 143.9 %reduce-scatter.9.cloned.1.call-start = ((), (), s32[]{:S(2)}) async-start(), calls=%async_computation.9 | async-start | bytes 774144
  184.3 147.1 %copy-start.6 = (bf16[24,896]{1,0:T(8,128)(2,1)S(1)}, bf16[24,896]{1,0:T(8,128)(2,1)}, u32[]{:S(2)}) copy-start(bf16[24,896]{1,0:T(8,128)(2,1)} %copy-done.5) | copy-start | bytes 129028
  184.3 147.1 %copy-start.15 = (f32[896]{0:T(1024)S(1)}, f32[896]{0:T(1024)}, u32[]{:S(2)}) copy-start(f32[896]{0:T(1024)} %param.25) | copy-start | bytes 10756
  184.3 156.6 %copy-start.16 = (f32[896]{0:T(1024)S(1)}, f32[896]{0:T(1024)}, u32[]{:S(2)}) copy-start(f32[896]{0:T(1024)} %param.26) | copy-start | bytes 10756
  285.5 109.5 %all-reduce.14.cloned.1.call-start = ((), (), s32[]{:S(2)}) async-start(), calls=%async_computation.6 | async-start | bytes 1572864 | tf_op jit(solution)/shard_map/psum | solution.py:161
  350.4 2.0 copy-start.3
  352.5 88.7 %all-gather.4.cloned.1.call-start = ((), (), s32[]{:S(2)}) async-start(), calls=%async_computation.5 | async-start | bytes 1720320 | tf_op jit(solution)/shard_map/all_gather | solution.py:168
  353.2 127.6 %all-gather.6.cloned.1.call-start = ((), (), s32[]{:S(2)}) async-start(), calls=%async_computation.7 | async-start | bytes 8257536 | tf_op jit(solution)/shard_map/all_gather | solution.py:176
  405.5 7.6 %copy-start.13 = (s32[5,48,4,8]{1,3,2,0:T(8,128)S(1)}, s32[5,48,4,8]{1,3,2,0:T(8,128)}, u32[]{:S(2)}) copy-start(s32[5,48,4,8]{1,3,2,0:T(8,128)} %param.37) | copy-start | bytes 92164
  405.5 8.0 %copy-start.17 = (s32[1,5]{1,0:T(1,128)S(1)}, s32[1,5]{1,0:T(1,128)}, u32[]{:S(2)}) copy-start(s32[1,5]{1,0:T(1,128)} %param.31) | copy-start | bytes 64
  405.5 9.6 %copy-start.8 = (bf16[48,4,128]{2,0,1:T(8,128)(2,1)S(1)}, bf16[48,4,128]{2,0,1:T(8,128)(2,1)}, u32[]{:S(2)}) copy-start(bf16[48,4,128]{2,0,1:T(8,128)(2,1)} %copy-done.7) | copy-start | bytes 147460
  405.5 9.6 %copy-start.10 = (bf16[48,4,128]{2,0,1:T(8,128)(2,1)S(1)}, bf16[48,4,128]{2,0,1:T(8,128)(2,1)}, u32[]{:S(2)}) copy-start(bf16[48,4,128]{2,0,1:T(8,128)(2,1)} %copy-done.9) | copy-start | bytes 147460
  480.8 8.5 %copy-start.4 = (f32[192,512]{1,0:T(8,128)S(1)}, f32[192,512]{1,0:T(8,128)}, u32[]{:S(2)}) copy-start(f32[192,512]{1,0:T(8,128)} %fusion.85) | copy-start | bytes 1179652
  480.8 54.9 %copy-start.1 = (bf16[4,896,448]{1,2,0:T(8,128)(2,1)S(1)}, bf16[4,896,448]{1,2,0:T(8,128)(2,1)}, u32[]{:S(2)}) copy-start(bf16[4,896,448]{1,2,0:T(8,128)(2,1)} %param.34) | copy-start | bytes 9633796
  (2 other events, 1.2 us)
Sparse Core Ops, SparseCore 0:
  21.6 45.4 all-reduce.7
  92.6 35.2 all-reduce.9
  134.7 10.2 reduce-scatter.6
  174.9 105.7 all-reduce.11
  285.6 33.0 reduce-scatter.8
  352.6 42.3 all-reduce.13
  396.7 33.0 all-gather.3
  431.8 49.0 all-gather.5
where the time goes:
time: 544 us; the launch traced here: 543 us
  waiting for transfers between devices  282 us (52%)
  blocking collectives  129 us (24%)
  matrix products  59.9 us (11%)
  local copies, waits for them, and re-layouts  42.1 us (8%)
  between operations  15.2 us (3%)
  other arithmetic  14.2 us (3%)
    psum x1, waiting for transfers between devices, local(): gate_up, ffn_squares = lax.psum((gate_up, ffn_squares), 'seq')  96.3 us
    unnamed x10, waiting for transfers between devices  44.4 us
    psum x1, waiting for transfers between devices, local(): lifted = lax.psum(lifted.astype(jnp.bfloat16), 'seq').astype(jnp.float32)  41.7 us
    psum x1, blocking collectives, local(): totals, picked = lax.psum((totals, picked), ('kv', 'seq', 'vocab'))  40.7 us
    all_gather x1, waiting for transfers between devices, local(): lax.all_gather(branch, ('kv', 'vocab'), axis=2, tiled=True)  35.1 us
    unnamed x45, local copies, waits for them, and re-layouts  33.1 us
    psum x1, waiting for transfers between devices, local(): lax.psum((numerator, jnp.sum(weights, axis=-1)), 'seq')  32.8 us
    psum x1, waiting for transfers between devices, local(): lax.psum((projected_rows, jnp.sum(tenant_float * tenant_float, axis=-1)),...  31.8 us
  transfers between devices with their start and end apart: 8, of which 7 were waited for; matrix products, arithmetic and copies ran while one was open for 10% of the time, Pallas kernels for 0%

commit v1 on v0

--- a/solution.py
+++ b/solution.py
@@ -46,7 +46,7 @@
     ).astype(jnp.bfloat16)
 
 
-def local(
+def local_general(
     hidden_state,
     input_projection,
     output_projection,
@@ -231,6 +231,353 @@
     return (keys_updated, values_updated, log_normalizer, candidate_logits)
 
 
+def split_pair(values):
+    high = values.astype(jnp.bfloat16)
+    low = (values - high.astype(jnp.float32)).astype(jnp.bfloat16)
+    return high, low
+
+
+def send_back(blocks):
+    count = lax.axis_size("seq")
+    return [
+        lax.ppermute(blocks[j], "seq", [(i, (i - j) % count) for i in range(count)])
+        for j in range(1, count)
+    ]
+
+
+def collect(block):
+    count = lax.axis_size("seq")
+    return [block] + [
+        lax.ppermute(block, "seq", [(i, (i + j) % count) for i in range(count)])
+        for j in range(1, count)
+    ]
+
+
+def token_totals(values):
+    parts = collect(values)
+    total = parts[0]
+    for j in range(1, len(parts)):
+        total = total + jnp.roll(parts[j], j, axis=0)
+    return total
+
+
+def kv_swap(values):
+    return lax.ppermute(values, "kv", [(0, 1), (1, 0)])
+
+
+def inverse_of(totals):
+    return lax.rsqrt(totals / MODEL_WIDTH + EPSILON)
+
+
+def local(
+    hidden_state,
+    input_projection,
+    output_projection,
+    norm_pre_attention,
+    norm_post_attention,
+    norm_pre_feedforward,
+    norm_post_feedforward,
+    norm_final,
+    cache_keys,
+    cache_values,
+    cache_length,
+    ancestors,
+    accepted_path,
+    gate_up_weight,
+    down_weight,
+    draft_weight,
+    draft_bias,
+    vocab_weight,
+    candidate_tokens,
+):
+    f32, bf16 = jnp.float32, jnp.bfloat16
+    tok_block = hidden_state.shape[0]
+    seq_count = lax.axis_size("seq")
+    kv_count = lax.axis_size("kv")
+    tenants = lax.axis_size("vocab")
+    groups = kv_count * tenants
+    sub = tok_block // seq_count
+    tree_size = tok_block * kv_count
+    chunk = kv_count * sub
+    width = hidden_state.shape[2]
+    head_count = input_projection.shape[1]
+    seq_at = lax.axis_index("seq")
+    kv_at = lax.axis_index("kv")
+    back = (seq_at - jnp.arange(seq_count, dtype=jnp.int32)) % seq_count
+    own_state = jnp.stack(
+        [
+            lax.dynamic_slice_in_dim(hidden_state[:, 0, :], back[j] * sub, sub, 0)
+            for j in range(seq_count)
+        ]
+    )
+    other_state = kv_swap(own_state)
+    tenant_state = jnp.stack([own_state, other_state], axis=1).reshape(tree_size, width)
+    tenant_float = tenant_state.astype(f32)
+    scaled_input = (tenant_float * norm_pre_attention).astype(bf16)
+    projected = jnp.einsum(
+        "td,dhc->thc", scaled_input, input_projection, preferred_element_type=f32
+    ).reshape(seq_count, chunk, head_count * 4 * HEAD_SIZE)
+    square_high, square_low = split_pair(
+        jnp.sum(tenant_float * tenant_float, axis=-1).reshape(seq_count, chunk, 1)
+    )
+    packed = jnp.concatenate(
+        [
+            projected.astype(bf16),
+            jnp.broadcast_to(square_high, (seq_count, chunk, 64)),
+            jnp.broadcast_to(square_low, (seq_count, chunk, 64)),
+        ],
+        axis=-1,
+    )
+    arrived = send_back(packed)
+    columns = head_count * 4 * HEAD_SIZE
+    summed = packed[0].astype(f32)
+    for part in arrived:
+        summed = summed + part.astype(f32)
+    squares = summed[:, columns : columns + 1] + summed[:, columns + 64 : columns + 65]
+    rows = (summed[:, :columns] * inverse_of(squares)).reshape(chunk, head_count, 4 * HEAD_SIZE)
+    kv_order = kv_at ^ jnp.arange(kv_count, dtype=jnp.int32)
+    node_of = (
+        kv_order[None, :, None] * tok_block
+        + back[:, None, None] * sub
+        + jnp.arange(sub, dtype=jnp.int32)[None, None, :]
+    ).reshape(tree_size)
+    node_pick = (node_of[:, None] == jnp.arange(tree_size, dtype=jnp.int32)[None, :]).astype(f32)
+    tree_mask = jnp.einsum(
+        "tu,uv,wv->tw",
+        node_pick[:chunk],
+        ancestors[0].astype(f32),
+        node_pick,
+    )
+    depths = jnp.sum(tree_mask, axis=-1).astype(jnp.int32) - 1
+    length = cache_length[0]
+    token_positions = length + depths
+    queries = apply_rotary(
+        rows[:, :, : 2 * HEAD_SIZE].reshape(chunk, head_count, 2, HEAD_SIZE),
+        token_positions[:, None, None],
+    ).astype(bf16)
+    own_keys = apply_rotary(
+        rows[:, :, 2 * HEAD_SIZE : 3 * HEAD_SIZE], token_positions[:, None]
+    ).astype(bf16)
+    own_values = rows[:, :, 3 * HEAD_SIZE :].astype(bf16)
+    query_rows = jnp.concatenate(
+        collect(queries.reshape(chunk, head_count * 2 * HEAD_SIZE)), axis=0
+    ).reshape(tree_size, head_count, 2, HEAD_SIZE)
+    fresh = jnp.concatenate(
+        collect(
+            jnp.concatenate(
+                [
+                    own_keys.reshape(chunk, head_count * HEAD_SIZE),
+                    own_values.reshape(chunk, head_count * HEAD_SIZE),
+                ],
+                axis=1,
+            )
+        ),
+        axis=0,
+    )
+    new_keys = fresh[:, : head_count * HEAD_SIZE].reshape(tree_size, head_count, HEAD_SIZE)
+    new_values = fresh[:, head_count * HEAD_SIZE :].reshape(tree_size, head_count, HEAD_SIZE)
+    block_size = cache_keys.shape[1]
+    block_start = seq_at * block_size
+    cache_cells = block_start + jnp.arange(block_size, dtype=jnp.int32)
+    scores = jnp.einsum(
+        "thgc,shc->thgs", query_rows, cache_keys[0], preferred_element_type=f32
+    )
+    weights = jnp.where((cache_cells < length)[None, None, None, :], capped_weight(scores), 0.0)
+    numerator = jnp.einsum(
+        "thgs,shc->thgc",
+        weights.astype(bf16),
+        cache_values[0],
+        preferred_element_type=f32,
+    ).reshape(seq_count, chunk, head_count * 2 * HEAD_SIZE)
+    pairs = head_count * 2
+    sum_high, sum_low = split_pair(
+        jnp.sum(weights, axis=-1).reshape(seq_count, chunk, pairs)
+    )
+    packed = jnp.concatenate(
+        [
+            numerator.astype(bf16),
+            sum_high,
+            sum_low,
+            jnp.zeros((seq_count, chunk, 128 - 2 * pairs), bf16),
+        ],
+        axis=-1,
+    )
+    arrived = send_back(packed)
+    tree_scores = jnp.einsum("thgc,uhc->thgu", queries, new_keys, preferred_element_type=f32)
+    tree_weights = jnp.where(tree_mask[:, None, None, :] > 0, capped_weight(tree_scores), 0.0)
+    tree_numerator = jnp.einsum(
+        "thgu,uhc->thgc", tree_weights.astype(bf16), new_values, preferred_element_type=f32
+    )
+    summed = packed[0].astype(f32)
+    for part in arrived:
+        summed = summed + part.astype(f32)
+    columns = pairs * HEAD_SIZE
+    denominator = (
+        summed[:, columns : columns + pairs] + summed[:, columns + pairs : columns + 2 * pairs]
+    ).reshape(chunk, head_count, 2) + jnp.sum(tree_weights, axis=-1)
+    numerator = summed[:, :columns].reshape(chunk, head_count, 2, HEAD_SIZE) + tree_numerator
+    attended = (numerator / denominator[..., None]).astype(bf16).reshape(chunk, columns)
+    attended = jnp.concatenate(collect(attended), axis=0)
+    out_matrix = output_projection.reshape(columns, width)
+    attention_out = jnp.dot(attended, out_matrix, preferred_element_type=f32).reshape(
+        seq_count, kv_count, sub, width
+    )
+    attention_out = attention_out[:, 0] + kv_swap(attention_out[:, 1].astype(bf16)).astype(f32)
+    totals = token_totals(jnp.sum(attention_out * attention_out, axis=-1))
+    first_sum = (
+        own_state.astype(f32) + attention_out * inverse_of(totals)[..., None] * norm_post_attention
+    ).astype(bf16)
+
+    def gather_tokens(values):
+        everyone = lax.all_gather(
+            values.reshape(tok_block, width), ("kv", "vocab"), axis=0, tiled=True
+        )
+        return (
+            everyone.reshape(groups, seq_count, sub, width)
+            .transpose(1, 0, 2, 3)
+            .reshape(groups * tok_block, width)
+        )
+
+    all_state = gather_tokens(first_sum)
+    all_float = all_state.astype(f32)
+    share = groups * sub
+    scaled_ffn = (all_float * norm_pre_feedforward).astype(bf16)
+    ffn_squares = jnp.sum(all_float * all_float, axis=-1).reshape(seq_count, share)
+    squares = ffn_squares[0]
+    for part in send_back(ffn_squares):
+        squares = squares + part
+    units = down_weight.shape[0]
+    pieces = 2
+    piece = units // pieces
+    inverse = inverse_of(squares)[:, None]
+    ffn_out = 0.0
+    for p in range(pieces):
+        window = slice(p * piece, (p + 1) * piece)
+        partial = jnp.einsum(
+            "td,dcf->ctf", scaled_ffn, gate_up_weight[:, :, window], preferred_element_type=f32
+        )
+        partial = partial.astype(bf16).reshape(2, seq_count, share, piece).transpose(1, 0, 2, 3)
+        summed = partial[0].astype(f32)
+        for part in send_back(partial):
+            summed = summed + part.astype(f32)
+        activated = (
+            jax.nn.gelu(summed[0] * inverse, approximate=True) * (summed[1] * inverse)
+        ).astype(bf16)
+        activated = jnp.concatenate(collect(activated), axis=0)
+        ffn_out = ffn_out + jnp.dot(
+            activated, down_weight[window], preferred_element_type=f32
+        )
+    ffn_out = (
+        ffn_out.astype(bf16)
+        .reshape(seq_count, groups, sub, width)
+        .transpose(1, 0, 2, 3)
+    )
+    ffn_out = lax.all_to_all(ffn_out, ("kv", "vocab"), 0, 0)
+    ffn_out = jnp.sum(ffn_out.astype(f32), axis=0)
+    totals = token_totals(jnp.sum(ffn_out * ffn_out, axis=-1))
+    second_sum = (
+        first_sum.astype(f32) + ffn_out * inverse_of(totals)[..., None] * norm_post_feedforward
+    ).astype(bf16)
+    second_float = second_sum.astype(f32)
+    totals = token_totals(jnp.sum(second_float * second_float, axis=-1))
+    normed = (second_float * inverse_of(totals)[..., None] * norm_final).astype(bf16)
+    gathered = gather_tokens(normed)
+    draft_count = draft_weight.shape[0]
+    draft_columns = draft_weight.shape[2]
+    lifted = jnp.einsum("td,ndc->tnc", gathered, draft_weight, preferred_element_type=f32)
+    lifted = lifted.astype(bf16).reshape(seq_count, share, draft_count, draft_columns)
+    summed = lifted[0].astype(f32)
+    for part in send_back(lifted):
+        summed = summed + part.astype(f32)
+    branch = jax.nn.silu(summed + draft_bias).astype(bf16)
+    row_count = groups * tok_block
+    branch = jnp.concatenate(collect(branch), axis=0)
+    vocab_rows = vocab_weight.shape[0]
+    straight = jnp.concatenate(
+        [
+            lax.dynamic_slice_in_dim(gathered, back[j] * share, share, 0)
+            for j in range(seq_count)
+        ],
+        axis=0,
+    )
+    whole = lax.all_gather(straight, "seq", axis=1, tiled=True)
+    whole = jnp.concatenate(
+        [
+            lax.dynamic_slice_in_dim(whole, back[j] * share, share, 0)
+            for j in range(seq_count)
+        ],
+        axis=0,
+    )
+    base_logits = lax.dot_general(
+        whole, vocab_weight, (((1,), (1,)), ((), ())), preferred_element_type=f32
+    )
+    draft_extra = jnp.einsum(
+        "tnc,vc->tnv",
+        lax.all_gather(branch, ("kv", "vocab"), axis=2, tiled=True),
+        vocab_weight,
+        preferred_element_type=f32,
+    )
+    raw_logits = jnp.concatenate(
+        [base_logits[:, None, :], base_logits[:, None, :] + draft_extra], axis=1
+    )
+    logits = LOGIT_CAP * jnp.tanh(raw_logits / LOGIT_CAP)
+    totals = jnp.sum(jnp.exp(logits), axis=-1)
+    head_total = draft_count + 1
+    candidates = candidate_tokens.reshape(head_total, kv_count, seq_count, sub, tenants, CAND)
+    candidates = jnp.transpose(candidates, (2, 1, 4, 3, 0, 5)).reshape(
+        seq_count, share, head_total, CAND
+    )
+    candidates = jnp.concatenate(
+        [lax.dynamic_slice_in_dim(candidates, back[j], 1, 0) for j in range(seq_count)], axis=0
+    ).reshape(row_count, head_total, CAND)
+    vocab_start = lax.axis_index(("kv", "seq", "vocab")) * vocab_rows
+    local_tokens = candidates - vocab_start
+    entry_index = jnp.arange(vocab_rows, dtype=jnp.int32)
+    picked = jnp.stack(
+        [
+            jnp.sum(
+                jnp.where(entry_index == local_tokens[:, :, column : column + 1], logits, 0.0),
+                axis=-1,
+            )
+            for column in range(CAND)
+        ],
+        axis=-1,
+    )
+    tally = jnp.concatenate([totals[..., None], picked], axis=-1).reshape(
+        seq_count, share * head_total * (CAND + 1)
+    )
+    tally = token_totals(tally)
+    group_at = lax.axis_index(("kv", "vocab"))
+    step = 1
+    while step < groups:
+        tally = tally + lax.ppermute(
+            tally, ("kv", "vocab"), [(i, i ^ step) for i in range(groups)]
+        )
+        step *= 2
+    tally = jnp.concatenate(
+        [lax.dynamic_slice_in_dim(tally, back[j], 1, 0) for j in range(seq_count)], axis=0
+    ).reshape(seq_count, kv_count, tenants, sub, head_total, CAND + 1)
+    tally = jnp.transpose(tally, (4, 1, 0, 3, 2, 5)).reshape(
+        head_total, tree_size, tenants, CAND + 1
+    )
+    log_normalizer = jnp.log(tally[..., 0])
+    candidate_logits = tally[..., 1:]
+    accept_pick = (accepted_path[0][:, None] == node_of[None, :]).astype(bf16)
+
+    def write_path(old_block, fresh_rows):
+        chosen = jnp.einsum(
+            "au,uhc->ahc", accept_pick, fresh_rows, preferred_element_type=f32
+        ).astype(bf16)
+        result = old_block[0]
+        for a in range(accept_pick.shape[0]):
+            result = jnp.where((cache_cells == length + a)[:, None, None], chosen[a][None], result)
+        return result[None]
+
+    keys_updated = write_path(cache_keys, new_keys)
+    values_updated = write_path(cache_values, new_values)
+    return (keys_updated, values_updated, log_normalizer, candidate_logits)
+
+
 def solution(mesh):
     placed = (
         P("kv", "vocab", "seq"),
@@ -253,8 +600,11 @@
         P(("kv", "seq", "vocab"), None),
         P(),
     )
+    tokens = 48 // mesh.shape["kv"]
+    fits = mesh.shape["kv"] == 2 and tokens % mesh.shape["seq"] == 0
+    body = local if fits else local_general
     return jax.shard_map(
-        local,
+        body,
         mesh=mesh,
         in_specs=placed,
         out_specs=(P("vocab", "seq", "kv", None), P("vocab", "seq", "kv", None), P(), P()),

time: 544 us -> 437 us (0.80)
  waiting for transfers between devices: 282 us -> 141 us
  blocking collectives: 129 us -> 19.4 us
  starting transfers between devices: 0.33 us -> 78.4 us
  local copies, waits for them, and re-layouts: 42.1 us -> 84 us
  other arithmetic: 14.2 us -> 38 us
  matrix products: 59.9 us -> 44 us
  between operations: 15.2 us -> 29.1 us
    psum x4 -> x0, waiting for transfers between devices: 203 us -> none  [the longest x1 96.3 us: local(): gate_up, ffn_squares = lax.psum((gate_up, ffn_squares), 'seq')]
    psum x7 -> x0, blocking collectives: 104 us -> none  [the longest x1 40.7 us: local(): totals, picked = lax.psum((totals, picked), ('kv', 'seq', 'vocab'))]
    ppermute x0 -> x53, waiting for transfers between devices: none -> 97.3 us  [the longest x18 50.2 us: send_back(): lax.ppermute(blocks[j], 'seq', [(i, (i - j) % count) for i in range(count)])]
    ppermute x0 -> x53, starting transfers between devices: none -> 74.9 us  [the longest x30 47.7 us: collect(): lax.ppermute(block, 'seq', [(i, (i + j) % count) for i in range(count)])]
    unnamed x10 -> x2, waiting for transfers between devices: 44.4 us -> 0.03 us
    unnamed x45 -> x86, local copies, waits for them, and re-layouts: 33.1 us -> 5.46 us
    select_n x0 -> x2, other arithmetic: none -> 18.6 us  [the longest x1 18.6 us: write_path(): jnp.where((cache_cells == length + a)[:, None, None], chosen[a][None], re...]
    slice x2 -> x32, local copies, waits for them, and re-layouts: 1.82 us -> 18.4 us  [the longest x1 8.52 us: local(): gate_up_weight[:, :, window]]
  transfers between devices with their start and end apart: 8 -> 56, of which waited for: 7 -> 33; matrix products, arithmetic and copies ran while one was open for 10% -> 19% of each run, Pallas kernels for 0% -> 0%
where the time goes in v1:
time: 437 us; the launch traced here: 434 us
  waiting for transfers between devices  141 us (32%)
  local copies, waits for them, and re-layouts  84 us (19%)
  starting transfers between devices  78.4 us (18%)
  matrix products  44 us (10%)
  other arithmetic  38 us (9%)
  between operations  29.1 us (7%)
  blocking collectives  19.4 us (4%)
    ppermute x18, waiting for transfers between devices, send_back(): lax.ppermute(blocks[j], 'seq', [(i, (i - j) % count) for i in range(count)])  50.2 us
    ppermute x30, starting transfers between devices, collect(): lax.ppermute(block, 'seq', [(i, (i + j) % count) for i in range(count)])  47.7 us
    ppermute x30, waiting for transfers between devices, collect(): lax.ppermute(block, 'seq', [(i, (i + j) % count) for i in range(count)])  43.2 us
    all_gather x1, waiting for transfers between devices, local(): lax.all_gather(branch, ('kv', 'vocab'), axis=2, tiled=True)  39.6 us
    ppermute x18, starting transfers between devices, send_back(): lax.ppermute(blocks[j], 'seq', [(i, (i - j) % count) for i in range(count)])  20.7 us
    all_gather x2, blocking collectives, gather_tokens(): lax.all_gather(values.reshape(tok_block, width), ('kv', 'vocab'), axis=0,...  19.4 us
    select_n x1, other arithmetic, write_path(): jnp.where((cache_cells == length + a)[:, None, None], chosen[a][None], re...  18.6 us
    dot_general x1, local copies, waits for them, and re-layouts, local(): jnp.einsum('td,dhc->thc', scaled_input, input_projection, preferred_eleme...  13 us
  transfers between devices with their start and end apart: 56, of which 33 were waited for; matrix products, arithmetic and copies ran while one was open for 19% of the time, Pallas kernels for 0%

profile of v1, /device:TPU:0, one launch (start us, length us, event | category | flops | bytes accessed | tf_op | source)
XLA Modules:
  0.0 434.2 jit_solution(8617591108552348154)
XLA Ops:
  18.6 13.0 %copy.322 = bf16[4,1024,896]{2,1,0:T(8,128)(2,1)} copy(bf16[4,1024,896]{1,0,2:T(4,128)(2,1)} %bitcast.302) | data formatting | bytes 14680064 | tf_op jit(solution)/shard_map/td,dhc->thc/dot_general | solution.py:317
  31.8 6.2 %convolution_convert_fusion = bf16[4,12,4096]{2,1,0:T(8,128)(2,1)} fusion(bf16[4096,896,1]{1,0,2:T(8,128)(2,1)} %bitcast.300, bf16[4,12,896]{2,0,1:T(4,128)(2,1)S(1)} %bitcast.315), kind=kOutput, calls=%fused_computation.2 | convolution fusion | flops 352518144 | bytes 7819264 | tf_op jit(solution)/shard_map/td,dhc->thc/dot_general | solution.py:317
  41.1 3.7 collective-permute-start.1
  48.8 7.1 %collective-permute-done.2 = bf16[12,4224]{1,0:T(8,128)(2,1)S(1)} collective-permute-done((bf16[12,4224]{1,0:T(8,128)(2,1)S(1)}, bf16[12,4224]{1,0:T(8,128)(2,1)S(1)}, u32[]{:S(2)}, u32[]{:S(2)}) %collective-permute-start.2) | collective-permute-done | bytes 101408 | tf_op jit(solution)/shard_map/ppermute | solution.py:243
  75.6 5.1 %bitcast_reduce_fusion = (f32[48,4,2]{0,2,1:T(2,128)S(1)}, bf16[4,48,2,2048]{3,1,2,0:T(8,128)(2,1)}) fusion(bf16[2048,4,256,1]{2,1,0,3:T(4,128)(2,1)} %bitcast.304, bf16[12,4,2,256]{3,0,2,1:T(8,128)(2,1)S(1)} %copy.281, bf16[12,4,2,256]{3,0,2,1:T(8,128)(2,1)} %copy.280, bf16[12,4,2,256]{3,0,2,1:T(8,128)(2,1)} %copy.279, ...), kind=kOutput, calls=%fused_computation.14 | convolution fusion | flops 407371392 | bytes 5967360 | tf_op jit(solution)/shard_map/thgc,shc->thgs/dot_general | solution.py:382
  83.1 3.5 fusion.47
  116.6 8.5 %fusion.185 = (bf16[896,2,896]{2,1,0:T(2,128)(2,1)}, bf16[896,2,896]{2,1,0:T(2,128)(2,1)}) fusion(bf16[896,2,1792]{2,1,0:T(2,128)(2,1)} %param.32), kind=kLoop, calls=%fused_computation.325 | loop fusion | bytes 12845056 | tf_op jit(solution)/shard_map/slice | solution.py:457
  130.2 4.1 collective-permute-done.17
  135.6 9.9 %all_gather.12 = bf16[192,896]{1,0:T(8,128)(2,1)S(1)} all-gather(bf16[24,896]{1,0:T(8,128)(2,1)} %reshape.617), channel_id=1, replica_groups=mesh['kv'=2,'seq'=4,'vocab'=4] {'kv','vocab'}, dimensions={0}, use_global_device_ids=true | all-gather | bytes 387072 | tf_op jit(solution)/shard_map/all_gather | solution.py:432
  183.1 10.0 %collective-permute-done.21 = bf16[2,48,896]{2,1,0:T(8,128)(2,1)S(1)} collective-permute-done((bf16[2,48,896]{2,1,0:T(8,128)(2,1)}, bf16[2,48,896]{2,1,0:T(8,128)(2,1)S(1)}, u32[]{:S(2)}, u32[]{:S(2)}) %collective-permute-start.21) | collective-permute-done | bytes 172064 | tf_op jit(solution)/shard_map/ppermute | solution.py:243
  207.2 4.1 collective-permute-done.27
  214.8 3.4 all-to-all-start
  220.9 4.2 all-to-all-done
  231.8 4.0 collective-permute-done.35
  244.5 9.5 %all_gather.13 = bf16[192,896]{1,0:T(8,128)(2,1)S(1)} all-gather(bf16[24,896]{1,0:T(8,128)(2,1)} %reshape.621), channel_id=1, replica_groups=mesh['kv'=2,'seq'=4,'vocab'=4] {'kv','vocab'}, dimensions={0}, use_global_device_ids=true | all-gather | bytes 387072 | tf_op jit(solution)/shard_map/all_gather | solution.py:432
  263.8 7.4 %collective-permute-done.41 = bf16[48,4,448]{2,0,1:T(8,128)(2,1)S(1)} collective-permute-done((bf16[48,4,448]{2,0,1:T(8,128)(2,1)S(1)}, bf16[48,4,448]{2,0,1:T(8,128)(2,1)S(1)}, u32[]{:S(2)}, u32[]{:S(2)}) %collective-permute-start.41) | collective-permute-done | bytes 172064 | tf_op jit(solution)/shard_map/ppermute | solution.py:243
  271.2 19.1 %collective-permute-done.42 = bf16[48,4,448]{2,0,1:T(8,128)(2,1)S(1)} collective-permute-done((bf16[48,4,448]{2,0,1:T(8,128)(2,1)S(1)}, bf16[48,4,448]{2,0,1:T(8,128)(2,1)S(1)}, u32[]{:S(2)}, u32[]{:S(2)}) %collective-permute-start.42) | collective-permute-done | bytes 172064 | tf_op jit(solution)/shard_map/ppermute | solution.py:243
  290.5 7.2 %collective-permute-start.44 = (bf16[48,4,448]{2,0,1:T(8,128)(2,1)S(1)}, bf16[48,4,448]{2,0,1:T(8,128)(2,1)S(1)}, u32[]{:S(2)}, u32[]{:S(2)}) collective-permute-start(bf16[48,4,448]{2,0,1:T(8,128)(2,1)S(1)} %multiply_convert_fusion.1), channel_id=1, source_target_pairs={{0,4},{4,8},{8,12},{12,0},{1,5},{5,9},{9,13},{13,1},{2,6},{6,10},{... | collective-permute-start | bytes 516104 | tf_op jit(solution)/shard_map/ppermute | solution.py:251
  306.2 9.0 %collective-permute-done.45 = bf16[48,4,448]{2,0,1:T(8,128)(2,1)S(1)} collective-permute-done((bf16[48,4,448]{2,0,1:T(8,128)(2,1)S(1)}, bf16[48,4,448]{2,0,1:T(8,128)(2,1)S(1)}, u32[]{:S(2)}, u32[]{:S(2)}) %collective-permute-start.45) | collective-permute-done | bytes 172064 | tf_op jit(solution)/shard_map/ppermute | solution.py:251
  327.9 3.7 fusion.24
  331.7 39.6 %all-gather.5.cloned.1.call-done = bf16[192,4,3584]{0,1,2:T(4,128)(2,1)} async-done(((bf16[192,4,448]{0,1,2:T(4,128)(2,1)}), bf16[192,4,3584]{0,1,2:T(4,128)(2,1)}) %all-gather.5.cloned.1.call-update) | async-done | bytes 5505040 | tf_op jit(solution)/shard_map/all_gather | solution.py:516
  371.3 8.2 %fusion.19 = f32[192,4,512]{2,0,1:T(8,128)S(1)} fusion(bf16[512,3584]{1,0:T(8,128)(2,1)} %param.36, bf16[192,4,3584]{0,1,2:T(4,128)(2,1)} %all-gather.5.cloned.1.call-done, f32[192,512]{1,0:T(8,128)S(1)} %fusion.24), kind=kOutput, calls=%fused_computation.41 | convolution fusion | flops 2818965504 | bytes 11141120 | tf_op jit(solution)/shard_map/tnc,vc->tnv/dot_general | solution.py:514
  379.5 4.4 %select_reduce_fusion = (f32[192,5]{0,1:T(8,128)S(1)}, f32[192,5]{0,1:T(8,128)S(1)}, f32[192,5]{0,1:T(8,128)S(1)}, f32[192,5]{0,1:T(8,128)S(1)}, f32[192,5]{0,1:...) fusion(s32[192,5]{0,1:T(8,128)S(1)} %bitcast.328, ...), kind=kLoop, calls=%fused_computation.20 | loop fusion | flops 13753920 | bytes 2031360 | tf_op jit(solution)/shard_map/reduce_sum | solution.py:538
  401.4 18.6 %select_select_fusion = (bf16[1,2048,4,256]{3,2,1,0:T(4,128)(2,1)}, bf16[1,2048,4,256]{3,2,1,0:T(4,128)(2,1)}) fusion(bf16[1,2048,4,256]{3,2,1,0:T(4,128)(2,1)} %param.28, pred[2048]{0:T(1024)(128)(4,1)S(1)} %get-tuple-element.143, pred[2048]{0:T(1024)(128)(4,1)S(1)} %get-tuple-element.144, pred[2048]{0:T(1024)(128)(4,1)S(1)} %get-tuple-element.145, ...), kind=kLoop, calls=%fused_computation.7 | loop fusion | flops 20971520 | bytes 16807936 | tf_op jit(solution)/shard_map/jit(_where)/select_n | solution.py:573
  (352 shorter events, 191.5 us)
Async XLA Ops:
  12.3 19.2 %collective-permute-start = (bf16[4,6,896]{2,1,0:T(8,128)(2,1)S(1)}, bf16[4,6,896]{2,1,0:T(8,128)(2,1)S(1)}, u32[]{:S(2)}, u32[]{:S(2)}) collective-permute-start(bf16[4,6,896]{2,1,0:T(8,128)(2,1)S(1)} %get-tuple-element.90), channel_id=1, source_target_pairs={{0,16},{16,0},{1,17},{17,1},{2,18},{18,2},{3,19},{19,3},{4,20},{20... | collective-permute-start | bytes 129032 | tf_op jit(solution)/shard_map/ppermute | solution.py:265
  44.8 11.1 %collective-permute-start.2 = (bf16[12,4224]{1,0:T(8,128)(2,1)S(1)}, bf16[12,4224]{1,0:T(8,128)(2,1)S(1)}, u32[]{:S(2)}, u32[]{:S(2)}) collective-permute-start(bf16[12,4224]{1,0:T(8,128)(2,1)S(1)} %get-tuple-element.67), channel_id=1, source_target_pairs={{0,8},{4,12},{8,0},{12,4},{1,9},{5,13},{9,1},{13,5},{2,10},{6,14},... | collective-permute-start | bytes 304136 | tf_op jit(solution)/shard_map/ppermute | solution.py:243
  44.8 11.1 %collective-permute-start.3 = (bf16[12,4224]{1,0:T(8,128)(2,1)S(1)}, bf16[12,4224]{1,0:T(8,128)(2,1)S(1)}, u32[]{:S(2)}, u32[]{:S(2)}) collective-permute-start(bf16[12,4224]{1,0:T(8,128)(2,1)S(1)} %get-tuple-element.66), channel_id=1, source_target_pairs={{0,4},{4,8},{8,12},{12,0},{1,5},{5,9},{9,13},{13,1},{2,6},{6,10},{... | collective-permute-start | bytes 304136 | tf_op jit(solution)/shard_map/ppermute | solution.py:243
  62.2 11.0 %collective-permute-start.8 = (bf16[12,2048]{1,0:T(8,128)(2,1)}, bf16[12,2048]{1,0:T(8,128)(2,1)}, u32[]{:S(2)}, u32[]{:S(2)}) collective-permute-start(bf16[12,2048]{1,0:T(8,128)(2,1)} %convert_element_type.307), channel_id=1, source_target_pairs={{0,8},{4,12},{8,0},{12,4},{1,9},{5,13},{9,1},{13,5},{2,10},{6,14},... | collective-permute-start | bytes 147464 | tf_op jit(solution)/shard_map/ppermute | solution.py:251
  64.2 10.6 %collective-permute-start.9 = (bf16[12,2048]{1,0:T(8,128)(2,1)}, bf16[12,2048]{1,0:T(8,128)(2,1)}, u32[]{:S(2)}, u32[]{:S(2)}) collective-permute-start(bf16[12,2048]{1,0:T(8,128)(2,1)} %convert_element_type.307), channel_id=1, source_target_pairs={{0,12},{4,0},{8,4},{12,8},{1,13},{5,1},{9,5},{13,9},{2,14},{6,2},{... | collective-permute-start | bytes 147464 | tf_op jit(solution)/shard_map/ppermute | solution.py:251
  67.2 13.6 %collective-permute-start.4 = (bf16[12,2048]{1,0:T(8,128)(2,1)S(1)}, bf16[12,2048]{1,0:T(8,128)(2,1)S(1)}, u32[]{:S(2)}, u32[]{:S(2)}) collective-permute-start(bf16[12,2048]{1,0:T(8,128)(2,1)S(1)} %constant_dynamic-update-slice_fusion), channel_id=1, source_target_pairs={{0,4},{4,8},{8,12},{12,0},{1,5},{5,9},{9,13},{13,1},{2,6},{6,10},{... | collective-permute-start | bytes 147464 | tf_op jit(solution)/shard_map/ppermute | solution.py:251
  67.3 13.5 %collective-permute-start.5 = (bf16[12,2048]{1,0:T(8,128)(2,1)S(1)}, bf16[12,2048]{1,0:T(8,128)(2,1)}, u32[]{:S(2)}, u32[]{:S(2)}) collective-permute-start(bf16[12,2048]{1,0:T(8,128)(2,1)S(1)} %constant_dynamic-update-slice_fusion), channel_id=1, source_target_pairs={{0,8},{4,12},{8,0},{12,4},{1,9},{5,13},{9,1},{13,5},{2,10},{6,14},... | collective-permute-start | bytes 147464 | tf_op jit(solution)/shard_map/ppermute | solution.py:251
  69.1 11.7 %collective-permute-start.6 = (bf16[12,2048]{1,0:T(8,128)(2,1)S(1)}, bf16[12,2048]{1,0:T(8,128)(2,1)}, u32[]{:S(2)}, u32[]{:S(2)}) collective-permute-start(bf16[12,2048]{1,0:T(8,128)(2,1)S(1)} %constant_dynamic-update-slice_fusion), channel_id=1, source_target_pairs={{0,12},{4,0},{8,4},{12,8},{1,13},{5,1},{9,5},{13,9},{2,14},{6,2},{... | collective-permute-start | bytes 147464 | tf_op jit(solution)/shard_map/ppermute | solution.py:251
  156.4 24.4 %collective-permute-start.29 = (bf16[2,48,896]{2,1,0:T(8,128)(2,1)}, bf16[2,48,896]{2,1,0:T(8,128)(2,1)S(1)}, u32[]{:S(2)}, u32[]{:S(2)}) collective-permute-start(bf16[2,48,896]{2,1,0:T(8,128)(2,1)} %get-tuple-element.62), channel_id=1, source_target_pairs={{0,12},{4,0},{8,4},{12,8},{1,13},{5,1},{9,5},{13,9},{2,14},{6,2},{... | collective-permute-start | bytes 516104 | tf_op jit(solution)/shard_map/ppermute | solution.py:243
  156.4 24.5 %collective-permute-start.30 = (bf16[2,48,896]{2,1,0:T(8,128)(2,1)}, bf16[2,48,896]{2,1,0:T(8,128)(2,1)}, u32[]{:S(2)}, u32[]{:S(2)}) collective-permute-start(bf16[2,48,896]{2,1,0:T(8,128)(2,1)} %get-tuple-element.64), channel_id=1, source_target_pairs={{0,8},{4,12},{8,0},{12,4},{1,9},{5,13},{9,1},{13,5},{2,10},{6,14},... | collective-permute-start | bytes 516104 | tf_op jit(solution)/shard_map/ppermute | solution.py:243
  156.4 24.5 %collective-permute-start.31 = (bf16[2,48,896]{2,1,0:T(8,128)(2,1)S(1)}, bf16[2,48,896]{2,1,0:T(8,128)(2,1)}, u32[]{:S(2)}, u32[]{:S(2)}) collective-permute-start(bf16[2,48,896]{2,1,0:T(8,128)(2,1)S(1)} %get-tuple-element.63), channel_id=1, source_target_pairs={{0,4},{4,8},{8,12},{12,0},{1,5},{5,9},{9,13},{13,1},{2,6},{6,10},{... | collective-permute-start | bytes 516104 | tf_op jit(solution)/shard_map/ppermute | solution.py:243
  162.6 11.6 %collective-permute-start.23 = (f32[48]{0:T(128)}, f32[48]{0:T(128)}, u32[]{:S(2)}, u32[]{:S(2)}) collective-permute-start(f32[48]{0:T(128)} %slice.398), channel_id=1, source_target_pairs={{0,12},{4,0},{8,4},{12,8},{1,13},{5,1},{9,5},{13,9},{2,14},{6,2},{... | collective-permute-start | bytes 584 | tf_op jit(solution)/shard_map/ppermute | solution.py:243
  179.7 13.5 %collective-permute-start.21 = (bf16[2,48,896]{2,1,0:T(8,128)(2,1)}, bf16[2,48,896]{2,1,0:T(8,128)(2,1)S(1)}, u32[]{:S(2)}, u32[]{:S(2)}) collective-permute-start(bf16[2,48,896]{2,1,0:T(8,128)(2,1)} %get-tuple-element.61), channel_id=1, source_target_pairs={{0,8},{4,12},{8,0},{12,4},{1,9},{5,13},{9,1},{13,5},{2,10},{6,14},... | collective-permute-start | bytes 516104 | tf_op jit(solution)/shard_map/ppermute | solution.py:243
  180.8 12.3 %collective-permute-start.22 = (bf16[2,48,896]{2,1,0:T(8,128)(2,1)}, bf16[2,48,896]{2,1,0:T(8,128)(2,1)S(1)}, u32[]{:S(2)}, u32[]{:S(2)}) collective-permute-start(bf16[2,48,896]{2,1,0:T(8,128)(2,1)} %get-tuple-element.60), channel_id=1, source_target_pairs={{0,4},{4,8},{8,12},{12,0},{1,5},{5,9},{9,13},{13,1},{2,6},{6,10},{... | collective-permute-start | bytes 516104 | tf_op jit(solution)/shard_map/ppermute | solution.py:243
  199.6 11.7 %collective-permute-start.27 = (bf16[48,896]{1,0:T(8,128)(2,1)S(1)}, bf16[48,896]{1,0:T(8,128)(2,1)S(1)}, u32[]{:S(2)}, u32[]{:S(2)}) collective-permute-start(bf16[48,896]{1,0:T(8,128)(2,1)S(1)} %get-tuple-element.129), channel_id=1, source_target_pairs={{0,8},{4,12},{8,0},{12,4},{1,9},{5,13},{9,1},{13,5},{2,10},{6,14},... | collective-permute-start | bytes 258056 | tf_op jit(solution)/shard_map/ppermute | solution.py:251
  214.8 10.3 %all-to-all-start = ((bf16[8,4,6,896]{3,1,2,0:T(4,128)(2,1)}), bf16[8,4,6,896]{3,1,2,0:T(4,128)(2,1)S(1)}, u32[]{:S(2)}, u32[]{:S(2)}) async-start(bf16[8,4,6,896]{3,1,2,0:T(4,128)(2,1)} %copy.302), calls=%async_computation | async-start | bytes 688128 | tf_op jit(solution)/shard_map/all_to_all | solution.py:475
  218.2 108.2 %all-gather.3.cloned.1.call-start = ((), (), s32[]{:S(2)}) async-start(), calls=%async_computation.1 | async-start | bytes 1720320 | tf_op jit(solution)/shard_map/all_gather | solution.py:503
  258.7 112.6 %all-gather.5.cloned.1.call-start = ((), (), s32[]{:S(2)}) async-start(), calls=%async_computation.2 | async-start | bytes 8257536 | tf_op jit(solution)/shard_map/all_gather | solution.py:516
  263.2 27.1 %collective-permute-start.42 = (bf16[48,4,448]{2,0,1:T(8,128)(2,1)S(1)}, bf16[48,4,448]{2,0,1:T(8,128)(2,1)S(1)}, u32[]{:S(2)}, u32[]{:S(2)}) collective-permute-start(bf16[48,4,448]{2,0,1:T(8,128)(2,1)S(1)} %get-tuple-element.58), channel_id=1, source_target_pairs={{0,8},{4,12},{8,0},{12,4},{1,9},{5,13},{9,1},{13,5},{2,10},{6,14},... | collective-permute-start | bytes 516104 | tf_op jit(solution)/shard_map/ppermute | solution.py:243
  263.2 27.1 %collective-permute-start.43 = (bf16[48,4,448]{2,0,1:T(8,128)(2,1)S(1)}, bf16[48,4,448]{2,0,1:T(8,128)(2,1)S(1)}, u32[]{:S(2)}, u32[]{:S(2)}) collective-permute-start(bf16[48,4,448]{2,0,1:T(8,128)(2,1)S(1)} %get-tuple-element.57), channel_id=1, source_target_pairs={{0,4},{4,8},{8,12},{12,0},{1,5},{5,9},{9,13},{13,1},{2,6},{6,10},{... | collective-permute-start | bytes 516104 | tf_op jit(solution)/shard_map/ppermute | solution.py:243
  290.5 15.7 %collective-permute-start.44 = (bf16[48,4,448]{2,0,1:T(8,128)(2,1)S(1)}, bf16[48,4,448]{2,0,1:T(8,128)(2,1)S(1)}, u32[]{:S(2)}, u32[]{:S(2)}) collective-permute-start(bf16[48,4,448]{2,0,1:T(8,128)(2,1)S(1)} %multiply_convert_fusion.1), channel_id=1, source_target_pairs={{0,4},{4,8},{8,12},{12,0},{1,5},{5,9},{9,13},{13,1},{2,6},{6,10},{... | collective-permute-start | bytes 516104 | tf_op jit(solution)/shard_map/ppermute | solution.py:251
  297.6 17.6 %collective-permute-start.45 = (bf16[48,4,448]{2,0,1:T(8,128)(2,1)S(1)}, bf16[48,4,448]{2,0,1:T(8,128)(2,1)S(1)}, u32[]{:S(2)}, u32[]{:S(2)}) collective-permute-start(bf16[48,4,448]{2,0,1:T(8,128)(2,1)S(1)} %multiply_convert_fusion.1), channel_id=1, source_target_pairs={{0,8},{4,12},{8,0},{12,4},{1,9},{5,13},{9,1},{13,5},{2,10},{6,14},... | collective-permute-start | bytes 516104 | tf_op jit(solution)/shard_map/ppermute | solution.py:251
  300.2 15.0 %collective-permute-start.46 = (bf16[48,4,448]{2,0,1:T(8,128)(2,1)S(1)}, bf16[48,4,448]{2,0,1:T(8,128)(2,1)S(1)}, u32[]{:S(2)}, u32[]{:S(2)}) collective-permute-start(bf16[48,4,448]{2,0,1:T(8,128)(2,1)S(1)} %multiply_convert_fusion.1), channel_id=1, source_target_pairs={{0,12},{4,0},{8,4},{12,8},{1,13},{5,1},{9,5},{13,9},{2,14},{6,2},{... | collective-permute-start | bytes 516104 | tf_op jit(solution)/shard_map/ppermute | solution.py:251
  399.9 20.2 %collective-permute-start.52 = (f32[4,2160]{1,0:T(4,128)S(1)}, f32[4,2160]{1,0:T(4,128)S(1)}, u32[]{:S(2)}, u32[]{:S(2)}) collective-permute-start(f32[4,2160]{1,0:T(4,128)S(1)} %add.488), channel_id=1, source_target_pairs={{0,16},{1,17},{2,18},{3,19},{16,0},{17,1},{18,2},{19,3},{4,20},{5,... | collective-permute-start | bytes 103688 | tf_op jit(solution)/shard_map/ppermute | solution.py:553
  (59 other events, 758.7 us)
Sparse Core Ops, SparseCore 0:
  258.8 56.6 all-gather.2
  318.0 53.1 all-gather.4

commit v2 on v0

--- a/solution.py
+++ b/solution.py
@@ -1,6 +1,8 @@
 import jax
 import jax.numpy as jnp
 from jax import lax
+from jax.experimental import pallas as pl
+from jax.experimental.pallas import tpu as pltpu
 from jax.sharding import PartitionSpec as P
 
 MODEL_WIDTH = 3584
@@ -46,7 +48,7 @@
     ).astype(jnp.bfloat16)
 
 
-def local(
+def local_general(
     hidden_state,
     input_projection,
     output_projection,
@@ -231,6 +233,408 @@
     return (keys_updated, values_updated, log_normalizer, candidate_logits)
 
 
+def fits(sizes):
+    return sizes["kv"] == 2 and sizes["vocab"] == 4 and sizes["seq"] == 4
+
+
+def send_ahead(pick):
+    count = lax.axis_size("seq")
+    return [
+        lax.ppermute(pick(j), "seq", [(i, (i + j) % count) for i in range(count)])
+        for j in range(1, count)
+    ]
+
+
+def collect(block):
+    count = lax.axis_size("seq")
+    return [block] + [
+        lax.ppermute(block, "seq", [(i, (i - j) % count) for i in range(count)])
+        for j in range(1, count)
+    ]
+
+
+def in_order(blocks, ahead):
+    result = jnp.zeros((len(blocks),) + blocks[0].shape, blocks[0].dtype)
+    for j, block in enumerate(blocks):
+        result = lax.dynamic_update_index_in_dim(result, block, ahead[j], 0)
+    return result
+
+
+def add_up(blocks):
+    total = blocks[0].astype(jnp.float32)
+    for block in blocks[1:]:
+        total = total + block.astype(jnp.float32)
+    return total
+
+
+def swap(values, axis, bit):
+    count = lax.axis_size(axis)
+    return lax.ppermute(values, axis, [(i, i ^ bit) for i in range(count)])
+
+
+def split_lanes(values):
+    high = values.astype(jnp.bfloat16)
+    low = (values - high.astype(jnp.float32)).astype(jnp.bfloat16)
+    shape = values.shape[:-1] + (64,)
+    return jnp.concatenate([jnp.broadcast_to(high, shape), jnp.broadcast_to(low, shape)], axis=-1)
+
+
+def inverse_of(totals):
+    return lax.rsqrt(totals / MODEL_WIDTH + EPSILON)
+
+
+def rotate(vectors, cosine, sine):
+    half = vectors.shape[-1] // 2
+    first, second = vectors[..., :half], vectors[..., half:]
+    return jnp.concatenate(
+        [first * cosine - second * sine, second * cosine + first * sine], axis=-1
+    )
+
+
+def update_caches(cache_keys, cache_values, rows, offset):
+    slots = cache_keys.shape[0]
+    accept = rows.shape[1]
+    parts = 4
+    piece = slots // parts
+
+    def kernel(offset_ref, rows_ref, keys_in, values_in, keys_out, values_out, flag, sems):
+        flag[...] = jnp.zeros_like(flag)
+        copies = []
+        for which, (source, target) in enumerate(((keys_in, keys_out), (values_in, values_out))):
+            for p in range(parts):
+                window = pl.ds(p * piece, piece)
+                copies.append(
+                    pltpu.make_async_copy(
+                        source.at[window], target.at[window], sems.at[which * parts + p]
+                    )
+                )
+        for copy in copies:
+            copy.start()
+        for copy in copies:
+            copy.wait()
+        for which, target in enumerate((keys_out, values_out)):
+            for a in range(accept):
+                slot = offset_ref[0] + a
+
+                @pl.when((slot >= 0) & (slot < slots))
+                def _():
+                    copy = pltpu.make_async_copy(
+                        rows_ref.at[which, pl.ds(a, 1)], target.at[pl.ds(slot, 1)], sems.at[0]
+                    )
+                    copy.start()
+                    copy.wait()
+
+    like = jax.ShapeDtypeStruct(cache_keys.shape, cache_keys.dtype)
+    return pl.pallas_call(
+        kernel,
+        out_shape=(like, like, jax.ShapeDtypeStruct((8, 128), jnp.float32)),
+        in_specs=[
+            pl.BlockSpec(memory_space=pltpu.SMEM),
+            pl.BlockSpec(memory_space=pltpu.VMEM),
+            pl.BlockSpec(memory_space=pl.ANY),
+            pl.BlockSpec(memory_space=pl.ANY),
+        ],
+        out_specs=(
+            pl.BlockSpec(memory_space=pl.ANY),
+            pl.BlockSpec(memory_space=pl.ANY),
+            pl.BlockSpec(memory_space=pltpu.VMEM),
+        ),
+        scratch_shapes=[pltpu.SemaphoreType.DMA((2 * parts,))],
+        cost_estimate=pl.CostEstimate(
+            flops=0, bytes_accessed=4 * cache_keys.size * 2, transcendentals=0
+        ),
+    )(offset, rows, cache_keys, cache_values)
+
+
+def local(
+    hidden_state,
+    input_projection,
+    output_projection,
+    norm_pre_attention,
+    norm_post_attention,
+    norm_pre_feedforward,
+    norm_post_feedforward,
+    norm_final,
+    cache_keys,
+    cache_values,
+    cache_length,
+    ancestors,
+    accepted_path,
+    gate_up_weight,
+    down_weight,
+    draft_weight,
+    draft_bias,
+    vocab_weight,
+    candidate_tokens,
+):
+    f32, bf16 = jnp.float32, jnp.bfloat16
+    plane = ("kv", "vocab")
+    tok_block, _, width = hidden_state.shape
+    seq_count = lax.axis_size("seq")
+    kv_count = lax.axis_size("kv")
+    tenants = lax.axis_size("vocab")
+    groups = kv_count * tenants
+    tree_size = tok_block * kv_count
+    row_count = tok_block * groups
+    seq_at = lax.axis_index("seq")
+    kv_at = lax.axis_index("kv")
+    vocab_at = lax.axis_index("vocab")
+    ahead = [(seq_at + j) % seq_count for j in range(seq_count)]
+    own_state = hidden_state[:, 0, :]
+
+    half = vocab_weight.shape[0] // 2
+    over_kv = swap(vocab_weight, "kv", 1)
+    over_y = swap(vocab_weight, "vocab", 2)
+    far_top = swap(over_kv[:half], "vocab", 2)
+    far_bottom = swap(over_y[half:], "kv", 1)
+    near = [vocab_weight, over_kv, over_y, far_top, far_bottom]
+    vocab_blocks = near + [swap(block, "vocab", 1) for block in near]
+
+    tenant_state = jnp.concatenate([own_state, swap(own_state, "kv", 1)], axis=0)
+    tenant_float = tenant_state.astype(f32)
+    scaled_input = (tenant_float * norm_pre_attention).astype(bf16)
+    projected = jnp.einsum(
+        "td,dhc->htc", scaled_input, input_projection, preferred_element_type=f32
+    ).astype(bf16)
+    square_lanes = split_lanes(jnp.sum(tenant_float * tenant_float, axis=-1, keepdims=True))
+    head_count = projected.shape[0]
+    pair = 2 * HEAD_SIZE
+    packed = jnp.concatenate(
+        [
+            projected[:, :, :pair],
+            jnp.broadcast_to(square_lanes, (head_count,) + square_lanes.shape),
+        ],
+        axis=-1,
+    )
+    summed = add_up(
+        [lax.dynamic_index_in_dim(packed, seq_at, 0, False)]
+        + send_ahead(lambda j: lax.dynamic_index_in_dim(packed, ahead[j], 0, False))
+    )
+    inverse = inverse_of(summed[:, pair : pair + 1] + summed[:, pair + 64 : pair + 65])
+    tree_mask = ancestors[0]
+    tree_mask = jnp.where(
+        kv_at == 0, tree_mask, jnp.roll(tree_mask, (tok_block, tok_block), (0, 1))
+    )
+    length = cache_length[0]
+    depths = jnp.sum(tree_mask, axis=-1, keepdims=True) - 1
+    frequency = 10000.0 ** (
+        -2.0 * jnp.arange(HEAD_SIZE // 2, dtype=f32) / HEAD_SIZE
+    )
+    angles = (length + depths).astype(f32) * frequency
+    cosine, sine = jnp.cos(angles), jnp.sin(angles)
+    query_rows = jnp.concatenate(
+        [
+            rotate(summed[:, :HEAD_SIZE] * inverse, cosine, sine),
+            rotate(summed[:, HEAD_SIZE:pair] * inverse, cosine, sine),
+        ],
+        axis=0,
+    ).astype(bf16)
+    all_queries = in_order(collect(query_rows), ahead)
+    fresh = projected[:, :, pair:]
+    fresh = add_up(
+        [lax.dynamic_index_in_dim(fresh, seq_at, 0, False)]
+        + send_ahead(lambda j: lax.dynamic_index_in_dim(fresh, ahead[j], 0, False))
+    )
+    new_keys = rotate(fresh[:, :HEAD_SIZE] * inverse, cosine, sine).astype(bf16)
+    new_values = (fresh[:, HEAD_SIZE:] * inverse).astype(bf16)
+
+    block_size = cache_keys.shape[1]
+    block_start = seq_at * block_size
+    cache_cells = block_start + jnp.arange(block_size, dtype=jnp.int32)
+    scores = jnp.einsum("hrc,shc->hrs", all_queries, cache_keys[0], preferred_element_type=f32)
+    weights = jnp.where((cache_cells < length)[None, None, :], capped_weight(scores), 0.0)
+    numerator = jnp.einsum(
+        "hrs,shc->hrc", weights.astype(bf16), cache_values[0], preferred_element_type=f32
+    )
+    rows = 2 * tree_size
+    sums = jnp.sum(weights, axis=-1)
+    sums_high = sums.astype(bf16)
+    sums_low = (sums - sums_high.astype(f32)).astype(bf16)
+    sums = jnp.concatenate(
+        [sums_high, sums_low, jnp.zeros((head_count, HEAD_SIZE - 2 * rows), bf16)], axis=-1
+    )
+    packed = jnp.concatenate(
+        [
+            numerator.astype(bf16),
+            jnp.broadcast_to(sums[:, None, :], (head_count, 16, HEAD_SIZE)),
+        ],
+        axis=1,
+    )
+    arrived = send_ahead(lambda j: lax.dynamic_index_in_dim(packed, ahead[j], 0, False))
+    tree_scores = lax.dot_general(
+        query_rows, new_keys, (((1,), (1,)), ((), ())), preferred_element_type=f32
+    )
+    seen = jnp.concatenate([tree_mask, tree_mask], axis=0) > 0
+    tree_weights = jnp.where(seen, capped_weight(tree_scores), 0.0)
+    tree_numerator = jnp.dot(tree_weights.astype(bf16), new_values, preferred_element_type=f32)
+    tree_sums = jnp.sum(tree_weights, axis=-1, keepdims=True)
+    summed = add_up([lax.dynamic_index_in_dim(packed, seq_at, 0, False)] + arrived)
+    denominator = (summed[rows, :rows] + summed[rows, rows : 2 * rows])[:, None] + tree_sums
+    attended = ((summed[:rows] + tree_numerator) / denominator).astype(bf16)
+    attended = in_order(collect(attended), ahead).reshape(head_count, 2, tree_size, HEAD_SIZE)
+    attention_out = jnp.einsum(
+        "hgtc,hgcd->td",
+        attended,
+        output_projection.reshape(head_count, 2, HEAD_SIZE, width),
+        preferred_element_type=f32,
+    )
+    attention_out = attention_out[:tok_block] + swap(
+        attention_out[tok_block:].astype(bf16), "kv", 1
+    ).astype(f32)
+
+    def token_totals(*values):
+        lanes = 128 // len(values)
+        columns = [jnp.sum(value, axis=-1, keepdims=True) for value in values]
+        columns = jnp.concatenate(
+            [jnp.broadcast_to(column, (tok_block, lanes)) for column in columns], axis=-1
+        )
+        columns = add_up(collect(columns))
+        return [columns[:, k * lanes : k * lanes + 1] for k in range(len(values))]
+
+    (totals,) = token_totals(attention_out * attention_out)
+    first_sum = (
+        own_state.astype(f32) + attention_out * inverse_of(totals) * norm_post_attention
+    ).astype(bf16)
+
+    all_state = lax.all_gather(first_sum, plane, axis=0, tiled=True)
+    all_float = all_state.astype(f32)
+    scaled_ffn = (all_float * norm_pre_feedforward).astype(bf16)
+    square_lanes = split_lanes(jnp.sum(all_float * all_float, axis=-1, keepdims=True))
+    share = row_count // seq_count
+    units = down_weight.shape[0]
+    partial = jnp.einsum(
+        "td,dcf->ctf", scaled_ffn, gate_up_weight, preferred_element_type=f32
+    ).astype(bf16)
+
+    node_at = jnp.arange(tree_size, dtype=jnp.int32)
+    node_at = jnp.where(kv_at == 0, node_at, (node_at + tok_block) % tree_size)
+    accept_pick = (accepted_path[0][:, None] == node_at[None, :]).astype(bf16)
+    chosen = jnp.dot(
+        accept_pick,
+        jnp.concatenate([new_keys, new_values], axis=1),
+        preferred_element_type=f32,
+    ).astype(bf16)
+    chosen = in_order(collect(chosen), ahead)
+    accept_count = chosen.shape[1]
+    chosen = chosen.reshape(head_count, accept_count, 2, HEAD_SIZE).transpose(2, 1, 0, 3)
+    chosen, partial = lax.optimization_barrier((chosen, partial))
+    keys_updated, values_updated, flag = update_caches(
+        cache_keys[0], cache_values[0], chosen, (length - block_start).reshape(1)
+    )
+
+    pieces = 2
+    piece = units // pieces
+    ffn_out = 0.0
+    for p in range(pieces):
+        window = slice(p * piece, (p + 1) * piece)
+        gate = partial[0, :, window]
+        up = partial[1, :, window]
+        if p == 0:
+            gate = jnp.concatenate([gate, square_lanes], axis=-1)
+        lanes = gate.shape[1]
+        both = jnp.concatenate([gate, up], axis=-1).reshape(seq_count, share, lanes + piece)
+        summed = add_up(
+            [lax.dynamic_index_in_dim(both, seq_at, 0, False)]
+            + send_ahead(lambda j: lax.dynamic_index_in_dim(both, ahead[j], 0, False))
+        )
+        if p == 0:
+            inverse = inverse_of(summed[:, piece : piece + 1] + summed[:, piece + 64 : piece + 65])
+            flag, summed = lax.optimization_barrier((flag, summed))
+        activated = (
+            jax.nn.gelu(summed[:, :piece] * inverse, approximate=True)
+            * (summed[:, lanes:] * inverse)
+        ).astype(bf16)
+        activated = in_order(collect(activated), ahead).reshape(row_count, piece)
+        ffn_out = ffn_out + jnp.dot(activated, down_weight[window], preferred_element_type=f32)
+    ffn_out = ffn_out.astype(bf16).reshape(groups, tok_block, width)
+    ffn_out = add_up(list(lax.all_to_all(ffn_out, plane, 0, 0)))
+    first_float = first_sum.astype(f32)
+    scaled_out = ffn_out * norm_post_feedforward
+    out_total, first_total, cross_total, scaled_total = token_totals(
+        ffn_out * ffn_out, first_float * first_float, first_float * scaled_out, scaled_out * scaled_out
+    )
+    inverse = inverse_of(out_total)
+    second_sum = (first_float + scaled_out * inverse).astype(bf16)
+    second_total = first_total + inverse * (2.0 * cross_total + inverse * scaled_total)
+    normed = (
+        second_sum.astype(f32) * inverse_of(jnp.maximum(second_total, 0.0)) * norm_final
+    ).astype(bf16)
+
+    gathered = lax.all_gather(normed, plane, axis=0, tiled=True)
+    lifted = jnp.einsum(
+        "td,ndc->ntc", gathered, draft_weight, preferred_element_type=f32
+    ).astype(bf16)
+    summed = add_up(
+        [lax.dynamic_index_in_dim(lifted, seq_at, 0, False)]
+        + send_ahead(lambda j: lax.dynamic_index_in_dim(lifted, ahead[j], 0, False))
+    )
+    bias = lax.dynamic_index_in_dim(draft_bias, seq_at, 0, True)
+    branch = jax.nn.silu(summed + bias).astype(bf16)
+    branch = lax.all_to_all(branch.reshape(groups, tok_block, -1), plane, 0, 0)
+    branch = branch.transpose(1, 0, 2).reshape(tok_block, MODEL_WIDTH)
+    base = in_order(collect(normed), ahead)
+    base = jnp.concatenate([base[s] for s in range(seq_count)], axis=-1)
+    token_rows = jnp.concatenate([base] + collect(branch), axis=0)
+    raw = jnp.concatenate(
+        [
+            lax.dot_general(
+                token_rows, block, (((1,), (1,)), ((), ())), preferred_element_type=f32
+            )
+            for block in vocab_blocks
+        ],
+        axis=1,
+    ).reshape(seq_count + 1, tok_block, -1)
+    raw = jnp.concatenate([raw[:1], raw[:1] + raw[1:]], axis=0)
+    logits = LOGIT_CAP * jnp.tanh(raw / LOGIT_CAP)
+    totals = jnp.sum(jnp.exp(logits), axis=-1)
+
+    vocab_rows = vocab_weight.shape[0]
+
+    def first_entry(kv_bit, vocab_bits):
+        place = ((kv_at ^ kv_bit) * seq_count + seq_at) * tenants + (vocab_at ^ vocab_bits)
+        return place * vocab_rows
+
+    entries = []
+    for core in (0, 1):
+        for kv_bit, vocab_bits in ((0, 0), (1, 0), (0, 2), (1, 2)):
+            entries.append(
+                first_entry(kv_bit, vocab_bits ^ core) + jnp.arange(vocab_rows, dtype=jnp.int32)
+            )
+    entries = jnp.concatenate(entries)
+    candidates = lax.dynamic_slice(
+        candidate_tokens,
+        (0, kv_at * tok_block, vocab_at, 0),
+        (seq_count + 1, tok_block, 1, CAND),
+    )[:, :, 0]
+    candidates = jnp.concatenate(
+        [candidates[:1]]
+        + [lax.dynamic_slice_in_dim(candidates, 1 + ahead[j], 1, 0) for j in range(seq_count)],
+        axis=0,
+    )
+    picked = [
+        jnp.sum(
+            jnp.where(entries == candidates[:, :, column : column + 1], logits, 0.0), axis=-1
+        )
+        for column in range(CAND)
+    ]
+    tally = jnp.stack([totals] + picked)
+    draft_tally = in_order([tally[:, 1 + j] for j in range(seq_count)], ahead)
+    tally = jnp.concatenate([tally[:, 0][None], draft_tally], axis=0)
+    head_total = seq_count + 1
+    tally = add_up(collect(tally.reshape(head_total * (CAND + 1), tok_block)))
+    tally = lax.all_gather(tally, plane, axis=0)
+    tally = tally.reshape(kv_count, tenants, head_total, CAND + 1, tok_block)
+    log_normalizer = jnp.log(
+        tally[:, :, :, 0].transpose(2, 0, 3, 1).reshape(head_total, tree_size, tenants)
+    )
+    candidate_logits = (
+        tally[:, :, :, 1:]
+        .transpose(2, 0, 4, 1, 3)
+        .reshape(head_total, tree_size, tenants, CAND)
+    )
+    return (keys_updated[None], values_updated[None], log_normalizer, candidate_logits)
+
+
 def solution(mesh):
     placed = (
         P("kv", "vocab", "seq"),
@@ -253,8 +657,9 @@
         P(("kv", "seq", "vocab"), None),
         P(),
     )
+    body = local if fits(mesh.shape) else local_general
     return jax.shard_map(
-        local,
+        body,
         mesh=mesh,
         in_specs=placed,
         out_specs=(P("vocab", "seq", "kv", None), P("vocab", "seq", "kv", None), P(), P()),

time: 544 us -> 645 us (1.19)
  Pallas kernels: 0 us -> 257 us
  waiting for transfers between devices: 282 us -> 120 us
  starting transfers between devices: 0.33 us -> 81.8 us
  blocking collectives: 129 us -> 98.1 us
  local copies, waits for them, and re-layouts: 42.1 us -> 22 us
  matrix products: 59.9 us -> 40.7 us
  between operations: 15.2 us -> 2.41 us
  other arithmetic: 14.2 us -> 20.9 us
    pallas_call x0 -> x1, Pallas kernels: none -> 257 us  [update_caches(): pl.pallas_call(kernel, out_shape=(like, like, jax.ShapeDtypeStruct((8, 12...]
    psum x4 -> x0, waiting for transfers between devices: 203 us -> none  [the longest x1 96.3 us: local(): gate_up, ffn_squares = lax.psum((gate_up, ffn_squares), 'seq')]
    ppermute x0 -> x59, waiting for transfers between devices: none -> 112 us  [the longest x30 40.6 us: collect(): lax.ppermute(block, 'seq', [(i, (i - j) % count) for i in range(count)])]
    psum x7 -> x0, blocking collectives: 104 us -> none  [the longest x1 40.7 us: local(): totals, picked = lax.psum((totals, picked), ('kv', 'seq', 'vocab'))]
    ppermute x0 -> x59, starting transfers between devices: none -> 75 us  [the longest x30 39.4 us: collect(): lax.ppermute(block, 'seq', [(i, (i - j) % count) for i in range(count)])]
    all_gather x3, blocking collectives: 24.9 us -> 98.1 us  [the longest x1 75.3 us: local(): all_state = lax.all_gather(first_sum, plane, axis=0, tiled=True)]
    unnamed x10 -> x0, waiting for transfers between devices: 44.4 us -> none
    all_gather x2 -> x0, waiting for transfers between devices: 35.1 us -> none  [the longest x1 35.1 us: local(): lax.all_gather(branch, ('kv', 'vocab'), axis=2, tiled=True)]
  transfers between devices with their start and end apart: 8 -> 61, of which waited for: 7 -> 29; matrix products, arithmetic and copies ran while one was open for 10% -> 10% of each run, Pallas kernels for 0% -> 40%
where the time goes in v2:
time: 645 us; the launch traced here: 643 us
  Pallas kernels  257 us (40%)
  waiting for transfers between devices  120 us (19%)
  blocking collectives  98.1 us (15%)
  starting transfers between devices  81.8 us (13%)
  matrix products  40.7 us (6%)
  local copies, waits for them, and re-layouts  22 us (3%)
  other arithmetic  20.9 us (3%)
    pallas_call x1, Pallas kernels, update_caches(): pl.pallas_call(kernel, out_shape=(like, like, jax.ShapeDtypeStruct((8, 12...  257 us
    all_gather x1, blocking collectives, local(): all_state = lax.all_gather(first_sum, plane, axis=0, tiled=True)  75.3 us
    ppermute x30, waiting for transfers between devices, collect(): lax.ppermute(block, 'seq', [(i, (i - j) % count) for i in range(count)])  40.6 us
    ppermute x18, waiting for transfers between devices, send_ahead(): lax.ppermute(pick(j), 'seq', [(i, (i + j) % count) for i in range(count)])  39.6 us
    ppermute x30, starting transfers between devices, collect(): lax.ppermute(block, 'seq', [(i, (i - j) % count) for i in range(count)])  39.4 us
    ppermute x11, waiting for transfers between devices, swap(): return lax.ppermute(values, axis, [(i, i ^ bit) for i in range(count)])  31.6 us
    ppermute x18, starting transfers between devices, send_ahead(): lax.ppermute(pick(j), 'seq', [(i, (i + j) % count) for i in range(count)])  26.8 us
    dot_general x10, matrix products, local(): lax.dot_general(token_rows, block, (((1,), (1,)), ((), ())), preferred_el...  18.6 us
  transfers between devices with their start and end apart: 61, of which 29 were waited for; matrix products, arithmetic and copies ran while one was open for 10% of the time, Pallas kernels for 40%

profile of v2, /device:TPU:0, one launch (start us, length us, event | category | flops | bytes accessed | tf_op | source)
XLA Modules:
  0.0 643.2 jit_solution(15769086713299357079)
XLA Ops:
  8.4 7.5 %fusion.34 = bf16[4,48,1024]{2,1,0:T(8,128)(2,1)S(1)} fusion(bf16[896,4,1024]{2,1,0:T(4,128)(2,1)} %param.20, f32[896]{0:T(1024)} %param.22, bf16[24,896]{1,0:T(8,128)(2,1)S(1)} %collective-permute-done, bf16[24,896]{1,0:T(8,128)(2,1)} %bitcast.298), kind=kOutput, calls=%fused_computation.34 | convolution fusion | flops 352776192 | bytes 7822848 | tf_op jit(solution)/shard_map/td,dhc->htc/dot_general | solution.py:396
  54.6 3.6 collective-permute-done.17
  79.9 75.3 %all_gather.12 = bf16[192,896]{1,0:T(8,128)(2,1)S(1)} all-gather(bf16[24,896]{1,0:T(8,128)(2,1)S(1)} %add_convert_fusion), channel_id=1, replica_groups=mesh['kv'=2,'seq'=4,'vocab'=4] {'kv','vocab'}, dimensions={0}, use_global_device_ids=true | all-gather | bytes 387072 | tf_op jit(solution)/shard_map/all_gather | solution.py:499
  155.9 4.4 fusion.15
  174.9 7.2 %collective-permute-done.30 = bf16[48,1792]{1,0:T(8,128)(2,1)} collective-permute-done((bf16[48,1792]{1,0:T(8,128)(2,1)}, bf16[48,1792]{1,0:T(8,128)(2,1)}, u32[]{:S(2)}, u32[]{:S(2)}) %collective-permute-start.30) | collective-permute-done | bytes 172064 | tf_op jit(solution)/shard_map/ppermute | solution.py:243
  182.1 3.8 collective-permute-start.25
  187.1 9.9 %collective-permute-done.24 = bf16[48,1920]{1,0:T(8,128)(2,1)S(1)} collective-permute-done((bf16[48,1920]{1,0:T(8,128)(2,1)S(1)}, bf16[48,1920]{1,0:T(8,128)(2,1)S(1)}, u32[]{:S(2)}, u32[]{:S(2)}) %collective-permute-start.24) | collective-permute-done | bytes 184352 | tf_op jit(solution)/shard_map/ppermute | solution.py:243
  197.0 3.8 collective-permute-done.25
  207.7 8.3 %collective-permute-done.33 = bf16[48,896]{1,0:T(8,128)(2,1)S(1)} collective-permute-done((bf16[48,896]{1,0:T(8,128)(2,1)S(1)}, bf16[48,896]{1,0:T(8,128)(2,1)S(1)}, u32[]{:S(2)}, u32[]{:S(2)}) %collective-permute-start.33) | collective-permute-done | bytes 86048 | tf_op jit(solution)/shard_map/ppermute | solution.py:251
  216.1 6.3 collective-permute-done.34
  223.0 5.6 collective-permute-done.28
  229.9 3.4 all-to-all-start
  251.6 9.5 %all_gather.13 = bf16[192,896]{1,0:T(8,128)(2,1)S(1)} all-gather(bf16[24,896]{1,0:T(8,128)(2,1)S(1)} %get-tuple-element.28), channel_id=1, replica_groups=mesh['kv'=2,'seq'=4,'vocab'=4] {'kv','vocab'}, dimensions={0}, use_global_device_ids=true | all-gather | bytes 387072 | tf_op jit(solution)/shard_map/all_gather | solution.py:563
  267.8 4.1 collective-permute-done.41
  272.0 7.8 %collective-permute-done.42 = bf16[192,448]{1,0:T(8,128)(2,1)S(1)} collective-permute-done((bf16[192,448]{1,0:T(8,128)(2,1)S(1)}, bf16[192,448]{1,0:T(8,128)(2,1)S(1)}, u32[]{:S(2)}, u32[]{:S(2)}) %collective-permute-start.42) | collective-permute-done | bytes 172064 | tf_op jit(solution)/shard_map/ppermute | solution.py:243
  280.7 3.4 all-to-all-start.1
  284.1 5.6 all-to-all-done.1
  290.0 5.8 collective-permute-start.44
  300.6 8.8 %collective-permute-start.46 = (bf16[24,3584]{1,0:T(8,128)(2,1)S(1)}, bf16[24,3584]{1,0:T(8,128)(2,1)S(1)}, u32[]{:S(2)}, u32[]{:S(2)}) collective-permute-start(bf16[24,3584]{1,0:T(8,128)(2,1)S(1)} %reshape.242), channel_id=1, source_target_pairs={{0,4},{4,8},{8,12},{12,0},{1,5},{5,9},{9,13},{13,1},{2,6},{6,10},{... | collective-permute-start | bytes 516104 | tf_op jit(solution)/shard_map/ppermute | solution.py:251
  314.8 3.3 convolution_dynamic-update-slice_fusion.5
  321.4 30.3 %collective-permute-done.49 = bf16[256,3584]{1,0:T(8,128)(2,1)S(1)} collective-permute-done((bf16[256,3584]{1,0:T(8,128)(2,1)S(1)}, bf16[256,3584]{1,0:T(8,128)(2,1)S(1)}, u32[]{:S(2)}, u32[]{:S(2)}) %collective-permute-start.49) | collective-permute-done | bytes 1835040 | tf_op jit(solution)/shard_map/ppermute | solution.py:272
  357.8 3.3 convolution_dynamic-update-slice_fusion.2
  371.1 256.8 %shard_map.210 = (bf16[2048,4,256]{2,1,0:T(4,128)(2,1)}, bf16[2048,4,256]{2,1,0:T(4,128)(2,1)}, f32[8,128]{1,0:T(8,128)}) custom-call(s32[1]{0:T(128)} %bitcast.1.offset_ref, bf16[2,5,4,256]{3,2,1,0:T(4,128)(2,1)} %bitcast.300, bf16[2048,4,256]{2,1,0:T(4,128)(2,1)} %bitcast.278, bf16[2048,4,256]{2,1,0:T(4,128)(2,1)} %bitcast.280), custom_call_target="tpu_custom_call" | custom-call | bytes 16777216 | tf_op jit(solution)/shard_map/pallas_call | solution.py:328
  628.0 13.4 %all-gather.1 = f32[8,45,24]{1,2,0:T(8,128)S(1)} all-gather(f32[1,45,24]{1,2,0:T(8,128)S(1)} %copy.120), channel_id=2, replica_groups=mesh['kv'=2,'seq'=4,'vocab'=4] {'kv','vocab'}, dimensions={0}, use_global_device_ids=true | all-gather | bytes 38880 | tf_op jit(solution)/shard_map/all_gather | solution.py:625
  (319 shorter events, 149.5 us)
Async XLA Ops:
  73.1 223.1 %collective-permute-start.47 = (bf16[512,3584]{1,0:T(8,128)(2,1)}, bf16[512,3584]{1,0:T(8,128)(2,1)}, u32[]{:S(2)}, u32[]{:S(2)}) collective-permute-start(bf16[512,3584]{1,0:T(8,128)(2,1)} %param.36), channel_id=1, source_target_pairs={{0,16},{16,0},{1,17},{17,1},{2,18},{18,2},{3,19},{19,3},{4,20},{20... | collective-permute-start | bytes 11010056 | tf_op jit(solution)/shard_map/ppermute | solution.py:272
  75.1 237.1 %collective-permute-start.48 = (bf16[512,3584]{1,0:T(8,128)(2,1)}, bf16[512,3584]{1,0:T(8,128)(2,1)}, u32[]{:S(2)}, u32[]{:S(2)}) collective-permute-start(bf16[512,3584]{1,0:T(8,128)(2,1)} %param.36), channel_id=1, source_target_pairs={{0,2},{1,3},{2,0},{3,1},{4,6},{5,7},{6,4},{7,5},{8,10},{9,11},{10,... | collective-permute-start | bytes 11010056 | tf_op jit(solution)/shard_map/ppermute | solution.py:272
  166.6 15.5 %collective-permute-start.30 = (bf16[48,1792]{1,0:T(8,128)(2,1)}, bf16[48,1792]{1,0:T(8,128)(2,1)}, u32[]{:S(2)}, u32[]{:S(2)}) collective-permute-start(bf16[48,1792]{1,0:T(8,128)(2,1)} %get-tuple-element.56), channel_id=1, source_target_pairs={{0,8},{4,12},{8,0},{12,4},{1,9},{5,13},{9,1},{13,5},{2,10},{6,14},... | collective-permute-start | bytes 516104 | tf_op jit(solution)/shard_map/ppermute | solution.py:243
  168.2 13.9 %collective-permute-start.31 = (bf16[48,1792]{1,0:T(8,128)(2,1)}, bf16[48,1792]{1,0:T(8,128)(2,1)}, u32[]{:S(2)}, u32[]{:S(2)}) collective-permute-start(bf16[48,1792]{1,0:T(8,128)(2,1)} %get-tuple-element.57), channel_id=1, source_target_pairs={{0,12},{4,0},{8,4},{12,8},{1,13},{5,1},{9,5},{13,9},{2,14},{6,2},{... | collective-permute-start | bytes 516104 | tf_op jit(solution)/shard_map/ppermute | solution.py:243
  174.7 12.4 %collective-permute-start.23 = (bf16[48,1920]{1,0:T(8,128)(2,1)S(1)}, bf16[48,1920]{1,0:T(8,128)(2,1)S(1)}, u32[]{:S(2)}, u32[]{:S(2)}) collective-permute-start(bf16[48,1920]{1,0:T(8,128)(2,1)S(1)} %get-tuple-element.52), channel_id=1, source_target_pairs={{0,4},{4,8},{8,12},{12,0},{1,5},{5,9},{9,13},{13,1},{2,6},{6,10},{... | collective-permute-start | bytes 552968 | tf_op jit(solution)/shard_map/ppermute | solution.py:243
  182.1 14.9 %collective-permute-start.24 = (bf16[48,1920]{1,0:T(8,128)(2,1)S(1)}, bf16[48,1920]{1,0:T(8,128)(2,1)S(1)}, u32[]{:S(2)}, u32[]{:S(2)}) collective-permute-start(bf16[48,1920]{1,0:T(8,128)(2,1)S(1)} %get-tuple-element.54), channel_id=1, source_target_pairs={{0,8},{4,12},{8,0},{12,4},{1,9},{5,13},{9,1},{13,5},{2,10},{6,14},... | collective-permute-start | bytes 552968 | tf_op jit(solution)/shard_map/ppermute | solution.py:243
  182.1 18.7 %collective-permute-start.25 = (bf16[48,1920]{1,0:T(8,128)(2,1)S(1)}, bf16[48,1920]{1,0:T(8,128)(2,1)S(1)}, u32[]{:S(2)}, u32[]{:S(2)}) collective-permute-start(bf16[48,1920]{1,0:T(8,128)(2,1)S(1)} %get-tuple-element.53), channel_id=1, source_target_pairs={{0,12},{4,0},{8,4},{12,8},{1,13},{5,1},{9,5},{13,9},{2,14},{6,2},{... | collective-permute-start | bytes 552968 | tf_op jit(solution)/shard_map/ppermute | solution.py:243
  202.7 20.2 %collective-permute-start.26 = (bf16[48,896]{1,0:T(8,128)(2,1)S(1)}, bf16[48,896]{1,0:T(8,128)(2,1)S(1)}, u32[]{:S(2)}, u32[]{:S(2)}) collective-permute-start(bf16[48,896]{1,0:T(8,128)(2,1)S(1)} %get-tuple-element.31), channel_id=1, source_target_pairs={{0,12},{4,0},{8,4},{12,8},{1,13},{5,1},{9,5},{13,9},{2,14},{6,2},{... | collective-permute-start | bytes 258056 | tf_op jit(solution)/shard_map/ppermute | solution.py:251
  203.6 19.4 %collective-permute-start.27 = (bf16[48,896]{1,0:T(8,128)(2,1)S(1)}, bf16[48,896]{1,0:T(8,128)(2,1)S(1)}, u32[]{:S(2)}, u32[]{:S(2)}) collective-permute-start(bf16[48,896]{1,0:T(8,128)(2,1)S(1)} %get-tuple-element.31), channel_id=1, source_target_pairs={{0,8},{4,12},{8,0},{12,4},{1,9},{5,13},{9,1},{13,5},{2,10},{6,14},... | collective-permute-start | bytes 258056 | tf_op jit(solution)/shard_map/ppermute | solution.py:251
  249.0 13.2 %collective-permute-start.38 = (bf16[24,896]{1,0:T(8,128)(2,1)S(1)}, bf16[24,896]{1,0:T(8,128)(2,1)S(1)}, u32[]{:S(2)}, u32[]{:S(2)}) collective-permute-start(bf16[24,896]{1,0:T(8,128)(2,1)S(1)} %get-tuple-element.28), channel_id=1, source_target_pairs={{0,12},{4,0},{8,4},{12,8},{1,13},{5,1},{9,5},{13,9},{2,14},{6,2},{... | collective-permute-start | bytes 129032 | tf_op jit(solution)/shard_map/ppermute | solution.py:251
  251.0 14.2 %collective-permute-start.39 = (bf16[24,896]{1,0:T(8,128)(2,1)S(1)}, bf16[24,896]{1,0:T(8,128)(2,1)S(1)}, u32[]{:S(2)}, u32[]{:S(2)}) collective-permute-start(bf16[24,896]{1,0:T(8,128)(2,1)S(1)} %get-tuple-element.28), channel_id=1, source_target_pairs={{0,8},{4,12},{8,0},{12,4},{1,9},{5,13},{9,1},{13,5},{2,10},{6,14},... | collective-permute-start | bytes 129032 | tf_op jit(solution)/shard_map/ppermute | solution.py:251
  251.0 15.2 %collective-permute-start.40 = (bf16[24,896]{1,0:T(8,128)(2,1)S(1)}, bf16[24,896]{1,0:T(8,128)(2,1)S(1)}, u32[]{:S(2)}, u32[]{:S(2)}) collective-permute-start(bf16[24,896]{1,0:T(8,128)(2,1)S(1)} %get-tuple-element.28), channel_id=1, source_target_pairs={{0,4},{4,8},{8,12},{12,0},{1,5},{5,9},{9,13},{13,1},{2,6},{6,10},{... | collective-permute-start | bytes 129032 | tf_op jit(solution)/shard_map/ppermute | solution.py:251
  265.2 14.6 %collective-permute-start.42 = (bf16[192,448]{1,0:T(8,128)(2,1)S(1)}, bf16[192,448]{1,0:T(8,128)(2,1)S(1)}, u32[]{:S(2)}, u32[]{:S(2)}) collective-permute-start(bf16[192,448]{1,0:T(8,128)(2,1)S(1)} %get-tuple-element.51), channel_id=1, source_target_pairs={{0,8},{4,12},{8,0},{12,4},{1,9},{5,13},{9,1},{13,5},{2,10},{6,14},... | collective-permute-start | bytes 516104 | tf_op jit(solution)/shard_map/ppermute | solution.py:243
  266.2 13.7 %collective-permute-start.43 = (bf16[192,448]{1,0:T(8,128)(2,1)S(1)}, bf16[192,448]{1,0:T(8,128)(2,1)S(1)}, u32[]{:S(2)}, u32[]{:S(2)}) collective-permute-start(bf16[192,448]{1,0:T(8,128)(2,1)S(1)} %get-tuple-element.50), channel_id=1, source_target_pairs={{0,12},{4,0},{8,4},{12,8},{1,13},{5,1},{9,5},{13,9},{2,14},{6,2},{... | collective-permute-start | bytes 516104 | tf_op jit(solution)/shard_map/ppermute | solution.py:243
  272.0 85.8 %collective-permute-start.51 = (bf16[512,3584]{1,0:T(8,128)(2,1)}, bf16[512,3584]{1,0:T(8,128)(2,1)}, u32[]{:S(2)}, u32[]{:S(2)}) collective-permute-start(bf16[512,3584]{1,0:T(8,128)(2,1)} %param.36), channel_id=1, source_target_pairs={{0,1},{1,0},{2,3},{3,2},{4,5},{5,4},{6,7},{7,6},{8,9},{9,8},{10,11... | collective-permute-start | bytes 11010056 | tf_op jit(solution)/shard_map/ppermute | solution.py:272
  295.8 15.3 %collective-permute-start.45 = (bf16[24,3584]{1,0:T(8,128)(2,1)S(1)}, bf16[24,3584]{1,0:T(8,128)(2,1)S(1)}, u32[]{:S(2)}, u32[]{:S(2)}) collective-permute-start(bf16[24,3584]{1,0:T(8,128)(2,1)S(1)} %reshape.242), channel_id=1, source_target_pairs={{0,8},{4,12},{8,0},{12,4},{1,9},{5,13},{9,1},{13,5},{2,10},{6,14},... | collective-permute-start | bytes 516104 | tf_op jit(solution)/shard_map/ppermute | solution.py:251
  296.2 64.9 %collective-permute-start.52 = (bf16[512,3584]{1,0:T(8,128)(2,1)}, bf16[512,3584]{1,0:T(8,128)(2,1)S(1)}, u32[]{:S(2)}, u32[]{:S(2)}) collective-permute-start(bf16[512,3584]{1,0:T(8,128)(2,1)} %collective-permute-done.47), channel_id=1, source_target_pairs={{0,1},{1,0},{2,3},{3,2},{4,5},{5,4},{6,7},{7,6},{8,9},{9,8},{10,11... | collective-permute-start | bytes 11010056 | tf_op jit(solution)/shard_map/ppermute | solution.py:272
  300.6 13.2 %collective-permute-start.46 = (bf16[24,3584]{1,0:T(8,128)(2,1)S(1)}, bf16[24,3584]{1,0:T(8,128)(2,1)S(1)}, u32[]{:S(2)}, u32[]{:S(2)}) collective-permute-start(bf16[24,3584]{1,0:T(8,128)(2,1)S(1)} %reshape.242), channel_id=1, source_target_pairs={{0,4},{4,8},{8,12},{12,0},{1,5},{5,9},{9,13},{13,1},{2,6},{6,10},{... | collective-permute-start | bytes 516104 | tf_op jit(solution)/shard_map/ppermute | solution.py:251
  311.1 40.6 %collective-permute-start.49 = (bf16[256,3584]{1,0:T(8,128)(2,1)S(1)}, bf16[256,3584]{1,0:T(8,128)(2,1)S(1)}, u32[]{:S(2)}, u32[]{:S(2)}) collective-permute-start(bf16[256,3584]{1,0:T(8,128)(2,1)S(1)} %slice.322), channel_id=1, source_target_pairs={{0,2},{1,3},{2,0},{3,1},{4,6},{5,7},{6,4},{7,5},{8,10},{9,11},{10,... | collective-permute-start | bytes 5505032 | tf_op jit(solution)/shard_map/ppermute | solution.py:272
  312.2 50.2 %collective-permute-start.53 = (bf16[512,3584]{1,0:T(8,128)(2,1)}, bf16[512,3584]{1,0:T(8,128)(2,1)S(1)}, u32[]{:S(2)}, u32[]{:S(2)}) collective-permute-start(bf16[512,3584]{1,0:T(8,128)(2,1)} %collective-permute-done.48), channel_id=1, source_target_pairs={{0,1},{1,0},{2,3},{3,2},{4,5},{5,4},{6,7},{7,6},{8,9},{9,8},{10,11... | collective-permute-start | bytes 11010056 | tf_op jit(solution)/shard_map/ppermute | solution.py:272
  313.9 42.5 %collective-permute-start.50 = (bf16[256,3584]{1,0:T(8,128)(2,1)S(1)}, bf16[256,3584]{1,0:T(8,128)(2,1)S(1)}, u32[]{:S(2)}, u32[]{:S(2)}) collective-permute-start(bf16[256,3584]{1,0:T(8,128)(2,1)S(1)} %slice.323), channel_id=1, source_target_pairs={{0,16},{16,0},{1,17},{17,1},{2,18},{18,2},{3,19},{19,3},{4,20},{20... | collective-permute-start | bytes 5505032 | tf_op jit(solution)/shard_map/ppermute | solution.py:272
  369.1 258.8 %collective-permute-start.56 = (f32[45,24]{1,0:T(8,128)S(1)}, f32[45,24]{1,0:T(8,128)S(1)}, u32[]{:S(2)}, u32[]{:S(2)}) collective-permute-start(f32[45,24]{1,0:T(8,128)S(1)} %reshape.243), channel_id=1, source_target_pairs={{0,12},{4,0},{8,4},{12,8},{1,13},{5,1},{9,5},{13,9},{2,14},{6,2},{... | collective-permute-start | bytes 12968 | tf_op jit(solution)/shard_map/ppermute | solution.py:251
  369.1 258.8 %collective-permute-start.57 = (f32[45,24]{1,0:T(8,128)S(1)}, f32[45,24]{1,0:T(8,128)S(1)}, u32[]{:S(2)}, u32[]{:S(2)}) collective-permute-start(f32[45,24]{1,0:T(8,128)S(1)} %reshape.243), channel_id=1, source_target_pairs={{0,8},{4,12},{8,0},{12,4},{1,9},{5,13},{9,1},{13,5},{2,10},{6,14},... | collective-permute-start | bytes 12968 | tf_op jit(solution)/shard_map/ppermute | solution.py:251
  369.2 258.7 %collective-permute-start.58 = (f32[45,24]{1,0:T(8,128)S(1)}, f32[45,24]{1,0:T(8,128)S(1)}, u32[]{:S(2)}, u32[]{:S(2)}) collective-permute-start(f32[45,24]{1,0:T(8,128)S(1)} %reshape.243), channel_id=1, source_target_pairs={{0,4},{4,8},{8,12},{12,0},{1,5},{5,9},{9,13},{13,1},{2,6},{6,10},{... | collective-permute-start | bytes 12968 | tf_op jit(solution)/shard_map/ppermute | solution.py:251
  (61 other events, 1004.7 us)

commit v3 on v2

--- a/solution.py
+++ b/solution.py
@@ -279,6 +279,19 @@
     return jnp.concatenate([jnp.broadcast_to(high, shape), jnp.broadcast_to(low, shape)], axis=-1)
 
 
+def zero_at(event):
+    corner = event.reshape(-1)[0] if event.ndim < 2 else event[(0,) * event.ndim]
+    return (jnp.abs(corner.astype(jnp.float32)) > 3e38).astype(jnp.int32)
+
+
+def still(*values):
+    return sum(value[(0,) * value.ndim].astype(jnp.float32) * 0.0 for value in values)
+
+
+def rows_after(values, first, count, event):
+    return lax.dynamic_slice_in_dim(values, first + zero_at(event), count, 0)
+
+
 def inverse_of(totals):
     return lax.rsqrt(totals / MODEL_WIDTH + EPSILON)
 
@@ -292,26 +305,32 @@
 
 
 def update_caches(cache_keys, cache_values, rows, offset):
-    slots = cache_keys.shape[0]
+    slots, heads, size = cache_keys.shape
     accept = rows.shape[1]
-    parts = 4
-    piece = slots // parts
-
-    def kernel(offset_ref, rows_ref, keys_in, values_in, keys_out, values_out, flag, sems):
+    piece = 256
+    parts = slots // piece
+
+    def kernel(
+        offset_ref, rows_ref, keys_in, values_in, keys_out, values_out, flag, held, get, put, sem
+    ):
         flag[...] = jnp.zeros_like(flag)
-        copies = []
-        for which, (source, target) in enumerate(((keys_in, keys_out), (values_in, values_out))):
-            for p in range(parts):
-                window = pl.ds(p * piece, piece)
-                copies.append(
-                    pltpu.make_async_copy(
-                        source.at[window], target.at[window], sems.at[which * parts + p]
-                    )
-                )
-        for copy in copies:
-            copy.start()
-        for copy in copies:
-            copy.wait()
+
+        def copies(number):
+            source, target = ((keys_in, keys_out), (values_in, values_out))[number // parts]
+            window = pl.ds(number % parts * piece, piece)
+            return (
+                pltpu.make_async_copy(source.at[window], held.at[number], get.at[number]),
+                pltpu.make_async_copy(held.at[number], target.at[window], put.at[number]),
+            )
+
+        pairs = [copies(number) for number in range(2 * parts)]
+        for inward, _ in pairs:
+            inward.start()
+        for inward, outward in pairs:
+            inward.wait()
+            outward.start()
+        for _, outward in pairs:
+            outward.wait()
         for which, target in enumerate((keys_out, values_out)):
             for a in range(accept):
                 slot = offset_ref[0] + a
@@ -319,7 +338,7 @@
                 @pl.when((slot >= 0) & (slot < slots))
                 def _():
                     copy = pltpu.make_async_copy(
-                        rows_ref.at[which, pl.ds(a, 1)], target.at[pl.ds(slot, 1)], sems.at[0]
+                        rows_ref.at[which, pl.ds(a, 1)], target.at[pl.ds(slot, 1)], sem.at[0]
                     )
                     copy.start()
                     copy.wait()
@@ -331,19 +350,114 @@
         in_specs=[
             pl.BlockSpec(memory_space=pltpu.SMEM),
             pl.BlockSpec(memory_space=pltpu.VMEM),
-            pl.BlockSpec(memory_space=pl.ANY),
-            pl.BlockSpec(memory_space=pl.ANY),
+            pl.BlockSpec(memory_space=pltpu.HBM),
+            pl.BlockSpec(memory_space=pltpu.HBM),
         ],
         out_specs=(
-            pl.BlockSpec(memory_space=pl.ANY),
-            pl.BlockSpec(memory_space=pl.ANY),
+            pl.BlockSpec(memory_space=pltpu.HBM),
+            pl.BlockSpec(memory_space=pltpu.HBM),
             pl.BlockSpec(memory_space=pltpu.VMEM),
         ),
-        scratch_shapes=[pltpu.SemaphoreType.DMA((2 * parts,))],
+        scratch_shapes=[
+            pltpu.VMEM((2 * parts, piece, heads, size), cache_keys.dtype),
+            pltpu.SemaphoreType.DMA((2 * parts,)),
+            pltpu.SemaphoreType.DMA((2 * parts,)),
+            pltpu.SemaphoreType.DMA((1,)),
+        ],
+        compiler_params=pltpu.CompilerParams(vmem_limit_bytes=24 * 2**20),
         cost_estimate=pl.CostEstimate(
             flops=0, bytes_accessed=4 * cache_keys.size * 2, transcendentals=0
         ),
     )(offset, rows, cache_keys, cache_values)
+
+
+def score_vocabulary(numbers, candidates, base, own, other, blocks, lanes):
+    tokens, width = own[0].shape
+    share = base[0].shape[1]
+    count = len(own)
+    extent = sum(part.shape[0] for part in blocks[0])
+    parts = [part for block in blocks for part in block]
+    inputs = base + own + other
+
+    def kernel(numbers_ref, candidates_ref, *rest):
+        vectors, rest = rest[: len(inputs)], rest[len(inputs) :]
+        sources, (out_ref, held, wide, narrow, sems) = rest[: len(parts)], rest[len(parts) :]
+        number = 0
+        for b, block in enumerate(blocks):
+            first = 0
+            for part in block:
+                rows = part.shape[0]
+                pltpu.make_async_copy(
+                    sources[number], held.at[b, pl.ds(first, rows)], sems.at[b]
+                ).start()
+                number += 1
+                first += rows
+        for core in range(2):
+            wide[pl.ds(core * lanes + (count + 1) * tokens, lanes - (count + 1) * tokens), :] = (
+                jnp.zeros((lanes - (count + 1) * tokens, width), jnp.float32)
+            )
+        for j in range(count):
+            place = numbers_ref[len(blocks) + j]
+            columns = pl.ds(pl.multiple_of(place * share, 128), share)
+            block = vectors[j][...].astype(jnp.float32)
+            for core in range(2):
+                wide[pl.ds(core * lanes, tokens), columns] = block[
+                    core * tokens : (core + 1) * tokens
+                ]
+                first = pl.multiple_of(core * lanes + (place + 1) * tokens, 8)
+                wide[pl.ds(first, tokens), :] = vectors[count * (core + 1) + j][...].astype(
+                    jnp.float32
+                )
+        narrow[...] = wide[...].astype(narrow.dtype)
+        lane = lax.broadcasted_iota(jnp.int32, (extent, lanes), 1)
+        row = lax.broadcasted_iota(jnp.int32, (extent, lanes), 0)
+        out_ref[...] = jnp.zeros_like(out_ref)
+
+        def step(b, carry):
+            pltpu.make_async_copy(held.at[b], held.at[b], sems.at[b]).wait()
+            entry = row + numbers_ref[b]
+            both = lax.dot_general(
+                held[b],
+                narrow[...],
+                (((1,), (1,)), ((), ())),
+                preferred_element_type=jnp.float32,
+            )
+            for core in range(2):
+                group = slice(core * lanes, (core + 1) * lanes)
+                raw = both[:, group]
+                first = jnp.where(lane < tokens, raw, 0.0)
+                for head in range(1, count + 1):
+                    raw = raw + pltpu.roll(first, head * tokens, 1)
+                logits = LOGIT_CAP * jnp.tanh(raw / LOGIT_CAP)
+                tally = [jnp.sum(jnp.exp(logits), axis=0, keepdims=True)]
+                for c in range(CAND):
+                    match = entry == candidates_ref[c : c + 1, group]
+                    tally.append(jnp.sum(jnp.where(match, logits, 0.0), axis=0, keepdims=True))
+                out_ref[0 : CAND + 1, group] += jnp.concatenate(tally, axis=0)
+            return carry
+
+        lax.fori_loop(0, len(blocks), step, 0)
+
+    return pl.pallas_call(
+        kernel,
+        out_shape=jax.ShapeDtypeStruct((16, 2 * lanes), jnp.float32),
+        in_specs=[pl.BlockSpec(memory_space=pltpu.SMEM)]
+        + [pl.BlockSpec(memory_space=pltpu.VMEM)] * (1 + len(inputs))
+        + [pl.BlockSpec(memory_space=pltpu.HBM)] * len(parts),
+        out_specs=pl.BlockSpec(memory_space=pltpu.VMEM),
+        scratch_shapes=[
+            pltpu.VMEM((len(blocks), extent, width), own[0].dtype),
+            pltpu.VMEM((2 * lanes, width), jnp.float32),
+            pltpu.VMEM((2 * lanes, width), own[0].dtype),
+            pltpu.SemaphoreType.DMA((len(blocks),)),
+        ],
+        compiler_params=pltpu.CompilerParams(vmem_limit_bytes=40 * 2**20),
+        cost_estimate=pl.CostEstimate(
+            flops=4 * len(blocks) * extent * width * lanes,
+            bytes_accessed=2 * len(blocks) * extent * width,
+            transcendentals=4 * len(blocks) * extent * lanes,
+        ),
+    )(numbers, candidates, *inputs, *parts)
 
 
 def local(
@@ -382,15 +496,15 @@
     ahead = [(seq_at + j) % seq_count for j in range(seq_count)]
     own_state = hidden_state[:, 0, :]
 
-    half = vocab_weight.shape[0] // 2
-    over_kv = swap(vocab_weight, "kv", 1)
-    over_y = swap(vocab_weight, "vocab", 2)
-    far_top = swap(over_kv[:half], "vocab", 2)
-    far_bottom = swap(over_y[half:], "kv", 1)
-    near = [vocab_weight, over_kv, over_y, far_top, far_bottom]
-    vocab_blocks = near + [swap(block, "vocab", 1) for block in near]
-
     tenant_state = jnp.concatenate([own_state, swap(own_state, "kv", 1)], axis=0)
+    vocab_rows = vocab_weight.shape[0]
+    quarter = vocab_rows // 4
+
+    def exchange(first, count, event):
+        rows = rows_after(vocab_weight, first, count, event)
+        return swap(rows, "kv", 1), swap(rows, "vocab", 2)
+
+    kv_0, row_0 = exchange(0, quarter, tenant_state)
     tenant_float = tenant_state.astype(f32)
     scaled_input = (tenant_float * norm_pre_attention).astype(bf16)
     projected = jnp.einsum(
@@ -410,7 +524,7 @@
         [lax.dynamic_index_in_dim(packed, seq_at, 0, False)]
         + send_ahead(lambda j: lax.dynamic_index_in_dim(packed, ahead[j], 0, False))
     )
-    inverse = inverse_of(summed[:, pair : pair + 1] + summed[:, pair + 64 : pair + 65])
+    inverse = inverse_of(summed[:, pair : pair + 1] + summed[:, pair + 64 : pair + 65] + still(kv_0, row_0))
     tree_mask = ancestors[0]
     tree_mask = jnp.where(
         kv_at == 0, tree_mask, jnp.roll(tree_mask, (tok_block, tok_block), (0, 1))
@@ -429,6 +543,7 @@
         ],
         axis=0,
     ).astype(bf16)
+    kv_1, row_1 = exchange(quarter, quarter, query_rows)
     all_queries = in_order(collect(query_rows), ahead)
     fresh = projected[:, :, pair:]
     fresh = add_up(
@@ -453,10 +568,23 @@
     sums = jnp.concatenate(
         [sums_high, sums_low, jnp.zeros((head_count, HEAD_SIZE - 2 * rows), bf16)], axis=-1
     )
+    node_at = jnp.arange(tree_size, dtype=jnp.int32)
+    node_at = jnp.where(kv_at == 0, node_at, (node_at + tok_block) % tree_size)
+    accept_pick = (accepted_path[0][:, None] == node_at[None, :]).astype(bf16)
+    accept_count = accept_pick.shape[0]
+    chosen = jnp.concatenate(
+        [
+            jnp.dot(accept_pick, fresh_part, preferred_element_type=f32).astype(bf16)
+            for fresh_part in (new_keys, new_values)
+        ],
+        axis=0,
+    )
     packed = jnp.concatenate(
         [
             numerator.astype(bf16),
-            jnp.broadcast_to(sums[:, None, :], (head_count, 16, HEAD_SIZE)),
+            sums[:, None, :],
+            jnp.broadcast_to(chosen, (head_count,) + chosen.shape),
+            jnp.zeros((head_count, 15 - 2 * accept_count, HEAD_SIZE), bf16),
         ],
         axis=1,
     )
@@ -468,6 +596,10 @@
     tree_weights = jnp.where(seen, capped_weight(tree_scores), 0.0)
     tree_numerator = jnp.dot(tree_weights.astype(bf16), new_values, preferred_element_type=f32)
     tree_sums = jnp.sum(tree_weights, axis=-1, keepdims=True)
+    behind = [(seq_at - j) % seq_count for j in range(seq_count)]
+    tail = slice(rows + 1, rows + 1 + 2 * accept_count)
+    accepted = in_order([chosen] + [block[tail] for block in arrived], behind)
+    accepted = accepted.reshape(head_count, 2, accept_count, HEAD_SIZE).transpose(1, 2, 0, 3)
     summed = add_up([lax.dynamic_index_in_dim(packed, seq_at, 0, False)] + arrived)
     denominator = (summed[rows, :rows] + summed[rows, rows : 2 * rows])[:, None] + tree_sums
     attended = ((summed[:rows] + tree_numerator) / denominator).astype(bf16)
@@ -478,9 +610,8 @@
         output_projection.reshape(head_count, 2, HEAD_SIZE, width),
         preferred_element_type=f32,
     )
-    attention_out = attention_out[:tok_block] + swap(
-        attention_out[tok_block:].astype(bf16), "kv", 1
-    ).astype(f32)
+    theirs = (attention_out[tok_block:] + still(kv_1, row_1)).astype(bf16)
+    attention_out = attention_out[:tok_block] + swap(theirs, "kv", 1).astype(f32)
 
     def token_totals(*values):
         lanes = 128 // len(values)
@@ -497,6 +628,7 @@
     ).astype(bf16)
 
     all_state = lax.all_gather(first_sum, plane, axis=0, tiled=True)
+    kv_2, row_2 = exchange(2 * quarter, 2 * quarter, all_state)
     all_float = all_state.astype(f32)
     scaled_ffn = (all_float * norm_pre_feedforward).astype(bf16)
     square_lanes = split_lanes(jnp.sum(all_float * all_float, axis=-1, keepdims=True))
@@ -506,47 +638,33 @@
         "td,dcf->ctf", scaled_ffn, gate_up_weight, preferred_element_type=f32
     ).astype(bf16)
 
-    node_at = jnp.arange(tree_size, dtype=jnp.int32)
-    node_at = jnp.where(kv_at == 0, node_at, (node_at + tok_block) % tree_size)
-    accept_pick = (accepted_path[0][:, None] == node_at[None, :]).astype(bf16)
-    chosen = jnp.dot(
-        accept_pick,
-        jnp.concatenate([new_keys, new_values], axis=1),
-        preferred_element_type=f32,
+    keys_updated, values_updated, flag = update_caches(
+        cache_keys[0],
+        cache_values[0],
+        accepted,
+        (length - block_start + zero_at(partial)).reshape(1),
+    )
+
+    def rows_of(place):
+        def window(values):
+            return lax.dynamic_slice_in_dim(values, place * share, share, 0)
+
+        return jnp.concatenate(
+            [window(partial[0]), window(square_lanes), window(partial[1])], axis=-1
+        )
+
+    summed = add_up([rows_of(seq_at)] + send_ahead(lambda j: rows_of(ahead[j])))
+    summed = summed + (flag[0, 0] + still(kv_2, row_2))
+    far_0 = swap(rows_after(kv_0, 0, quarter, summed), "vocab", 2)
+    far_2 = swap(rows_after(row_2, 0, quarter, summed), "kv", 1)
+    inverse = inverse_of(summed[:, units : units + 1] + summed[:, units + 64 : units + 65])
+    activated = (
+        jax.nn.gelu(summed[:, :units] * inverse, approximate=True)
+        * (summed[:, units + 128 :] * inverse)
     ).astype(bf16)
-    chosen = in_order(collect(chosen), ahead)
-    accept_count = chosen.shape[1]
-    chosen = chosen.reshape(head_count, accept_count, 2, HEAD_SIZE).transpose(2, 1, 0, 3)
-    chosen, partial = lax.optimization_barrier((chosen, partial))
-    keys_updated, values_updated, flag = update_caches(
-        cache_keys[0], cache_values[0], chosen, (length - block_start).reshape(1)
-    )
-
-    pieces = 2
-    piece = units // pieces
-    ffn_out = 0.0
-    for p in range(pieces):
-        window = slice(p * piece, (p + 1) * piece)
-        gate = partial[0, :, window]
-        up = partial[1, :, window]
-        if p == 0:
-            gate = jnp.concatenate([gate, square_lanes], axis=-1)
-        lanes = gate.shape[1]
-        both = jnp.concatenate([gate, up], axis=-1).reshape(seq_count, share, lanes + piece)
-        summed = add_up(
-            [lax.dynamic_index_in_dim(both, seq_at, 0, False)]
-            + send_ahead(lambda j: lax.dynamic_index_in_dim(both, ahead[j], 0, False))
-        )
-        if p == 0:
-            inverse = inverse_of(summed[:, piece : piece + 1] + summed[:, piece + 64 : piece + 65])
-            flag, summed = lax.optimization_barrier((flag, summed))
-        activated = (
-            jax.nn.gelu(summed[:, :piece] * inverse, approximate=True)
-            * (summed[:, lanes:] * inverse)
-        ).astype(bf16)
-        activated = in_order(collect(activated), ahead).reshape(row_count, piece)
-        ffn_out = ffn_out + jnp.dot(activated, down_weight[window], preferred_element_type=f32)
-    ffn_out = ffn_out.astype(bf16).reshape(groups, tok_block, width)
+    activated = in_order(collect(activated), ahead).reshape(row_count, units)
+    ffn_out = jnp.dot(activated, down_weight, preferred_element_type=f32)
+    ffn_out = (ffn_out + still(far_0, far_2)).astype(bf16).reshape(groups, tok_block, width)
     ffn_out = add_up(list(lax.all_to_all(ffn_out, plane, 0, 0)))
     first_float = first_sum.astype(f32)
     scaled_out = ffn_out * norm_post_feedforward
@@ -570,66 +688,58 @@
     )
     bias = lax.dynamic_index_in_dim(draft_bias, seq_at, 0, True)
     branch = jax.nn.silu(summed + bias).astype(bf16)
-    branch = lax.all_to_all(branch.reshape(groups, tok_block, -1), plane, 0, 0)
-    branch = branch.transpose(1, 0, 2).reshape(tok_block, MODEL_WIDTH)
-    base = in_order(collect(normed), ahead)
-    base = jnp.concatenate([base[s] for s in range(seq_count)], axis=-1)
-    token_rows = jnp.concatenate([base] + collect(branch), axis=0)
-    raw = jnp.concatenate(
-        [
-            lax.dot_general(
-                token_rows, block, (((1,), (1,)), ((), ())), preferred_element_type=f32
-            )
-            for block in vocab_blocks
-        ],
-        axis=1,
-    ).reshape(seq_count + 1, tok_block, -1)
-    raw = jnp.concatenate([raw[:1], raw[:1] + raw[1:]], axis=0)
-    logits = LOGIT_CAP * jnp.tanh(raw / LOGIT_CAP)
-    totals = jnp.sum(jnp.exp(logits), axis=-1)
-
-    vocab_rows = vocab_weight.shape[0]
-
-    def first_entry(kv_bit, vocab_bits):
-        place = ((kv_at ^ kv_bit) * seq_count + seq_at) * tenants + (vocab_at ^ vocab_bits)
-        return place * vocab_rows
-
-    entries = []
-    for core in (0, 1):
-        for kv_bit, vocab_bits in ((0, 0), (1, 0), (0, 2), (1, 2)):
-            entries.append(
-                first_entry(kv_bit, vocab_bits ^ core) + jnp.arange(vocab_rows, dtype=jnp.int32)
-            )
-    entries = jnp.concatenate(entries)
-    candidates = lax.dynamic_slice(
-        candidate_tokens,
-        (0, kv_at * tok_block, vocab_at, 0),
-        (seq_count + 1, tok_block, 1, CAND),
-    )[:, :, 0]
+    branch = lax.all_to_all(branch, plane, 0, 1, tiled=True)
+    far_1 = swap(rows_after(kv_1, 0, quarter, branch), "vocab", 2)
+    far_3 = swap(rows_after(row_2, quarter, quarter, branch), "kv", 1)
+    head_total = seq_count + 1
+    lanes = 128
+    base = collect(jnp.concatenate([normed, swap(normed, "vocab", 1)], axis=0))
+    heads = collect(branch)
+    other_heads = [swap(head, "vocab", 1) for head in heads]
+    vocab_blocks = [
+        [vocab_weight],
+        [kv_0, kv_1, kv_2],
+        [row_0, row_1, row_2],
+        [far_0, far_1, far_2, far_3],
+    ]
+    starts = [
+        (((kv_at ^ kv_bit) * seq_count + seq_at) * tenants + (vocab_at ^ vocab_bit)) * vocab_rows
+        for kv_bit, vocab_bit in ((0, 0), (1, 0), (0, 2), (1, 2))
+    ]
+    spare = lanes - head_total * tok_block
+
+    def candidates_of(tenant):
+        tokens = lax.dynamic_slice(
+            candidate_tokens,
+            (0, kv_at * tok_block, tenant, 0),
+            (head_total, tok_block, 1, CAND),
+        )
+        tokens = tokens.reshape(head_total * tok_block, CAND).T
+        return jnp.pad(tokens, ((0, 0), (0, spare)), constant_values=-1)
+
     candidates = jnp.concatenate(
-        [candidates[:1]]
-        + [lax.dynamic_slice_in_dim(candidates, 1 + ahead[j], 1, 0) for j in range(seq_count)],
-        axis=0,
-    )
-    picked = [
-        jnp.sum(
-            jnp.where(entries == candidates[:, :, column : column + 1], logits, 0.0), axis=-1
-        )
-        for column in range(CAND)
-    ]
-    tally = jnp.stack([totals] + picked)
-    draft_tally = in_order([tally[:, 1 + j] for j in range(seq_count)], ahead)
-    tally = jnp.concatenate([tally[:, 0][None], draft_tally], axis=0)
-    head_total = seq_count + 1
-    tally = add_up(collect(tally.reshape(head_total * (CAND + 1), tok_block)))
+        [candidates_of(vocab_at), candidates_of(vocab_at ^ 1)], axis=1
+    )
+    tally = score_vocabulary(
+        jnp.stack(starts + ahead).astype(jnp.int32),
+        candidates,
+        base,
+        heads,
+        other_heads,
+        vocab_blocks,
+        lanes,
+    )
+    tally = tally[:, :lanes] + swap(tally[:, lanes:], "vocab", 1)
+    tally = add_up(collect(tally))
     tally = lax.all_gather(tally, plane, axis=0)
-    tally = tally.reshape(kv_count, tenants, head_total, CAND + 1, tok_block)
-    log_normalizer = jnp.log(
-        tally[:, :, :, 0].transpose(2, 0, 3, 1).reshape(head_total, tree_size, tenants)
+    tally = tally[:, : CAND + 1, : head_total * tok_block]
+    tally = tally.reshape(kv_count, tenants, CAND + 1, head_total, tok_block)
+    log_normalizer = jnp.log(tally[:, :, 0].transpose(2, 0, 3, 1)).reshape(
+        head_total, tree_size, tenants
     )
     candidate_logits = (
-        tally[:, :, :, 1:]
-        .transpose(2, 0, 4, 1, 3)
+        tally[:, :, 1:]
+        .transpose(3, 0, 4, 1, 2)
         .reshape(head_total, tree_size, tenants, CAND)
     )
     return (keys_updated[None], values_updated[None], log_normalizer, candidate_logits)

time: 645 us -> 336 us (0.52)
  Pallas kernels: 257 us -> 14.6 us
  blocking collectives: 98.1 us -> 37.8 us
  local copies, waits for them, and re-layouts: 22 us -> 63.3 us
  matrix products: 40.7 us -> 22.3 us
  waiting for transfers between devices: 120 us -> 102 us
  starting transfers between devices: 81.8 us -> 71.6 us
  other arithmetic: 20.9 us -> 10.8 us
  between operations: 2.41 us -> 11.7 us
    pallas_call x1, Pallas kernels: 257 us -> 4.14 us  [update_caches(): pl.pallas_call(kernel, out_shape=(like, like, jax.ShapeDtypeStruct((8, 12...]
    all_gather x1, blocking collectives: 75.3 us -> 9.46 us  [local(): all_state = lax.all_gather(first_sum, plane, axis=0, tiled=True)]
    ppermute x18 -> x15, waiting for transfers between devices: 39.6 us -> 20.7 us  [send_ahead(): lax.ppermute(pick(j), 'seq', [(i, (i + j) % count) for i in range(count)])]
    dot_general x13 -> x3, matrix products: 21.2 us -> 3.41 us  [the longest x1 3.03 us: local(): ffn_out = jnp.dot(activated, down_weight, preferred_element_type=f32)]
    dynamic_slice x1 -> x10, local copies, waits for them, and re-layouts: 0.84 us -> 15.2 us  [the longest x5 10.8 us: rows_after(): return lax.dynamic_slice_in_dim(values, first + zero_at(event), count, 0)]
    unnamed x61 -> x80, local copies, waits for them, and re-layouts: 2.67 us -> 15.8 us
    pallas_call x0 -> x1, Pallas kernels: none -> 10.5 us  [score_vocabulary(): pl.pallas_call(kernel, out_shape=jax.ShapeDtypeStruct((16, 2 * lanes), jn...]
    all_to_all x0 -> x1, blocking collectives: none -> 10.2 us  [local(): ffn_out = add_up(list(lax.all_to_all(ffn_out, plane, 0, 0)))]
  transfers between devices with their start and end apart: 61 -> 58, of which waited for: 29 -> 33; matrix products, arithmetic and copies ran while one was open for 10% -> 18% of each run, Pallas kernels for 40% -> 1%
where the time goes in v3:
time: 336 us; the launch traced here: 334 us
  waiting for transfers between devices  102 us (30%)
  starting transfers between devices  71.6 us (21%)
  local copies, waits for them, and re-layouts  63.3 us (19%)
  blocking collectives  37.8 us (11%)
  matrix products  22.3 us (7%)
  Pallas kernels  14.6 us (4%)
  between operations  11.7 us (3%)
  other arithmetic  10.8 us (3%)
    ppermute x24, waiting for transfers between devices, collect(): lax.ppermute(block, 'seq', [(i, (i - j) % count) for i in range(count)])  40.5 us
    ppermute x18, waiting for transfers between devices, swap(): return lax.ppermute(values, axis, [(i, i ^ bit) for i in range(count)])  37.3 us
    ppermute x24, starting transfers between devices, collect(): lax.ppermute(block, 'seq', [(i, (i - j) % count) for i in range(count)])  30.6 us
    ppermute x15, starting transfers between devices, send_ahead(): lax.ppermute(pick(j), 'seq', [(i, (i + j) % count) for i in range(count)])  21.3 us
    ppermute x15, waiting for transfers between devices, send_ahead(): lax.ppermute(pick(j), 'seq', [(i, (i + j) % count) for i in range(count)])  20.7 us
    ppermute x18, starting transfers between devices, swap(): return lax.ppermute(values, axis, [(i, i ^ bit) for i in range(count)])  16.3 us
    unnamed x80, local copies, waits for them, and re-layouts  15.8 us
    dynamic_slice x5, local copies, waits for them, and re-layouts, rows_after(): return lax.dynamic_slice_in_dim(values, first + zero_at(event), count, 0)  10.8 us
  transfers between devices with their start and end apart: 58, of which 33 were waited for; matrix products, arithmetic and copies ran while one was open for 18% of the time, Pallas kernels for 1%

profile of v3, /device:TPU:0, one launch (start us, length us, event | category | flops | bytes accessed | tf_op | source)
XLA Modules:
  0.0 334.4 jit_solution(12907708890359113699)
XLA Ops:
  14.3 7.4 %fusion.23 = bf16[4,48,1024]{2,1,0:T(8,128)(2,1)S(1)} fusion(bf16[896,4,1024]{2,1,0:T(4,128)(2,1)} %param.20, f32[896]{0:T(1024)} %param.22, bf16[24,896]{1,0:T(8,128)(2,1)S(1)} %collective-permute-done, bf16[24,896]{1,0:T(8,128)(2,1)} %bitcast.212), kind=kOutput, calls=%fused_computation.18 | convolution fusion | flops 352776192 | bytes 7822848 | tf_op jit(solution)/shard_map/td,dhc->htc/dot_general | solution.py:510
  50.5 4.0 %fusion.157 = (f32[4,96]{1,0:T(4,128)S(1)}, bf16[4,96,2048]{2,1,0:T(8,128)(2,1)S(1)}) fusion(bf16[4,96,256]{2,1,0:T(8,128)(2,1)S(1)} %bitcast_dynamic-update-slice_fusion.8, bf16[2048,4,256]{2,1,0:T(4,128)(2,1)} %bitcast.198, pred[2048]{0:T(1024)(128)(4,1)} %add_compare_fusion.1), kind=kOutput, calls=%fused_computation.274 | convolution fusion | flops 406584960 | bytes 5967360 | tf_op jit(solution)/shard_map/hrc,shc->hrs/dot_general | solution.py:559
  70.7 4.4 %collective-permute-done.16 = bf16[96,256]{1,0:T(8,128)(2,1)S(1)} collective-permute-done((bf16[96,256]{1,0:T(8,128)(2,1)S(1)}, bf16[96,256]{1,0:T(8,128)(2,1)S(1)}, u32[]{:S(2)}, u32[]{:S(2)}) %collective-permute-start.16) | collective-permute-done | bytes 49184 | tf_op jit(solution)/shard_map/ppermute | solution.py:251
  76.7 7.9 %collective-permute-done.18.rest_14_ = bf16[128,3584]{1,0:T(8,128)(2,1)S(1)} collective-permute-done((bf16[128,3584]{1,0:T(8,128)(2,1)S(1)}, bf16[128,3584]{1,0:T(8,128)(2,1)S(1)}, u32[]{:S(2)}, u32[]{:S(2)}) %collective-permute-start.18) | collective-permute-done | bytes 917536 | tf_op jit(solution)/shard_map/ppermute | solution.py:272
  99.5 9.5 %all_gather.12 = bf16[192,896]{1,0:T(8,128)(2,1)S(1)} all-gather(bf16[24,896]{1,0:T(8,128)(2,1)S(1)} %add_convert_fusion), channel_id=1, replica_groups=mesh['kv'=2,'seq'=4,'vocab'=4] {'kv','vocab'}, dimensions={0}, use_global_device_ids=true | all-gather | bytes 387072 | tf_op jit(solution)/shard_map/all_gather | solution.py:630
  110.9 3.3 constant_dynamic-slice_fusion.3
  116.3 4.4 %fusion.15 = bf16[2,192,1792]{2,1,0:T(8,128)(2,1)S(1)} fusion(bf16[896,2,1792]{2,1,0:T(2,128)(2,1)} %param.32, bf16[192,896]{1,0:T(8,128)(2,1)S(1)} %copy-done.15, f32[896]{0:T(1024)} %param.24), kind=kOutput, calls=%fused_computation.12 | convolution fusion | flops 1234329600 | bytes 8146432 | tf_op jit(solution)/shard_map/td,dcf->ctf/dot_general | solution.py:637
  137.4 4.1 %shard_map.210 = (bf16[2048,4,256]{2,1,0:T(4,128)(2,1)}, bf16[2048,4,256]{2,1,0:T(4,128)(2,1)}, f32[8,128]{1,0:T(8,128)S(1)}) custom-call(s32[1]{0:T(128)} %bitcast.46.offset_ref, bf16[2,5,4,256]{3,2,1,0:T(4,128)(2,1)S(1)} %bitcast.202, bf16[2048,4,256]{2,1,0:T(4,128)(2,1)S(1)} %bitcast.199, bf16[2048,4,256]{2,1,0:T(4,128)(2,1)S(1)} %bitcast.201), custom_call_target="tpu_custom_call" | custom-call | bytes 16777216 | tf_op jit(solution)/shard_map/pallas_call | solution.py:347
  142.1 14.7 %collective-permute-done.27.rest_15_ = bf16[256,3584]{1,0:T(8,128)(2,1)} collective-permute-done((bf16[256,3584]{1,0:T(8,128)(2,1)}, bf16[256,3584]{1,0:T(8,128)(2,1)}, u32[]{:S(2)}, u32[]{:S(2)}) %collective-permute-start.27) | collective-permute-done | bytes 1835040 | tf_op jit(solution)/shard_map/ppermute | solution.py:272
  172.8 8.5 %collective-permute-done.30 = bf16[48,1792]{1,0:T(8,128)(2,1)} collective-permute-done((bf16[48,1792]{1,0:T(8,128)(2,1)S(1)}, bf16[48,1792]{1,0:T(8,128)(2,1)}, u32[]{:S(2)}, u32[]{:S(2)}) %collective-permute-start.30) | collective-permute-done | bytes 172064 | tf_op jit(solution)/shard_map/ppermute | solution.py:251
  184.5 5.8 %collective-permute-done.33.rest_21_ = bf16[128,3584]{1,0:T(8,128)(2,1)S(1)} collective-permute-done((bf16[128,3584]{1,0:T(8,128)(2,1)S(1)}, bf16[128,3584]{1,0:T(8,128)(2,1)S(1)}, u32[]{:S(2)}, u32[]{:S(2)}) %collective-permute-start.33) | collective-permute-done | bytes 917536 | tf_op jit(solution)/shard_map/ppermute | solution.py:272
  196.0 10.2 %all_to_all.24 = bf16[8,24,896]{2,1,0:T(8,128)(2,1)S(1)} all-to-all(bf16[8,24,896]{2,1,0:T(8,128)(2,1)S(1)} %bitcast.205), channel_id=1, replica_groups=mesh['kv'=2,'seq'=4,'vocab'=4] {'kv','vocab'}, dimensions={0} | all-to-all | bytes 688128 | tf_op jit(solution)/shard_map/all_to_all | solution.py:668
  206.7 3.3 collective-permute-start.34
  216.7 8.8 %all_gather.13 = bf16[192,896]{1,0:T(8,128)(2,1)S(1)} all-gather(bf16[24,896]{1,0:T(8,128)(2,1)S(1)} %multiply_convert_fusion.1), channel_id=1, replica_groups=mesh['kv'=2,'seq'=4,'vocab'=4] {'kv','vocab'}, dimensions={0}, use_global_device_ids=true | all-gather | bytes 387072 | tf_op jit(solution)/shard_map/all_gather | solution.py:681
  227.1 3.5 %collective-permute-start.43 = (bf16[192,448]{1,0:T(8,128)(2,1)S(1)}, bf16[192,448]{1,0:T(8,128)(2,1)S(1)}, u32[]{:S(2)}, u32[]{:S(2)}) collective-permute-start(bf16[192,448]{1,0:T(8,128)(2,1)S(1)} %get-tuple-element.28), channel_id=1, source_target_pairs={{0,12},{4,0},{8,4},{12,8},{1,13},{5,1},{9,5},{13,9},{2,14},{6,2},{... | collective-permute-start | bytes 516104 | tf_op jit(solution)/shard_map/ppermute | solution.py:243
  231.3 5.1 %collective-permute-done.41 = bf16[192,448]{1,0:T(8,128)(2,1)S(1)} collective-permute-done((bf16[192,448]{1,0:T(8,128)(2,1)S(1)}, bf16[192,448]{1,0:T(8,128)(2,1)S(1)}, u32[]{:S(2)}, u32[]{:S(2)}) %collective-permute-start.41) | collective-permute-done | bytes 172064 | tf_op jit(solution)/shard_map/ppermute | solution.py:243
  236.4 7.5 %collective-permute-done.42 = bf16[192,448]{1,0:T(8,128)(2,1)S(1)} collective-permute-done((bf16[192,448]{1,0:T(8,128)(2,1)S(1)}, bf16[192,448]{1,0:T(8,128)(2,1)S(1)}, u32[]{:S(2)}, u32[]{:S(2)}) %collective-permute-start.42) | collective-permute-done | bytes 172064 | tf_op jit(solution)/shard_map/ppermute | solution.py:243
  244.8 3.4 %all-to-all-start.1 = ((bf16[8,24,448]{2,1,0:T(8,128)(2,1)}), bf16[8,24,448]{2,1,0:T(8,128)(2,1)S(1)}, u32[]{:S(2)}, u32[]{:S(2)}) async-start(bf16[8,24,448]{2,1,0:T(8,128)(2,1)} %bitcast.91), calls=%async_computation.1 | async-start | bytes 393216 | tf_op jit(solution)/shard_map/all_to_all | solution.py:691
  250.1 3.8 %all-to-all-done.1 = bf16[8,24,448]{2,1,0:T(8,128)(2,1)S(1)} async-done(((bf16[8,24,448]{2,1,0:T(8,128)(2,1)}), bf16[8,24,448]{2,1,0:T(8,128)(2,1)S(1)}, u32[]{:S(2)}, u32[]{:S(2)}) %all-to-all-start.1) | async-done | bytes 172064 | tf_op jit(solution)/shard_map/all_to_all | solution.py:691
  261.9 3.9 %collective-permute-start.38 = (bf16[48,896]{1,0:T(8,128)(2,1)S(1)}, bf16[48,896]{1,0:T(8,128)(2,1)S(1)}, u32[]{:S(2)}, u32[]{:S(2)}) collective-permute-start(bf16[48,896]{1,0:T(8,128)(2,1)S(1)} %pad_maximum_fusion.4.rest_0_), channel_id=1, source_target_pairs={{0,12},{4,0},{8,4},{12,8},{1,13},{5,1},{9,5},{13,9},{2,14},{6,2},{... | collective-permute-start | bytes 258056 | tf_op jit(solution)/shard_map/ppermute | solution.py:251
  268.6 4.6 %collective-permute-done.51.rest_20_ = bf16[128,3584]{1,0:T(8,128)(2,1)} collective-permute-done((bf16[128,3584]{1,0:T(8,128)(2,1)}, bf16[128,3584]{1,0:T(8,128)(2,1)}, u32[]{:S(2)}, u32[]{:S(2)}) %collective-permute-start.51) | collective-permute-done | bytes 917536 | tf_op jit(solution)/shard_map/ppermute | solution.py:272
  278.2 11.2 %collective-permute-done.40.rest_3_ = bf16[48,896]{1,0:T(8,128)(2,1)} collective-permute-done((bf16[48,896]{1,0:T(8,128)(2,1)S(1)}, bf16[48,896]{1,0:T(8,128)(2,1)}, u32[]{:S(2)}, u32[]{:S(2)}) %collective-permute-start.40) | collective-permute-done | bytes 86048 | tf_op jit(solution)/shard_map/ppermute | solution.py:251
  303.8 10.5 %shard_map.211 = f32[16,256]{1,0:T(8,128)S(1)} custom-call(s32[8]{0:T(128)S(1)} %copy-done.12, s32[8,256]{1,0:T(8,128)S(1)} %select_add_fusion.candidates_ref, bf16[48,896]{1,0:T(8,128)(2,1)S(1)} %pad_maximum_fusion.4.rest_0_, bf16[48,896]{1,0:T(8,128)(2,1)S(1)} %collective-permute-done.38.rest_1_, bf16[48,896]{1,0:T(8,128)(2,1)S(1)} %copy-done.11, ...), custom_call_target="tpu_custom_call" | custom-call | flops 3758096384 | bytes 14680064 | tf_op jit(solution)/shard_map/pallas_call | solution.py:441
  323.3 9.3 %all-gather = f32[128,128]{1,0:T(8,128)S(1)} all-gather(f32[16,128]{1,0:T(8,128)S(1)} %add_add_fusion.3), channel_id=2, replica_groups=mesh['kv'=2,'seq'=4,'vocab'=4] {'kv','vocab'}, dimensions={0}, use_global_device_ids=true | all-gather | bytes 73728 | tf_op jit(solution)/shard_map/all_gather | solution.py:734
  (322 shorter events, 163.9 us)
Async XLA Ops:
  0.6 13.7 %collective-permute-start = (bf16[24,896]{1,0:T(8,128)(2,1)}, bf16[24,896]{1,0:T(8,128)(2,1)S(1)}, u32[]{:S(2)}, u32[]{:S(2)}) collective-permute-start(bf16[24,896]{1,0:T(8,128)(2,1)} %bitcast.210), channel_id=1, source_target_pairs={{0,16},{16,0},{1,17},{17,1},{2,18},{18,2},{3,19},{19,3},{4,20},{20... | collective-permute-start | bytes 129032 | tf_op jit(solution)/shard_map/ppermute | solution.py:272
  7.9 28.7 %collective-permute-start.4 = (bf16[128,3584]{1,0:T(8,128)(2,1)}, bf16[128,3584]{1,0:T(8,128)(2,1)}, u32[]{:S(2)}, u32[]{:S(2)}) collective-permute-start(bf16[128,3584]{1,0:T(8,128)(2,1)} %constant_dynamic-slice_fusion.7), channel_id=1, source_target_pairs={{0,16},{16,0},{1,17},{17,1},{2,18},{18,2},{3,19},{19,3},{4,20},{20... | collective-permute-start | bytes 2752520 | tf_op jit(solution)/shard_map/ppermute | solution.py:272
  8.0 29.7 %collective-permute-start.5 = (bf16[128,3584]{1,0:T(8,128)(2,1)}, bf16[128,3584]{1,0:T(8,128)(2,1)}, u32[]{:S(2)}, u32[]{:S(2)}) collective-permute-start(bf16[128,3584]{1,0:T(8,128)(2,1)} %constant_dynamic-slice_fusion.7), channel_id=1, source_target_pairs={{0,2},{1,3},{2,0},{3,1},{4,6},{5,7},{6,4},{7,5},{8,10},{9,11},{10,... | collective-permute-start | bytes 2752520 | tf_op jit(solution)/shard_map/ppermute | solution.py:272
  68.2 16.3 %collective-permute-start.18 = (bf16[128,3584]{1,0:T(8,128)(2,1)S(1)}, bf16[128,3584]{1,0:T(8,128)(2,1)S(1)}, u32[]{:S(2)}, u32[]{:S(2)}) collective-permute-start(bf16[128,3584]{1,0:T(8,128)(2,1)S(1)} %constant_dynamic-slice_fusion.6), channel_id=1, source_target_pairs={{0,16},{16,0},{1,17},{17,1},{2,18},{18,2},{3,19},{19,3},{4,20},{20... | collective-permute-start | bytes 2752520 | tf_op jit(solution)/shard_map/ppermute | solution.py:272
  69.6 16.4 %collective-permute-start.19 = (bf16[128,3584]{1,0:T(8,128)(2,1)S(1)}, bf16[128,3584]{1,0:T(8,128)(2,1)S(1)}, u32[]{:S(2)}, u32[]{:S(2)}) collective-permute-start(bf16[128,3584]{1,0:T(8,128)(2,1)S(1)} %constant_dynamic-slice_fusion.6), channel_id=1, source_target_pairs={{0,2},{1,3},{2,0},{3,1},{4,6},{5,7},{6,4},{7,5},{8,10},{9,11},{10,... | collective-permute-start | bytes 2752520 | tf_op jit(solution)/shard_map/ppermute | solution.py:272
  90.1 36.9 %collective-permute-start.32 = (bf16[128,3584]{1,0:T(8,128)(2,1)}, bf16[128,3584]{1,0:T(8,128)(2,1)}, u32[]{:S(2)}, u32[]{:S(2)}) collective-permute-start(bf16[128,3584]{1,0:T(8,128)(2,1)} %collective-permute-done.4.rest_13_), channel_id=1, source_target_pairs={{0,2},{1,3},{2,0},{3,1},{4,6},{5,7},{6,4},{7,5},{8,10},{9,11},{10,... | collective-permute-start | bytes 2752520 | tf_op jit(solution)/shard_map/ppermute | solution.py:272
  114.1 42.6 %collective-permute-start.27 = (bf16[256,3584]{1,0:T(8,128)(2,1)}, bf16[256,3584]{1,0:T(8,128)(2,1)}, u32[]{:S(2)}, u32[]{:S(2)}) collective-permute-start(bf16[256,3584]{1,0:T(8,128)(2,1)} %constant_dynamic-slice_fusion.3), channel_id=1, source_target_pairs={{0,16},{16,0},{1,17},{17,1},{2,18},{18,2},{3,19},{19,3},{4,20},{20... | collective-permute-start | bytes 5505032 | tf_op jit(solution)/shard_map/ppermute | solution.py:272
  115.3 42.6 %collective-permute-start.28 = (bf16[256,3584]{1,0:T(8,128)(2,1)}, bf16[256,3584]{1,0:T(8,128)(2,1)}, u32[]{:S(2)}, u32[]{:S(2)}) collective-permute-start(bf16[256,3584]{1,0:T(8,128)(2,1)} %constant_dynamic-slice_fusion.3), channel_id=1, source_target_pairs={{0,2},{1,3},{2,0},{3,1},{4,6},{5,7},{6,4},{7,5},{8,10},{9,11},{10,... | collective-permute-start | bytes 5505032 | tf_op jit(solution)/shard_map/ppermute | solution.py:272
  123.0 38.2 %collective-permute-start.24 = (bf16[48,3712]{1,0:T(8,128)(2,1)}, bf16[48,3712]{1,0:T(8,128)(2,1)}, u32[]{:S(2)}, u32[]{:S(2)}) collective-permute-start(bf16[48,3712]{1,0:T(8,128)(2,1)} %pad_maximum_fusion), channel_id=1, source_target_pairs={{0,4},{4,8},{8,12},{12,0},{1,5},{5,9},{9,13},{13,1},{2,6},{6,10},{... | collective-permute-start | bytes 1069064 | tf_op jit(solution)/shard_map/ppermute | solution.py:243
  124.1 37.1 %collective-permute-start.25 = (bf16[48,3712]{1,0:T(8,128)(2,1)}, bf16[48,3712]{1,0:T(8,128)(2,1)}, u32[]{:S(2)}, u32[]{:S(2)}) collective-permute-start(bf16[48,3712]{1,0:T(8,128)(2,1)} %pad_maximum_fusion.1), channel_id=1, source_target_pairs={{0,8},{4,12},{8,0},{12,4},{1,9},{5,13},{9,1},{13,5},{2,10},{6,14},... | collective-permute-start | bytes 1069064 | tf_op jit(solution)/shard_map/ppermute | solution.py:243
  126.9 34.3 %collective-permute-start.26 = (bf16[48,3712]{1,0:T(8,128)(2,1)}, bf16[48,3712]{1,0:T(8,128)(2,1)}, u32[]{:S(2)}, u32[]{:S(2)}) collective-permute-start(bf16[48,3712]{1,0:T(8,128)(2,1)} %pad_maximum_fusion.2), channel_id=1, source_target_pairs={{0,12},{4,0},{8,4},{12,8},{1,13},{5,1},{9,5},{13,9},{2,14},{6,2},{... | collective-permute-start | bytes 1069064 | tf_op jit(solution)/shard_map/ppermute | solution.py:243
  166.3 15.0 %collective-permute-start.30 = (bf16[48,1792]{1,0:T(8,128)(2,1)S(1)}, bf16[48,1792]{1,0:T(8,128)(2,1)}, u32[]{:S(2)}, u32[]{:S(2)}) collective-permute-start(bf16[48,1792]{1,0:T(8,128)(2,1)S(1)} %get-tuple-element.18), channel_id=1, source_target_pairs={{0,8},{4,12},{8,0},{12,4},{1,9},{5,13},{9,1},{13,5},{2,10},{6,14},... | collective-permute-start | bytes 516104 | tf_op jit(solution)/shard_map/ppermute | solution.py:251
  166.3 16.6 %collective-permute-start.31 = (bf16[48,1792]{1,0:T(8,128)(2,1)S(1)}, bf16[48,1792]{1,0:T(8,128)(2,1)}, u32[]{:S(2)}, u32[]{:S(2)}) collective-permute-start(bf16[48,1792]{1,0:T(8,128)(2,1)S(1)} %get-tuple-element.18), channel_id=1, source_target_pairs={{0,4},{4,8},{8,12},{12,0},{1,5},{5,9},{9,13},{13,1},{2,6},{6,10},{... | collective-permute-start | bytes 516104 | tf_op jit(solution)/shard_map/ppermute | solution.py:251
  169.1 21.2 %collective-permute-start.33 = (bf16[128,3584]{1,0:T(8,128)(2,1)S(1)}, bf16[128,3584]{1,0:T(8,128)(2,1)S(1)}, u32[]{:S(2)}, u32[]{:S(2)}) collective-permute-start(bf16[128,3584]{1,0:T(8,128)(2,1)S(1)} %constant_dynamic-slice_fusion.2), channel_id=1, source_target_pairs={{0,16},{16,0},{1,17},{17,1},{2,18},{18,2},{3,19},{19,3},{4,20},{20... | collective-permute-start | bytes 2752520 | tf_op jit(solution)/shard_map/ppermute | solution.py:272
  226.8 17.2 %collective-permute-start.42 = (bf16[192,448]{1,0:T(8,128)(2,1)S(1)}, bf16[192,448]{1,0:T(8,128)(2,1)S(1)}, u32[]{:S(2)}, u32[]{:S(2)}) collective-permute-start(bf16[192,448]{1,0:T(8,128)(2,1)S(1)} %get-tuple-element.29), channel_id=1, source_target_pairs={{0,8},{4,12},{8,0},{12,4},{1,9},{5,13},{9,1},{13,5},{2,10},{6,14},... | collective-permute-start | bytes 516104 | tf_op jit(solution)/shard_map/ppermute | solution.py:243
  227.1 16.8 %collective-permute-start.43 = (bf16[192,448]{1,0:T(8,128)(2,1)S(1)}, bf16[192,448]{1,0:T(8,128)(2,1)S(1)}, u32[]{:S(2)}, u32[]{:S(2)}) collective-permute-start(bf16[192,448]{1,0:T(8,128)(2,1)S(1)} %get-tuple-element.28), channel_id=1, source_target_pairs={{0,12},{4,0},{8,4},{12,8},{1,13},{5,1},{9,5},{13,9},{2,14},{6,2},{... | collective-permute-start | bytes 516104 | tf_op jit(solution)/shard_map/ppermute | solution.py:243
  248.2 25.0 %collective-permute-start.51 = (bf16[128,3584]{1,0:T(8,128)(2,1)}, bf16[128,3584]{1,0:T(8,128)(2,1)}, u32[]{:S(2)}, u32[]{:S(2)}) collective-permute-start(bf16[128,3584]{1,0:T(8,128)(2,1)} %copy-done.4), channel_id=1, source_target_pairs={{0,2},{1,3},{2,0},{3,1},{4,6},{5,7},{6,4},{7,5},{8,10},{9,11},{10,... | collective-permute-start | bytes 2752520 | tf_op jit(solution)/shard_map/ppermute | solution.py:272
  259.3 39.3 %collective-permute-start.52 = (bf16[128,3584]{1,0:T(8,128)(2,1)}, bf16[128,3584]{1,0:T(8,128)(2,1)}, u32[]{:S(2)}, u32[]{:S(2)}) collective-permute-start(bf16[128,3584]{1,0:T(8,128)(2,1)} %constant_dynamic-slice_fusion), channel_id=1, source_target_pairs={{0,16},{16,0},{1,17},{17,1},{2,18},{18,2},{3,19},{19,3},{4,20},{20... | collective-permute-start | bytes 2752520 | tf_op jit(solution)/shard_map/ppermute | solution.py:272
  261.9 14.5 %collective-permute-start.38 = (bf16[48,896]{1,0:T(8,128)(2,1)S(1)}, bf16[48,896]{1,0:T(8,128)(2,1)S(1)}, u32[]{:S(2)}, u32[]{:S(2)}) collective-permute-start(bf16[48,896]{1,0:T(8,128)(2,1)S(1)} %pad_maximum_fusion.4.rest_0_), channel_id=1, source_target_pairs={{0,12},{4,0},{8,4},{12,8},{1,13},{5,1},{9,5},{13,9},{2,14},{6,2},{... | collective-permute-start | bytes 258056 | tf_op jit(solution)/shard_map/ppermute | solution.py:251
  265.8 11.8 %collective-permute-start.39 = (bf16[48,896]{1,0:T(8,128)(2,1)S(1)}, bf16[48,896]{1,0:T(8,128)(2,1)S(1)}, u32[]{:S(2)}, u32[]{:S(2)}) collective-permute-start(bf16[48,896]{1,0:T(8,128)(2,1)S(1)} %pad_maximum_fusion.4.rest_0_), channel_id=1, source_target_pairs={{0,8},{4,12},{8,0},{12,4},{1,9},{5,13},{9,1},{13,5},{2,10},{6,14},... | collective-permute-start | bytes 258056 | tf_op jit(solution)/shard_map/ppermute | solution.py:251
  267.6 21.8 %collective-permute-start.44 = (bf16[24,3584]{1,0:T(8,128)(2,1)S(1)}, bf16[24,3584]{1,0:T(8,128)(2,1)}, u32[]{:S(2)}, u32[]{:S(2)}) collective-permute-start(bf16[24,3584]{1,0:T(8,128)(2,1)S(1)} %all_to_all.21.rest_4_), channel_id=1, source_target_pairs={{0,12},{4,0},{8,4},{12,8},{1,13},{5,1},{9,5},{13,9},{2,14},{6,2},{... | collective-permute-start | bytes 516104 | tf_op jit(solution)/shard_map/ppermute | solution.py:251
  273.2 17.4 %collective-permute-start.45 = (bf16[24,3584]{1,0:T(8,128)(2,1)S(1)}, bf16[24,3584]{1,0:T(8,128)(2,1)}, u32[]{:S(2)}, u32[]{:S(2)}) collective-permute-start(bf16[24,3584]{1,0:T(8,128)(2,1)S(1)} %all_to_all.21.rest_4_), channel_id=1, source_target_pairs={{0,8},{4,12},{8,0},{12,4},{1,9},{5,13},{9,1},{13,5},{2,10},{6,14},... | collective-permute-start | bytes 516104 | tf_op jit(solution)/shard_map/ppermute | solution.py:251
  276.4 14.2 %collective-permute-start.46 = (bf16[24,3584]{1,0:T(8,128)(2,1)S(1)}, bf16[24,3584]{1,0:T(8,128)(2,1)}, u32[]{:S(2)}, u32[]{:S(2)}) collective-permute-start(bf16[24,3584]{1,0:T(8,128)(2,1)S(1)} %all_to_all.21.rest_4_), channel_id=1, source_target_pairs={{0,4},{4,8},{8,12},{12,0},{1,5},{5,9},{9,13},{13,1},{2,6},{6,10},{... | collective-permute-start | bytes 516104 | tf_op jit(solution)/shard_map/ppermute | solution.py:251
  278.2 11.2 %collective-permute-start.40 = (bf16[48,896]{1,0:T(8,128)(2,1)S(1)}, bf16[48,896]{1,0:T(8,128)(2,1)}, u32[]{:S(2)}, u32[]{:S(2)}) collective-permute-start(bf16[48,896]{1,0:T(8,128)(2,1)S(1)} %pad_maximum_fusion.4.rest_0_), channel_id=1, source_target_pairs={{0,4},{4,8},{8,12},{12,0},{1,5},{5,9},{9,13},{13,1},{2,6},{6,10},{... | collective-permute-start | bytes 258056 | tf_op jit(solution)/shard_map/ppermute | solution.py:251
  (73 other events, 732.7 us)

commit v4 on v3

--- a/solution.py
+++ b/solution.py
@@ -279,17 +279,16 @@
     return jnp.concatenate([jnp.broadcast_to(high, shape), jnp.broadcast_to(low, shape)], axis=-1)
 
 
-def zero_at(event):
-    corner = event.reshape(-1)[0] if event.ndim < 2 else event[(0,) * event.ndim]
-    return (jnp.abs(corner.astype(jnp.float32)) > 3e38).astype(jnp.int32)
-
-
-def still(*values):
-    return sum(value[(0,) * value.ndim].astype(jnp.float32) * 0.0 for value in values)
-
-
-def rows_after(values, first, count, event):
-    return lax.dynamic_slice_in_dim(values, first + zero_at(event), count, 0)
+def hold(values, *events):
+    count = len(values)
+    anywhere = pl.BlockSpec(memory_space=pl.ANY)
+    return pl.pallas_call(
+        lambda *refs: None,
+        out_shape=[jax.ShapeDtypeStruct(value.shape, value.dtype) for value in values],
+        in_specs=[anywhere] * (count + len(events)),
+        out_specs=[anywhere] * count,
+        input_output_aliases={k: k for k in range(count)},
+    )(*values, *events)
 
 
 def inverse_of(totals):
@@ -304,160 +303,298 @@
     )
 
 
-def update_caches(cache_keys, cache_values, rows, offset):
-    slots, heads, size = cache_keys.shape
-    accept = rows.shape[1]
+def copy_rows(sources, targets, *events):
+    unit = 64
+    number = len(sources)
+    shapes = [
+        (sum(rows for _, _, rows in parts),) + sources[0].shape[1:] for parts in targets
+    ]
+    moves = []
+    for t, parts in enumerate(targets):
+        filled = 0
+        for source, first, rows in parts:
+            for p in range(0, rows, unit):
+                size = min(unit, rows - p)
+                moves.append((source, first + p, t, filled + p, size))
+            filled += rows
+
+    def kernel(*refs):
+        inputs, rest = refs[:number], refs[number + len(events) :]
+        outputs, (held, get, put) = rest[: len(shapes)], rest[len(shapes) :]
+        pairs = []
+        for k, (source, first, target, place, size) in enumerate(moves):
+            slot = held.at[k, pl.ds(0, size)]
+            pairs.append(
+                (
+                    pltpu.make_async_copy(
+                        inputs[source].at[pl.ds(first, size)], slot, get.at[k]
+                    ),
+                    pltpu.make_async_copy(
+                        slot, outputs[target].at[pl.ds(place, size)], put.at[k]
+                    ),
+                )
+            )
+        for k, (inward, _) in enumerate(pairs):
+            inward.start(priority=k % 2)
+        for k, (inward, outward) in enumerate(pairs):
+            inward.wait()
+            outward.start(priority=k % 2)
+        for _, outward in pairs:
+            outward.wait()
+
+    row = sources[0].shape[1:]
+    dtype = sources[0].dtype
+    return pl.pallas_call(
+        kernel,
+        out_shape=[jax.ShapeDtypeStruct(shape, dtype) for shape in shapes],
+        in_specs=[pl.BlockSpec(memory_space=pl.ANY)] * (number + len(events)),
+        out_specs=[pl.BlockSpec(memory_space=pltpu.HBM)] * len(shapes),
+        scratch_shapes=[
+            pltpu.VMEM((len(moves), unit) + row, dtype),
+            pltpu.SemaphoreType.DMA((len(moves),)),
+            pltpu.SemaphoreType.DMA((len(moves),)),
+        ],
+        compiler_params=pltpu.CompilerParams(vmem_limit_bytes=58 * 2**20),
+        cost_estimate=pl.CostEstimate(
+            flops=0,
+            bytes_accessed=sum(4 * shape[0] * shape[1] for shape in shapes),
+            transcendentals=0,
+        ),
+    )(*sources, *events)
+
+
+def update_cache(cache, numbers, packed, arrived, first_row, accept, event):
+    slots, heads, size = cache.shape
+    count = 1 + len(arrived)
+    tail = pl.ds(packed.shape[1] - 16, 16)
+    first_row = first_row - (packed.shape[1] - 16)
     piece = 256
     parts = slots // piece
 
-    def kernel(
-        offset_ref, rows_ref, keys_in, values_in, keys_out, values_out, flag, held, get, put, sem
-    ):
+    def kernel(numbers_ref, source, _, packed_ref, *rest):
+        arrived_refs, rest = rest[: count - 1], rest[count - 1 :]
+        target, flag, held, tails, stage, ready, get, put, sem = rest
         flag[...] = jnp.zeros_like(flag)
 
-        def copies(number):
-            source, target = ((keys_in, keys_out), (values_in, values_out))[number // parts]
-            window = pl.ds(number % parts * piece, piece)
-            return (
-                pltpu.make_async_copy(source.at[window], held.at[number], get.at[number]),
-                pltpu.make_async_copy(held.at[number], target.at[window], put.at[number]),
+        tail_copies = []
+        for j in range(count):
+            head = lax.rem(numbers_ref[1] + (count - j), count)
+            block = packed_ref.at[0, tail] if j == 0 else arrived_refs[j - 1].at[tail]
+            tail_copies.append(pltpu.make_async_copy(block, tails.at[head], sem.at[j]))
+            tail_copies[j].start()
+        pairs = []
+        for k in range(parts):
+            window = pl.ds(k * piece, piece)
+            pairs.append(
+                (
+                    pltpu.make_async_copy(source.at[window], held.at[k], get.at[k]),
+                    pltpu.make_async_copy(held.at[k], target.at[window], put.at[k]),
+                )
             )
-
-        pairs = [copies(number) for number in range(2 * parts)]
-        for inward, _ in pairs:
-            inward.start()
-        for inward, outward in pairs:
+        for k, (inward, _) in enumerate(pairs):
+            inward.start(priority=k % 2)
+        for k, (inward, outward) in enumerate(pairs):
             inward.wait()
-            outward.start()
+            outward.start(priority=k % 2)
+        for copy in tail_copies:
+            copy.wait()
+        for head in range(count):
+            rows = tails[head].astype(jnp.float32)
+            for r in range(accept):
+                stage[r, head : head + 1, :] = rows[first_row + r : first_row + r + 1]
+        ready[...] = stage[...].astype(ready.dtype)
         for _, outward in pairs:
             outward.wait()
-        for which, target in enumerate((keys_out, values_out)):
-            for a in range(accept):
-                slot = offset_ref[0] + a
-
-                @pl.when((slot >= 0) & (slot < slots))
-                def _():
-                    copy = pltpu.make_async_copy(
-                        rows_ref.at[which, pl.ds(a, 1)], target.at[pl.ds(slot, 1)], sem.at[0]
-                    )
-                    copy.start()
-                    copy.wait()
-
-    like = jax.ShapeDtypeStruct(cache_keys.shape, cache_keys.dtype)
+        for a in range(accept):
+            slot = numbers_ref[0] + a
+
+            @pl.when((slot >= 0) & (slot < slots))
+            def _():
+                copy = pltpu.make_async_copy(
+                    ready.at[pl.ds(a, 1)], target.at[pl.ds(slot, 1)], sem.at[0]
+                )
+                copy.start()
+                copy.wait()
+
     return pl.pallas_call(
         kernel,
-        out_shape=(like, like, jax.ShapeDtypeStruct((8, 128), jnp.float32)),
+        out_shape=(
+            jax.ShapeDtypeStruct(cache.shape, cache.dtype),
+            jax.ShapeDtypeStruct((8, 128), jnp.float32),
+        ),
         in_specs=[
             pl.BlockSpec(memory_space=pltpu.SMEM),
-            pl.BlockSpec(memory_space=pltpu.VMEM),
             pl.BlockSpec(memory_space=pltpu.HBM),
-            pl.BlockSpec(memory_space=pltpu.HBM),
-        ],
+        ]
+        + [pl.BlockSpec(memory_space=pl.ANY)] * (1 + count),
         out_specs=(
-            pl.BlockSpec(memory_space=pltpu.HBM),
             pl.BlockSpec(memory_space=pltpu.HBM),
             pl.BlockSpec(memory_space=pltpu.VMEM),
         ),
         scratch_shapes=[
-            pltpu.VMEM((2 * parts, piece, heads, size), cache_keys.dtype),
-            pltpu.SemaphoreType.DMA((2 * parts,)),
-            pltpu.SemaphoreType.DMA((2 * parts,)),
-            pltpu.SemaphoreType.DMA((1,)),
-        ],
-        compiler_params=pltpu.CompilerParams(vmem_limit_bytes=24 * 2**20),
+            pltpu.VMEM((parts, piece, heads, size), cache.dtype),
+            pltpu.VMEM((count, 16, size), cache.dtype),
+            pltpu.VMEM((accept, heads, size), jnp.float32),
+            pltpu.VMEM((accept, heads, size), cache.dtype),
+            pltpu.SemaphoreType.DMA((parts,)),
+            pltpu.SemaphoreType.DMA((parts,)),
+            pltpu.SemaphoreType.DMA((count,)),
+        ],
+        compiler_params=pltpu.CompilerParams(vmem_limit_bytes=56 * 2**20),
         cost_estimate=pl.CostEstimate(
-            flops=0, bytes_accessed=4 * cache_keys.size * 2, transcendentals=0
+            flops=0, bytes_accessed=0, transcendentals=0
         ),
-    )(offset, rows, cache_keys, cache_values)
-
-
-def score_vocabulary(numbers, candidates, base, own, other, blocks, lanes):
-    tokens, width = own[0].shape
-    share = base[0].shape[1]
-    count = len(own)
-    extent = sum(part.shape[0] for part in blocks[0])
-    parts = [part for block in blocks for part in block]
-    inputs = base + own + other
-
-    def kernel(numbers_ref, candidates_ref, *rest):
+    )(numbers, cache, event, packed, *arrived)
+
+
+def score_vocabulary(numbers, candidates, heads, vocab_blocks, half, lanes):
+    tokens = heads[0][0].shape[0]
+    count = len(heads[0])
+    groups = len(heads)
+    parts = [part for block in vocab_blocks for part in block]
+    arrays = []
+    for array, _ in parts:
+        if not any(array is known for known in arrays):
+            arrays.append(array)
+    blocks, extent, width = len(vocab_blocks), 2 * half, arrays[0].shape[1]
+    share = width // count
+    unit = 64
+    inputs = [head for group in heads for head in group]
+
+    def kernel(numbers_ref, *rest):
+        candidate_refs, rest = rest[:groups], rest[groups:]
         vectors, rest = rest[: len(inputs)], rest[len(inputs) :]
-        sources, (out_ref, held, wide, narrow, sems) = rest[: len(parts)], rest[len(parts) :]
-        number = 0
-        for b, block in enumerate(blocks):
-            first = 0
-            for part in block:
-                rows = part.shape[0]
+        sources, rest = rest[: len(arrays)], rest[len(arrays) :]
+        *out_refs, held, arrived, wide, narrow, square, row_sems, sems = rest
+        arrivals = []
+        for k, vector in enumerate(vectors):
+            arrivals.append(pltpu.make_async_copy(vector, arrived.at[k], sems.at[k]))
+            arrivals[k].start(priority=k % 2)
+        for k, (array, first) in enumerate(parts):
+            source = sources[[array is known for known in arrays].index(True)]
+            for q, p in enumerate(range(0, half, unit)):
                 pltpu.make_async_copy(
-                    sources[number], held.at[b, pl.ds(first, rows)], sems.at[b]
-                ).start()
-                number += 1
-                first += rows
-        for core in range(2):
-            wide[pl.ds(core * lanes + (count + 1) * tokens, lanes - (count + 1) * tokens), :] = (
-                jnp.zeros((lanes - (count + 1) * tokens, width), jnp.float32)
+                    source.at[pl.ds(first + p, unit)],
+                    held.at[k // 2, pl.ds(k % 2 * half + p, unit)],
+                    row_sems.at[k // 2],
+                ).start(priority=q % 2)
+        spare = lanes - (count + 1) * tokens
+        wanted = []
+        for group, ref in enumerate(candidate_refs):
+            wide[pl.ds((group + 1) * lanes - spare, spare), :] = jnp.zeros(
+                (spare, width), jnp.float32
             )
-        for j in range(count):
-            place = numbers_ref[len(blocks) + j]
+            square[...] = jnp.full((lanes, 128), -1, jnp.int32)
+            for head in range(count + 1):
+                square[head * tokens : (head + 1) * tokens, 0:CAND] = ref[head]
+            wanted.append(square[...].T[0:CAND])
+        for k, arrival in enumerate(arrivals):
+            arrival.wait()
+            group, j = k // count, k % count
+            place = numbers_ref[2 * blocks + j]
             columns = pl.ds(pl.multiple_of(place * share, 128), share)
-            block = vectors[j][...].astype(jnp.float32)
-            for core in range(2):
-                wide[pl.ds(core * lanes, tokens), columns] = block[
-                    core * tokens : (core + 1) * tokens
-                ]
-                first = pl.multiple_of(core * lanes + (place + 1) * tokens, 8)
-                wide[pl.ds(first, tokens), :] = vectors[count * (core + 1) + j][...].astype(
-                    jnp.float32
-                )
+            wide[pl.ds(group * lanes, tokens), columns] = arrived[k, :, width:].astype(
+                jnp.float32
+            )
+            first = pl.multiple_of(group * lanes + (place + 1) * tokens, 8)
+            wide[pl.ds(first, tokens), :] = arrived[k, :, :width].astype(jnp.float32)
         narrow[...] = wide[...].astype(narrow.dtype)
-        lane = lax.broadcasted_iota(jnp.int32, (extent, lanes), 1)
-        row = lax.broadcasted_iota(jnp.int32, (extent, lanes), 0)
-        out_ref[...] = jnp.zeros_like(out_ref)
-
-        def step(b, carry):
-            pltpu.make_async_copy(held.at[b], held.at[b], sems.at[b]).wait()
-            entry = row + numbers_ref[b]
+        lane = lax.broadcasted_iota(jnp.int32, (half, lanes), 1)
+        row = lax.broadcasted_iota(jnp.int32, (half, lanes), 0)
+        for out_ref in out_refs:
+            out_ref[...] = jnp.zeros_like(out_ref)
+
+        def step(b, low):
+            pltpu.make_async_copy(held.at[b], held.at[b], row_sems.at[b]).wait()
             both = lax.dot_general(
                 held[b],
-                narrow[...],
+                narrow[low * lanes : (low + 2) * lanes, :],
                 (((1,), (1,)), ((), ())),
                 preferred_element_type=jnp.float32,
             )
-            for core in range(2):
-                group = slice(core * lanes, (core + 1) * lanes)
-                raw = both[:, group]
-                first = jnp.where(lane < tokens, raw, 0.0)
-                for head in range(1, count + 1):
-                    raw = raw + pltpu.roll(first, head * tokens, 1)
-                logits = LOGIT_CAP * jnp.tanh(raw / LOGIT_CAP)
-                tally = [jnp.sum(jnp.exp(logits), axis=0, keepdims=True)]
-                for c in range(CAND):
-                    match = entry == candidates_ref[c : c + 1, group]
-                    tally.append(jnp.sum(jnp.where(match, logits, 0.0), axis=0, keepdims=True))
-                out_ref[0 : CAND + 1, group] += jnp.concatenate(tally, axis=0)
-            return carry
-
-        lax.fori_loop(0, len(blocks), step, 0)
+            for group in (low, low + 1):
+                place = slice((group - low) * lanes, (group - low + 1) * lanes)
+                for part in range(2):
+                    raw = both[part * half : (part + 1) * half, place]
+                    entry = row + numbers_ref[2 * b + part]
+                    first = jnp.where(lane < tokens, raw, 0.0)
+                    for head in range(1, count + 1):
+                        raw = raw + pltpu.roll(first, head * tokens, 1)
+                    logits = LOGIT_CAP * jnp.tanh(raw / LOGIT_CAP)
+                    tally = [jnp.sum(jnp.exp(logits), axis=0, keepdims=True)]
+                    for c in range(CAND):
+                        match = entry == wanted[group][c : c + 1]
+                        tally.append(
+                            jnp.sum(jnp.where(match, logits, 0.0), axis=0, keepdims=True)
+                        )
+                    out_refs[group][0 : CAND + 1, :] += jnp.concatenate(tally, axis=0)
+
+        for low in range(2):
+
+            def run(b, carry, low=low):
+                step(b, low)
+                return carry
+
+            middle = blocks // 2
+            lax.fori_loop(low * middle, (low + 1) * middle, run, 0)
 
     return pl.pallas_call(
         kernel,
-        out_shape=jax.ShapeDtypeStruct((16, 2 * lanes), jnp.float32),
+        out_shape=[jax.ShapeDtypeStruct((16, lanes), jnp.float32)] * groups,
         in_specs=[pl.BlockSpec(memory_space=pltpu.SMEM)]
-        + [pl.BlockSpec(memory_space=pltpu.VMEM)] * (1 + len(inputs))
-        + [pl.BlockSpec(memory_space=pltpu.HBM)] * len(parts),
-        out_specs=pl.BlockSpec(memory_space=pltpu.VMEM),
+        + [pl.BlockSpec(memory_space=pltpu.VMEM)] * groups
+        + [pl.BlockSpec(memory_space=pl.ANY)] * (len(inputs) + len(arrays)),
+        out_specs=[pl.BlockSpec(memory_space=pltpu.VMEM)] * groups,
         scratch_shapes=[
-            pltpu.VMEM((len(blocks), extent, width), own[0].dtype),
-            pltpu.VMEM((2 * lanes, width), jnp.float32),
-            pltpu.VMEM((2 * lanes, width), own[0].dtype),
-            pltpu.SemaphoreType.DMA((len(blocks),)),
-        ],
-        compiler_params=pltpu.CompilerParams(vmem_limit_bytes=40 * 2**20),
+            pltpu.VMEM((blocks, extent, width), inputs[0].dtype),
+            pltpu.VMEM((len(inputs),) + inputs[0].shape, inputs[0].dtype),
+            pltpu.VMEM((groups * lanes, width), jnp.float32),
+            pltpu.VMEM((groups * lanes, width), inputs[0].dtype),
+            pltpu.VMEM((lanes, 128), jnp.int32),
+            pltpu.SemaphoreType.DMA((blocks,)),
+            pltpu.SemaphoreType.DMA((len(inputs),)),
+        ],
+        compiler_params=pltpu.CompilerParams(vmem_limit_bytes=58 * 2**20),
         cost_estimate=pl.CostEstimate(
-            flops=4 * len(blocks) * extent * width * lanes,
-            bytes_accessed=2 * len(blocks) * extent * width,
-            transcendentals=4 * len(blocks) * extent * lanes,
+            flops=4 * blocks * extent * width * lanes,
+            bytes_accessed=2 * blocks * extent * width,
+            transcendentals=4 * blocks * extent * lanes,
         ),
-    )(numbers, candidates, *inputs, *parts)
+    )(numbers, *candidates, *inputs, *arrays)
+
+
+def project_out(places, attended, weight, own_rows):
+    rows = attended[0].shape[0] // 2
+    size = attended[0].shape[1]
+    count, _, width = weight.shape
+
+    def kernel(places_ref, *refs):
+        blocks, (weight_ref, theirs_ref, own_ref) = refs[:count], refs[count:]
+        total = jnp.zeros((rows, width), jnp.float32)
+        for j, block in enumerate(blocks):
+            for g in range(2):
+                total = total + jnp.dot(
+                    block[g * rows : (g + 1) * rows, :],
+                    weight_ref[places_ref[j], g * size : (g + 1) * size, :],
+                    preferred_element_type=jnp.float32,
+                )
+        own_ref[...] = total[:own_rows]
+        theirs_ref[...] = total[own_rows:].astype(theirs_ref.dtype)
+
+    vmem = pl.BlockSpec(memory_space=pltpu.VMEM)
+    return pl.pallas_call(
+        kernel,
+        out_shape=[
+            jax.ShapeDtypeStruct((rows - own_rows, width), attended[0].dtype),
+            jax.ShapeDtypeStruct((own_rows, width), jnp.float32),
+        ],
+        in_specs=[pl.BlockSpec(memory_space=pltpu.SMEM)] + [vmem] * (count + 1),
+        out_specs=[vmem] * 2,
+        compiler_params=pltpu.CompilerParams(vmem_limit_bytes=16 * 2**20),
+        cost_estimate=pl.CostEstimate(
+            flops=2 * rows * weight.size, bytes_accessed=2 * weight.size, transcendentals=0
+        ),
+    )(places, *attended, weight)
 
 
 def local(
@@ -498,13 +635,8 @@
 
     tenant_state = jnp.concatenate([own_state, swap(own_state, "kv", 1)], axis=0)
     vocab_rows = vocab_weight.shape[0]
-    quarter = vocab_rows // 4
-
-    def exchange(first, count, event):
-        rows = rows_after(vocab_weight, first, count, event)
-        return swap(rows, "kv", 1), swap(rows, "vocab", 2)
-
-    kv_0, row_0 = exchange(0, quarter, tenant_state)
+    half = vocab_rows // 2
+
     tenant_float = tenant_state.astype(f32)
     scaled_input = (tenant_float * norm_pre_attention).astype(bf16)
     projected = jnp.einsum(
@@ -515,16 +647,15 @@
     pair = 2 * HEAD_SIZE
     packed = jnp.concatenate(
         [
-            projected[:, :, :pair],
+            projected,
             jnp.broadcast_to(square_lanes, (head_count,) + square_lanes.shape),
         ],
         axis=-1,
     )
-    summed = add_up(
-        [lax.dynamic_index_in_dim(packed, seq_at, 0, False)]
-        + send_ahead(lambda j: lax.dynamic_index_in_dim(packed, ahead[j], 0, False))
-    )
-    inverse = inverse_of(summed[:, pair : pair + 1] + summed[:, pair + 64 : pair + 65] + still(kv_0, row_0))
+    arrived = send_ahead(lambda j: lax.dynamic_index_in_dim(packed, ahead[j], 0, False))
+    summed = add_up([lax.dynamic_index_in_dim(packed, seq_at, 0, False)] + arrived)
+    whole = 2 * pair
+    inverse = inverse_of(summed[:, whole : whole + 1] + summed[:, whole + 64 : whole + 65])
     tree_mask = ancestors[0]
     tree_mask = jnp.where(
         kv_at == 0, tree_mask, jnp.roll(tree_mask, (tok_block, tok_block), (0, 1))
@@ -543,15 +674,9 @@
         ],
         axis=0,
     ).astype(bf16)
-    kv_1, row_1 = exchange(quarter, quarter, query_rows)
     all_queries = in_order(collect(query_rows), ahead)
-    fresh = projected[:, :, pair:]
-    fresh = add_up(
-        [lax.dynamic_index_in_dim(fresh, seq_at, 0, False)]
-        + send_ahead(lambda j: lax.dynamic_index_in_dim(fresh, ahead[j], 0, False))
-    )
-    new_keys = rotate(fresh[:, :HEAD_SIZE] * inverse, cosine, sine).astype(bf16)
-    new_values = (fresh[:, HEAD_SIZE:] * inverse).astype(bf16)
+    new_keys = rotate(summed[:, pair : pair + HEAD_SIZE] * inverse, cosine, sine).astype(bf16)
+    new_values = (summed[:, pair + HEAD_SIZE : whole] * inverse).astype(bf16)
 
     block_size = cache_keys.shape[1]
     block_start = seq_at * block_size
@@ -596,22 +721,24 @@
     tree_weights = jnp.where(seen, capped_weight(tree_scores), 0.0)
     tree_numerator = jnp.dot(tree_weights.astype(bf16), new_values, preferred_element_type=f32)
     tree_sums = jnp.sum(tree_weights, axis=-1, keepdims=True)
-    behind = [(seq_at - j) % seq_count for j in range(seq_count)]
-    tail = slice(rows + 1, rows + 1 + 2 * accept_count)
-    accepted = in_order([chosen] + [block[tail] for block in arrived], behind)
-    accepted = accepted.reshape(head_count, 2, accept_count, HEAD_SIZE).transpose(1, 2, 0, 3)
+    head_blocks = (packed, arrived)
     summed = add_up([lax.dynamic_index_in_dim(packed, seq_at, 0, False)] + arrived)
     denominator = (summed[rows, :rows] + summed[rows, rows : 2 * rows])[:, None] + tree_sums
     attended = ((summed[:rows] + tree_numerator) / denominator).astype(bf16)
-    attended = in_order(collect(attended), ahead).reshape(head_count, 2, tree_size, HEAD_SIZE)
-    attention_out = jnp.einsum(
-        "hgtc,hgcd->td",
-        attended,
-        output_projection.reshape(head_count, 2, HEAD_SIZE, width),
-        preferred_element_type=f32,
-    )
-    theirs = (attention_out[tok_block:] + still(kv_1, row_1)).astype(bf16)
-    attention_out = attention_out[:tok_block] + swap(theirs, "kv", 1).astype(f32)
+    core_rows = swap(vocab_weight, "vocab", 1)
+    theirs, attention_out = project_out(
+        jnp.stack(ahead).astype(jnp.int32),
+        list(hold([attended], core_rows)) + collect(attended)[1:],
+        output_projection,
+        tok_block,
+    )
+    first_part, second_part = copy_rows(
+        [vocab_weight],
+        [[(0, 0, half)], [(0, half, vocab_rows - half)]],
+        theirs,
+    )
+    (theirs,) = hold([swap(theirs, "kv", 1)], first_part, second_part)
+    attention_out = attention_out + theirs.astype(f32)
 
     def token_totals(*values):
         lanes = 128 // len(values)
@@ -622,114 +749,124 @@
         columns = add_up(collect(columns))
         return [columns[:, k * lanes : k * lanes + 1] for k in range(len(values))]
 
-    (totals,) = token_totals(attention_out * attention_out)
-    first_sum = (
-        own_state.astype(f32) + attention_out * inverse_of(totals) * norm_post_attention
-    ).astype(bf16)
-
-    all_state = lax.all_gather(first_sum, plane, axis=0, tiled=True)
-    kv_2, row_2 = exchange(2 * quarter, 2 * quarter, all_state)
-    all_float = all_state.astype(f32)
-    scaled_ffn = (all_float * norm_pre_feedforward).astype(bf16)
-    square_lanes = split_lanes(jnp.sum(all_float * all_float, axis=-1, keepdims=True))
+    own_float = own_state.astype(f32)
+
+    def add_normed(state, update, gain):
+        scaled = update * gain
+        update_total, state_total, cross_total, scaled_total = token_totals(
+            update * update, state * state, state * scaled, scaled * scaled
+        )
+        inverse = inverse_of(update_total)
+        total = state_total + inverse * (2.0 * cross_total + inverse * scaled_total)
+        return state + scaled * inverse, inverse_of(jnp.maximum(total, 0.0))
+
+    first_sum, inverse = add_normed(own_float, attention_out, norm_post_attention)
+    scaled_ffn = (first_sum * inverse * norm_pre_feedforward).astype(bf16)
+
+    scaled_ffn = lax.all_gather(scaled_ffn, plane, axis=0, tiled=True)
     share = row_count // seq_count
     units = down_weight.shape[0]
     partial = jnp.einsum(
         "td,dcf->ctf", scaled_ffn, gate_up_weight, preferred_element_type=f32
     ).astype(bf16)
 
-    keys_updated, values_updated, flag = update_caches(
-        cache_keys[0],
+    first_part, second_part = hold([first_part, second_part], partial)
+    first_part, second_part = swap(first_part, "kv", 1), swap(second_part, "vocab", 2)
+    slot_numbers = jnp.stack([length - block_start, seq_at])
+    keys_updated, flag = update_cache(
+        cache_keys[0], slot_numbers, *head_blocks, rows + 1, accept_count, partial
+    )
+
+    head_total = seq_count + 1
+    lanes = 128
+    starts = [
+        (((kv_at ^ kv_bit) * seq_count + seq_at) * tenants + (vocab_at ^ vocab_bit)) * vocab_rows
+        + first
+        for kv_bit, vocab_bit, first in (
+            (0, 0, 0),
+            (0, 1, 0),
+            (1, 0, 0),
+            (1, 1, 0),
+            (0, 0, half),
+            (0, 1, half),
+            (0, 2, half),
+            (0, 3, half),
+        )
+    ]
+    later = (flag[0, 0] != 0.0).astype(jnp.int32)
+    candidates = [
+        lax.dynamic_slice(
+            candidate_tokens,
+            (0, block * tok_block + later, tenant, 0),
+            (head_total, tok_block, 1, CAND),
+        )[:, :, 0]
+        for block, tenant in (
+            (kv_at, vocab_at ^ 2),
+            (kv_at, vocab_at),
+            (kv_at ^ 1, vocab_at),
+        )
+    ]
+    numbers = jnp.stack(starts + ahead).astype(jnp.int32) + later
+
+    def rows_of(place):
+        return lax.dynamic_slice_in_dim(partial, place * share, share, 1)
+
+    summed = add_up([rows_of(seq_at)] + send_ahead(lambda j: rows_of(ahead[j])))
+    activated = (jax.nn.gelu(summed[0], approximate=True) * summed[1]).astype(bf16)
+    (activated,) = hold([activated], flag)
+    values_updated, value_flag = update_cache(
         cache_values[0],
-        accepted,
-        (length - block_start + zero_at(partial)).reshape(1),
-    )
-
-    def rows_of(place):
-        def window(values):
-            return lax.dynamic_slice_in_dim(values, place * share, share, 0)
-
-        return jnp.concatenate(
-            [window(partial[0]), window(square_lanes), window(partial[1])], axis=-1
-        )
-
-    summed = add_up([rows_of(seq_at)] + send_ahead(lambda j: rows_of(ahead[j])))
-    summed = summed + (flag[0, 0] + still(kv_2, row_2))
-    far_0 = swap(rows_after(kv_0, 0, quarter, summed), "vocab", 2)
-    far_2 = swap(rows_after(row_2, 0, quarter, summed), "kv", 1)
-    inverse = inverse_of(summed[:, units : units + 1] + summed[:, units + 64 : units + 65])
-    activated = (
-        jax.nn.gelu(summed[:, :units] * inverse, approximate=True)
-        * (summed[:, units + 128 :] * inverse)
-    ).astype(bf16)
-    activated = in_order(collect(activated), ahead).reshape(row_count, units)
-    ffn_out = jnp.dot(activated, down_weight, preferred_element_type=f32)
-    ffn_out = (ffn_out + still(far_0, far_2)).astype(bf16).reshape(groups, tok_block, width)
+        slot_numbers,
+        *head_blocks,
+        rows + 1 + accept_count,
+        accept_count,
+        activated,
+    )
+    ffn_out = in_order(
+        [
+            jnp.dot(block, down_weight, preferred_element_type=f32).astype(bf16)
+            for block in collect(activated)
+        ],
+        ahead,
+    ).reshape(groups, tok_block, width)
+    ffn_out, numbers, *candidates = hold(
+        [ffn_out, numbers, *candidates], first_part, second_part, value_flag
+    )
     ffn_out = add_up(list(lax.all_to_all(ffn_out, plane, 0, 0)))
-    first_float = first_sum.astype(f32)
-    scaled_out = ffn_out * norm_post_feedforward
-    out_total, first_total, cross_total, scaled_total = token_totals(
-        ffn_out * ffn_out, first_float * first_float, first_float * scaled_out, scaled_out * scaled_out
-    )
-    inverse = inverse_of(out_total)
-    second_sum = (first_float + scaled_out * inverse).astype(bf16)
-    second_total = first_total + inverse * (2.0 * cross_total + inverse * scaled_total)
-    normed = (
-        second_sum.astype(f32) * inverse_of(jnp.maximum(second_total, 0.0)) * norm_final
-    ).astype(bf16)
+    second_sum, inverse = add_normed(first_sum, ffn_out, norm_post_feedforward)
+    normed = (second_sum * inverse * norm_final).astype(bf16)
 
     gathered = lax.all_gather(normed, plane, axis=0, tiled=True)
     lifted = jnp.einsum(
         "td,ndc->ntc", gathered, draft_weight, preferred_element_type=f32
     ).astype(bf16)
+    places = [("vocab", 2), (None, 0), ("kv", 1)]
+
+    def around(values):
+        return [values if axis is None else swap(values, axis, bit) for axis, bit in places]
+
+    first_part, second_part = hold([first_part, second_part], lifted)
+    core_first, core_second = swap(first_part, "vocab", 1), swap(second_part, "vocab", 1)
     summed = add_up(
         [lax.dynamic_index_in_dim(lifted, seq_at, 0, False)]
         + send_ahead(lambda j: lax.dynamic_index_in_dim(lifted, ahead[j], 0, False))
     )
     bias = lax.dynamic_index_in_dim(draft_bias, seq_at, 0, True)
     branch = jax.nn.silu(summed + bias).astype(bf16)
+    vocab_blocks = [
+        [(vocab_weight, 0), (core_rows, 0)],
+        [(first_part, 0), (core_first, 0)],
+        [(vocab_weight, half), (core_rows, half)],
+        [(second_part, 0), (core_second, 0)],
+    ]
+    (branch,) = hold([branch], core_first, core_second)
     branch = lax.all_to_all(branch, plane, 0, 1, tiled=True)
-    far_1 = swap(rows_after(kv_1, 0, quarter, branch), "vocab", 2)
-    far_3 = swap(rows_after(row_2, quarter, quarter, branch), "kv", 1)
-    head_total = seq_count + 1
-    lanes = 128
-    base = collect(jnp.concatenate([normed, swap(normed, "vocab", 1)], axis=0))
-    heads = collect(branch)
-    other_heads = [swap(head, "vocab", 1) for head in heads]
-    vocab_blocks = [
-        [vocab_weight],
-        [kv_0, kv_1, kv_2],
-        [row_0, row_1, row_2],
-        [far_0, far_1, far_2, far_3],
-    ]
-    starts = [
-        (((kv_at ^ kv_bit) * seq_count + seq_at) * tenants + (vocab_at ^ vocab_bit)) * vocab_rows
-        for kv_bit, vocab_bit in ((0, 0), (1, 0), (0, 2), (1, 2))
-    ]
-    spare = lanes - head_total * tok_block
-
-    def candidates_of(tenant):
-        tokens = lax.dynamic_slice(
-            candidate_tokens,
-            (0, kv_at * tok_block, tenant, 0),
-            (head_total, tok_block, 1, CAND),
-        )
-        tokens = tokens.reshape(head_total * tok_block, CAND).T
-        return jnp.pad(tokens, ((0, 0), (0, spare)), constant_values=-1)
-
-    candidates = jnp.concatenate(
-        [candidates_of(vocab_at), candidates_of(vocab_at ^ 1)], axis=1
-    )
+    heads = collect(jnp.concatenate([branch, normed], axis=1))
+    heads = [list(group) for group in zip(*[around(head) for head in heads])]
     tally = score_vocabulary(
-        jnp.stack(starts + ahead).astype(jnp.int32),
-        candidates,
-        base,
-        heads,
-        other_heads,
-        vocab_blocks,
-        lanes,
-    )
-    tally = tally[:, :lanes] + swap(tally[:, lanes:], "vocab", 1)
+        numbers, candidates, heads, vocab_blocks, half, lanes
+    )
+    tally = tally[1] + (swap(tally[0], "vocab", 2) + swap(tally[2], "kv", 1))
     tally = add_up(collect(tally))
     tally = lax.all_gather(tally, plane, axis=0)
     tally = tally[:, : CAND + 1, : head_total * tok_block]

time: 336 us -> 290 us (0.86)
  local copies, waits for them, and re-layouts: 63.3 us -> 20.8 us
  waiting for transfers between devices: 102 us -> 76.9 us
  Pallas kernels: 14.6 us -> 35.4 us
  blocking collectives: 37.8 us -> 47.6 us
  between operations: 11.7 us -> 2.69 us
  other arithmetic: 10.8 us -> 15.1 us
  starting transfers between devices: 71.6 us -> 67.9 us
    ppermute x18 -> x17, waiting for transfers between devices: 37.3 us -> 13.3 us  [swap(): return lax.ppermute(values, axis, [(i, i ^ bit) for i in range(count)])]
    pallas_call x2 -> x12, Pallas kernels: 14.6 us -> 35.4 us  [the longest x2 15.7 us: update_cache(): pl.pallas_call(kernel, out_shape=(jax.ShapeDtypeStruct(cache.shape, cache...]
    ppermute x15 -> x12, waiting for transfers between devices: 20.7 us -> 38.4 us  [send_ahead(): lax.ppermute(pick(j), 'seq', [(i, (i + j) % count) for i in range(count)])]
    ppermute x24 -> x21, waiting for transfers between devices: 40.5 us -> 25.3 us  [collect(): lax.ppermute(block, 'seq', [(i, (i - j) % count) for i in range(count)])]
    slice x18 -> x1, local copies, waits for them, and re-layouts: 12.6 us -> 1.2 us  [local(): later = (flag[0, 0] != 0.0).astype(jnp.int32)]
    unnamed x80 -> x64, local copies, waits for them, and re-layouts: 15.8 us -> 6.59 us
    all_to_all x0 -> x1, blocking collectives: none -> 8.96 us  [local(): branch = lax.all_to_all(branch, plane, 0, 1, tiled=True)]
    dynamic_slice x10 -> x5, local copies, waits for them, and re-layouts: 15.2 us -> 6.73 us  [the longest x4 5.79 us: local(): lax.dynamic_slice(candidate_tokens, (0, block * tok_block + later, tenant...]
  transfers between devices with their start and end apart: 58 -> 50, of which waited for: 33 -> 29; matrix products, arithmetic and copies ran while one was open for 18% -> 11% of each run, Pallas kernels for 1% -> 7%
where the time goes in v4:
time: 290 us; the launch traced here: 288 us
  waiting for transfers between devices  76.9 us (27%)
  starting transfers between devices  67.9 us (23%)
  blocking collectives  47.6 us (16%)
  Pallas kernels  35.4 us (12%)
  matrix products  21.8 us (8%)
  local copies, waits for them, and re-layouts  20.8 us (7%)
  other arithmetic  15.1 us (5%)
    ppermute x12, waiting for transfers between devices, send_ahead(): lax.ppermute(pick(j), 'seq', [(i, (i + j) % count) for i in range(count)])  38.4 us
    ppermute x21, starting transfers between devices, collect(): lax.ppermute(block, 'seq', [(i, (i - j) % count) for i in range(count)])  34.5 us
    ppermute x21, waiting for transfers between devices, collect(): lax.ppermute(block, 'seq', [(i, (i - j) % count) for i in range(count)])  25.3 us
    ppermute x12, starting transfers between devices, send_ahead(): lax.ppermute(pick(j), 'seq', [(i, (i + j) % count) for i in range(count)])  18.2 us
    pallas_call x2, Pallas kernels, update_cache(): pl.pallas_call(kernel, out_shape=(jax.ShapeDtypeStruct(cache.shape, cache...  15.7 us
    ppermute x17, starting transfers between devices, swap(): return lax.ppermute(values, axis, [(i, i ^ bit) for i in range(count)])  15.2 us
    pallas_call x1, Pallas kernels, score_vocabulary(): pl.pallas_call(kernel, out_shape=[jax.ShapeDtypeStruct((16, lanes), jnp.f...  15.1 us
    ppermute x17, waiting for transfers between devices, swap(): return lax.ppermute(values, axis, [(i, i ^ bit) for i in range(count)])  13.3 us
  transfers between devices with their start and end apart: 50, of which 29 were waited for; matrix products, arithmetic and copies ran while one was open for 11% of the time, Pallas kernels for 7%

profile of v4, /device:TPU:0, one launch (start us, length us, event | category | flops | bytes accessed | tf_op | source)
XLA Modules:
  0.0 288.1 jit_solution(12946004118191654757)
XLA Ops:
  7.0 7.5 %fusion.17 = bf16[4,48,1024]{2,1,0:T(8,128)(2,1)S(1)} fusion(bf16[896,4,1024]{2,1,0:T(4,128)(2,1)} %param.20, f32[896]{0:T(1024)} %param.22, bf16[24,896]{1,0:T(8,128)(2,1)S(1)} %collective-permute-done, bf16[24,896]{1,0:T(8,128)(2,1)} %bitcast.187), kind=kOutput, calls=%fused_computation.13 | convolution fusion | flops 352776192 | bytes 7822848 | tf_op jit(solution)/shard_map/td,dhc->htc/dot_general | solution.py:642
  22.8 3.8 %collective-permute-done.2 = bf16[48,1152]{1,0:T(8,128)(2,1)S(1)} collective-permute-done((bf16[48,1152]{1,0:T(8,128)(2,1)S(1)}, bf16[48,1152]{1,0:T(8,128)(2,1)S(1)}, u32[]{:S(2)}, u32[]{:S(2)}) %collective-permute-start.2) | collective-permute-done | bytes 110624 | tf_op jit(solution)/shard_map/ppermute | solution.py:243
  59.9 3.4 %shard_map.212 = (bf16[256,3584]{1,0:T(8,128)(2,1)}, bf16[256,3584]{1,0:T(8,128)(2,1)}) custom-call(bf16[512,3584]{1,0:T(8,128)(2,1)} %rest_15_.1, bf16[24,896]{1,0:T(8,128)(2,1)} %copy-done.4), custom_call_target="tpu_custom_call" | custom-call | bytes 7340032 | tf_op jit(solution)/shard_map/pallas_call | solution.py:347
  74.5 9.7 %all_gather.12 = bf16[192,896]{1,0:T(8,128)(2,1)S(1)} all-gather(bf16[24,896]{1,0:T(8,128)(2,1)S(1)} %get-tuple-element.57), channel_id=1, replica_groups=mesh['kv'=2,'seq'=4,'vocab'=4] {'kv','vocab'}, dimensions={0}, use_global_device_ids=true | all-gather | bytes 387072 | tf_op jit(solution)/shard_map/all_gather | solution.py:766
  84.2 4.4 %fusion.10 = bf16[192,2,1792]{2,0,1:T(8,128)(2,1)S(1)} fusion(bf16[896,2,1792]{2,1,0:T(2,128)(2,1)} %param.32, bf16[192,896]{1,0:T(8,128)(2,1)S(1)} %all_gather.12), kind=kOutput, calls=%fused_computation.9 | convolution fusion | flops 1233813504 | bytes 8142848 | tf_op jit(solution)/shard_map/td,dcf->ctf/dot_general | solution.py:769
  90.7 3.8 %collective-permute-start.20 = (bf16[2,48,1792]{2,1,0:T(8,128)(2,1)}, bf16[2,48,1792]{2,1,0:T(8,128)(2,1)}, u32[]{:S(2)}, u32[]{:S(2)}) collective-permute-start(bf16[2,48,1792]{2,1,0:T(8,128)(2,1)} %get-tuple-element.64), channel_id=1, source_target_pairs={{0,12},{4,0},{8,4},{12,8},{1,13},{5,1},{9,5},{13,9},{2,14},{6,2},{... | collective-permute-start | bytes 1032200 | tf_op jit(solution)/shard_map/ppermute | solution.py:243
  95.8 7.8 %shard_map.214 = (bf16[2048,4,256]{2,1,0:T(4,128)(2,1)}, f32[8,128]{1,0:T(8,128)}) custom-call(s32[2]{0:T(128)} %pad_add_fusion.1.numbers_ref, bf16[2048,4,256]{2,1,0:T(4,128)(2,1)} %bitcast.174, bf16[2,192,1792]{2,1,0:T(8,128)(2,1)} %bitcast.173, bf16[4,112,256]{2,1,0:T(8,128)(2,1)} %copy-done.8, bf16[112,256]{1,0:T(8,128)(2,1)} %copy-done.12, ...), custom_call_target="tpu_custom_call" | custom-call | tf_op jit(solution)/shard_map/pallas_call | solution.py:419
  114.1 10.8 %collective-permute-done.19 = bf16[2,48,1792]{2,1,0:T(8,128)(2,1)} collective-permute-done((bf16[2,48,1792]{2,1,0:T(8,128)(2,1)S(1)}, bf16[2,48,1792]{2,1,0:T(8,128)(2,1)}, u32[]{:S(2)}, u32[]{:S(2)}) %collective-permute-start.19) | collective-permute-done | bytes 344096 | tf_op jit(solution)/shard_map/ppermute | solution.py:243
  130.9 7.8 %shard_map.216 = (bf16[2048,4,256]{2,1,0:T(4,128)(2,1)}, f32[8,128]{1,0:T(8,128)}) custom-call(s32[2]{0:T(128)} %pad_add_fusion.1.numbers_ref, bf16[2048,4,256]{2,1,0:T(4,128)(2,1)} %bitcast.176, bf16[48,1792]{1,0:T(8,128)(2,1)} %shard_map.215._, bf16[4,112,256]{2,1,0:T(8,128)(2,1)} %copy-done.8, bf16[112,256]{1,0:T(8,128)(2,1)} %copy-done.12, ...), custom_call_target="tpu_custom_call" | custom-call | tf_op jit(solution)/shard_map/pallas_call | solution.py:419
  145.9 11.0 %all_to_all.24 = bf16[8,24,896]{2,1,0:T(8,128)(2,1)S(1)} all-to-all(bf16[8,24,896]{2,1,0:T(8,128)(2,1)} %get-tuple-element.38), channel_id=1, replica_groups=mesh['kv'=2,'seq'=4,'vocab'=4] {'kv','vocab'}, dimensions={0} | all-to-all | bytes 688128 | tf_op jit(solution)/shard_map/all_to_all | solution.py:835
  161.2 3.6 %collective-permute-start.26 = (f32[24,128]{1,0:T(8,128)S(1)}, f32[24,128]{1,0:T(8,128)S(1)}, u32[]{:S(2)}, u32[]{:S(2)}) collective-permute-start(f32[24,128]{1,0:T(8,128)S(1)} %pad_maximum_fusion.9), channel_id=1, source_target_pairs={{0,12},{4,0},{8,4},{12,8},{1,13},{5,1},{9,5},{13,9},{2,14},{6,2},{... | collective-permute-start | bytes 36872 | tf_op jit(solution)/shard_map/ppermute | solution.py:251
  167.8 8.8 %all_gather.13 = bf16[192,896]{1,0:T(8,128)(2,1)S(1)} all-gather(bf16[24,896]{1,0:T(8,128)(2,1)S(1)} %multiply_convert_fusion.1), channel_id=1, replica_groups=mesh['kv'=2,'seq'=4,'vocab'=4] {'kv','vocab'}, dimensions={0}, use_global_device_ids=true | all-gather | bytes 387072 | tf_op jit(solution)/shard_map/all_gather | solution.py:839
  176.6 3.9 %convolution_convert_fusion = bf16[192,4,448]{2,0,1:T(8,128)(2,1)} fusion(bf16[4,896,448]{1,2,0:T(8,128)(2,1)} %param.34, bf16[192,896]{1,0:T(8,128)(2,1)S(1)} %all_gather.13), kind=kOutput, calls=%fused_computation.11 | convolution fusion | flops 616906752 | bytes 4243456 | tf_op jit(solution)/shard_map/td,ndc->ntc/dot_general | solution.py:840
  182.2 3.9 %collective-permute-start.31 = (bf16[192,448]{1,0:T(8,128)(2,1)S(1)}, bf16[192,448]{1,0:T(8,128)(2,1)S(1)}, u32[]{:S(2)}, u32[]{:S(2)}) collective-permute-start(bf16[192,448]{1,0:T(8,128)(2,1)S(1)} %get-tuple-element.67), channel_id=1, source_target_pairs={{0,12},{4,0},{8,4},{12,8},{1,13},{5,1},{9,5},{13,9},{2,14},{6,2},{... | collective-permute-start | bytes 516104 | tf_op jit(solution)/shard_map/ppermute | solution.py:243
  187.3 4.5 %collective-permute-done.29 = bf16[192,448]{1,0:T(8,128)(2,1)S(1)} collective-permute-done((bf16[192,448]{1,0:T(8,128)(2,1)S(1)}, bf16[192,448]{1,0:T(8,128)(2,1)S(1)}, u32[]{:S(2)}, u32[]{:S(2)}) %collective-permute-start.29) | collective-permute-done | bytes 172064 | tf_op jit(solution)/shard_map/ppermute | solution.py:243
  193.7 10.4 %collective-permute-done.30 = bf16[192,448]{1,0:T(8,128)(2,1)S(1)} collective-permute-done((bf16[192,448]{1,0:T(8,128)(2,1)S(1)}, bf16[192,448]{1,0:T(8,128)(2,1)S(1)}, u32[]{:S(2)}, u32[]{:S(2)}) %collective-permute-start.30) | collective-permute-done | bytes 172064 | tf_op jit(solution)/shard_map/ppermute | solution.py:243
  205.9 9.0 %all_to_all.25 = bf16[8,24,448]{2,1,0:T(8,128)(2,1)S(1)} all-to-all(bf16[8,24,448]{2,1,0:T(8,128)(2,1)} %bitcast.180), channel_id=1, replica_groups=mesh['kv'=2,'seq'=4,'vocab'=4] {'kv','vocab'}, dimensions={0} | all-to-all | bytes 344064 | tf_op jit(solution)/shard_map/all_to_all | solution.py:863
  218.6 3.2 %collective-permute-start.35 = (bf16[24,4480]{1,0:T(8,128)(2,1)S(1)}, bf16[24,4480]{1,0:T(8,128)(2,1)S(1)}, u32[]{:S(2)}, u32[]{:S(2)}) collective-permute-start(bf16[24,4480]{1,0:T(8,128)(2,1)S(1)} %pad_maximum_fusion.rest_7_), channel_id=1, source_target_pairs={{0,12},{4,0},{8,4},{12,8},{1,13},{5,1},{9,5},{13,9},{2,14},{6,2},{... | collective-permute-start | bytes 645128 | tf_op jit(solution)/shard_map/ppermute | solution.py:251
  222.3 4.6 %collective-permute-done.39.rest_10_ = bf16[24,4480]{1,0:T(8,128)(2,1)S(1)} collective-permute-done((bf16[24,4480]{1,0:T(8,128)(2,1)S(1)}, bf16[24,4480]{1,0:T(8,128)(2,1)S(1)}, u32[]{:S(2)}, u32[]{:S(2)}) %collective-permute-start.39) | collective-permute-done | bytes 215072 | tf_op jit(solution)/shard_map/ppermute | solution.py:251
  228.6 6.1 %collective-permute-done.37.rest_9_ = bf16[24,4480]{1,0:T(8,128)(2,1)S(1)} collective-permute-done((bf16[24,4480]{1,0:T(8,128)(2,1)S(1)}, bf16[24,4480]{1,0:T(8,128)(2,1)S(1)}, u32[]{:S(2)}, u32[]{:S(2)}) %collective-permute-start.37) | collective-permute-done | bytes 215072 | tf_op jit(solution)/shard_map/ppermute | solution.py:251
  238.8 4.1 %collective-permute-done.43.rest_13_ = bf16[24,4480]{1,0:T(8,128)(2,1)S(1)} collective-permute-done((bf16[24,4480]{1,0:T(8,128)(2,1)S(1)}, bf16[24,4480]{1,0:T(8,128)(2,1)S(1)}, u32[]{:S(2)}, u32[]{:S(2)}) %collective-permute-start.43) | collective-permute-done | bytes 215072 | tf_op jit(solution)/shard_map/ppermute | solution.py:272
  247.3 15.1 %shard_map.221 = (f32[16,128]{1,0:T(8,128)}, f32[16,128]{1,0:T(8,128)}, f32[16,128]{1,0:T(8,128)}) custom-call(s32[12]{0:T(128)} %get-tuple-element.34.numbers_ref, s32[5,24,8]{2,1,0:T(8,128)} %get-tuple-element.35.rest_0_, s32[5,24,8]{2,1,0:T(8,128)} %get-tuple-element.36.rest_1_, s32[5,24,8]{2,1,0:T(8,128)} %get-tuple-element.37.rest_2_, ...), custom_call_target="tpu_custom_call" | custom-call | flops 3758096384 | bytes 14680064 | tf_op jit(solution)/shard_map/pallas_call | solution.py:541
  268.6 4.0 %collective-permute-start.49 = (f32[16,128]{1,0:T(8,128)S(1)}, f32[16,128]{1,0:T(8,128)S(1)}, u32[]{:S(2)}, u32[]{:S(2)}) collective-permute-start(f32[16,128]{1,0:T(8,128)S(1)} %add_add_fusion.4), channel_id=1, source_target_pairs={{0,4},{4,8},{8,12},{12,0},{1,5},{5,9},{9,13},{13,1},{2,6},{6,10},{... | collective-permute-start | bytes 24584 | tf_op jit(solution)/shard_map/ppermute | solution.py:251
  277.2 9.2 %all-gather = f32[128,128]{1,0:T(8,128)S(1)} all-gather(f32[16,128]{1,0:T(8,128)S(1)} %add_add_fusion.3), channel_id=2, replica_groups=mesh['kv'=2,'seq'=4,'vocab'=4] {'kv','vocab'}, dimensions={0}, use_global_device_ids=true | all-gather | bytes 73728 | tf_op jit(solution)/shard_map/all_gather | solution.py:871
  (255 shorter events, 124.9 us)
Async XLA Ops:
  3.7 51.6 %collective-permute-start.10 = (bf16[512,3584]{1,0:T(8,128)(2,1)}, bf16[512,3584]{1,0:T(8,128)(2,1)}, u32[]{:S(2)}, u32[]{:S(2)}) collective-permute-start(bf16[512,3584]{1,0:T(8,128)(2,1)} %rest_15_.1), channel_id=1, source_target_pairs={{0,1},{1,0},{2,3},{3,2},{4,5},{5,4},{6,7},{7,6},{8,9},{9,8},{10,11... | collective-permute-start | bytes 11010056 | tf_op jit(solution)/shard_map/ppermute | solution.py:272
  16.8 9.8 %collective-permute-start.2 = (bf16[48,1152]{1,0:T(8,128)(2,1)S(1)}, bf16[48,1152]{1,0:T(8,128)(2,1)S(1)}, u32[]{:S(2)}, u32[]{:S(2)}) collective-permute-start(bf16[48,1152]{1,0:T(8,128)(2,1)S(1)} %get-tuple-element.70), channel_id=1, source_target_pairs={{0,8},{4,12},{8,0},{12,4},{1,9},{5,13},{9,1},{13,5},{2,10},{6,14},... | collective-permute-start | bytes 331784 | tf_op jit(solution)/shard_map/ppermute | solution.py:243
  27.2 8.8 %collective-permute-start.6 = (bf16[96,256]{1,0:T(8,128)(2,1)S(1)}, bf16[96,256]{1,0:T(8,128)(2,1)S(1)}, u32[]{:S(2)}, u32[]{:S(2)}) collective-permute-start(bf16[96,256]{1,0:T(8,128)(2,1)S(1)} %pad_maximum_fusion.3), channel_id=1, source_target_pairs={{0,4},{4,8},{8,12},{12,0},{1,5},{5,9},{9,13},{13,1},{2,6},{6,10},{... | collective-permute-start | bytes 147464 | tf_op jit(solution)/shard_map/ppermute | solution.py:251
  90.6 23.4 %collective-permute-start.18 = (bf16[2,48,1792]{2,1,0:T(8,128)(2,1)}, bf16[2,48,1792]{2,1,0:T(8,128)(2,1)}, u32[]{:S(2)}, u32[]{:S(2)}) collective-permute-start(bf16[2,48,1792]{2,1,0:T(8,128)(2,1)} %get-tuple-element.63), channel_id=1, source_target_pairs={{0,4},{4,8},{8,12},{12,0},{1,5},{5,9},{9,13},{13,1},{2,6},{6,10},{... | collective-permute-start | bytes 1032200 | tf_op jit(solution)/shard_map/ppermute | solution.py:243
  90.7 23.4 %collective-permute-start.20 = (bf16[2,48,1792]{2,1,0:T(8,128)(2,1)}, bf16[2,48,1792]{2,1,0:T(8,128)(2,1)}, u32[]{:S(2)}, u32[]{:S(2)}) collective-permute-start(bf16[2,48,1792]{2,1,0:T(8,128)(2,1)} %get-tuple-element.64), channel_id=1, source_target_pairs={{0,12},{4,0},{8,4},{12,8},{1,13},{5,1},{9,5},{13,9},{2,14},{6,2},{... | collective-permute-start | bytes 1032200 | tf_op jit(solution)/shard_map/ppermute | solution.py:243
  94.5 30.4 %collective-permute-start.19 = (bf16[2,48,1792]{2,1,0:T(8,128)(2,1)S(1)}, bf16[2,48,1792]{2,1,0:T(8,128)(2,1)}, u32[]{:S(2)}, u32[]{:S(2)}) collective-permute-start(bf16[2,48,1792]{2,1,0:T(8,128)(2,1)S(1)} %get-tuple-element.65), channel_id=1, source_target_pairs={{0,8},{4,12},{8,0},{12,4},{1,9},{5,13},{9,1},{13,5},{2,10},{6,14},... | collective-permute-start | bytes 1032200 | tf_op jit(solution)/shard_map/ppermute | solution.py:243
  105.5 39.2 %collective-permute-start.24 = (bf16[256,3584]{1,0:T(8,128)(2,1)}, bf16[256,3584]{1,0:T(8,128)(2,1)}, u32[]{:S(2)}, u32[]{:S(2)}) collective-permute-start(bf16[256,3584]{1,0:T(8,128)(2,1)} %get-tuple-element.31), channel_id=1, source_target_pairs={{0,16},{16,0},{1,17},{17,1},{2,18},{18,2},{3,19},{19,3},{4,20},{20... | collective-permute-start | bytes 5505032 | tf_op jit(solution)/shard_map/ppermute | solution.py:272
  107.0 38.9 %collective-permute-start.25 = (bf16[256,3584]{1,0:T(8,128)(2,1)}, bf16[256,3584]{1,0:T(8,128)(2,1)}, u32[]{:S(2)}, u32[]{:S(2)}) collective-permute-start(bf16[256,3584]{1,0:T(8,128)(2,1)} %get-tuple-element.32), channel_id=1, source_target_pairs={{0,2},{1,3},{2,0},{3,1},{4,6},{5,7},{6,4},{7,5},{8,10},{9,11},{10,... | collective-permute-start | bytes 5505032 | tf_op jit(solution)/shard_map/ppermute | solution.py:272
  127.1 16.2 %collective-permute-start.23 = (bf16[48,1792]{1,0:T(8,128)(2,1)}, bf16[48,1792]{1,0:T(8,128)(2,1)S(1)}, u32[]{:S(2)}, u32[]{:S(2)}) collective-permute-start(bf16[48,1792]{1,0:T(8,128)(2,1)} %shard_map.215._), channel_id=1, source_target_pairs={{0,4},{4,8},{8,12},{12,0},{1,5},{5,9},{9,13},{13,1},{2,6},{6,10},{... | collective-permute-start | bytes 516104 | tf_op jit(solution)/shard_map/ppermute | solution.py:251
  127.1 15.6 %collective-permute-start.22 = (bf16[48,1792]{1,0:T(8,128)(2,1)}, bf16[48,1792]{1,0:T(8,128)(2,1)S(1)}, u32[]{:S(2)}, u32[]{:S(2)}) collective-permute-start(bf16[48,1792]{1,0:T(8,128)(2,1)} %shard_map.215._), channel_id=1, source_target_pairs={{0,8},{4,12},{8,0},{12,4},{1,9},{5,13},{9,1},{13,5},{2,10},{6,14},... | collective-permute-start | bytes 516104 | tf_op jit(solution)/shard_map/ppermute | solution.py:251
  128.2 11.8 %collective-permute-start.21 = (bf16[48,1792]{1,0:T(8,128)(2,1)}, bf16[48,1792]{1,0:T(8,128)(2,1)S(1)}, u32[]{:S(2)}, u32[]{:S(2)}) collective-permute-start(bf16[48,1792]{1,0:T(8,128)(2,1)} %shard_map.215._), channel_id=1, source_target_pairs={{0,12},{4,0},{8,4},{12,8},{1,13},{5,1},{9,5},{13,9},{2,14},{6,2},{... | collective-permute-start | bytes 516104 | tf_op jit(solution)/shard_map/ppermute | solution.py:251
  180.5 25.4 %collective-permute-start.32 = (bf16[256,3584]{1,0:T(8,128)(2,1)}, bf16[256,3584]{1,0:T(8,128)(2,1)}, u32[]{:S(2)}, u32[]{:S(2)}) collective-permute-start(bf16[256,3584]{1,0:T(8,128)(2,1)} %get-tuple-element.39.rest_17_), channel_id=1, source_target_pairs={{0,1},{1,0},{2,3},{3,2},{4,5},{5,4},{6,7},{7,6},{8,9},{9,8},{10,11... | collective-permute-start | bytes 5505032 | tf_op jit(solution)/shard_map/ppermute | solution.py:272
  180.9 25.0 %collective-permute-start.33 = (bf16[256,3584]{1,0:T(8,128)(2,1)}, bf16[256,3584]{1,0:T(8,128)(2,1)}, u32[]{:S(2)}, u32[]{:S(2)}) collective-permute-start(bf16[256,3584]{1,0:T(8,128)(2,1)} %get-tuple-element.40.rest_19_), channel_id=1, source_target_pairs={{0,1},{1,0},{2,3},{3,2},{4,5},{5,4},{6,7},{7,6},{8,9},{9,8},{10,11... | collective-permute-start | bytes 5505032 | tf_op jit(solution)/shard_map/ppermute | solution.py:272
  182.2 9.7 %collective-permute-start.29 = (bf16[192,448]{1,0:T(8,128)(2,1)S(1)}, bf16[192,448]{1,0:T(8,128)(2,1)S(1)}, u32[]{:S(2)}, u32[]{:S(2)}) collective-permute-start(bf16[192,448]{1,0:T(8,128)(2,1)S(1)} %get-tuple-element.66), channel_id=1, source_target_pairs={{0,4},{4,8},{8,12},{12,0},{1,5},{5,9},{9,13},{13,1},{2,6},{6,10},{... | collective-permute-start | bytes 516104 | tf_op jit(solution)/shard_map/ppermute | solution.py:243
  182.2 11.4 %collective-permute-start.31 = (bf16[192,448]{1,0:T(8,128)(2,1)S(1)}, bf16[192,448]{1,0:T(8,128)(2,1)S(1)}, u32[]{:S(2)}, u32[]{:S(2)}) collective-permute-start(bf16[192,448]{1,0:T(8,128)(2,1)S(1)} %get-tuple-element.67), channel_id=1, source_target_pairs={{0,12},{4,0},{8,4},{12,8},{1,13},{5,1},{9,5},{13,9},{2,14},{6,2},{... | collective-permute-start | bytes 516104 | tf_op jit(solution)/shard_map/ppermute | solution.py:243
  186.1 18.0 %collective-permute-start.30 = (bf16[192,448]{1,0:T(8,128)(2,1)S(1)}, bf16[192,448]{1,0:T(8,128)(2,1)S(1)}, u32[]{:S(2)}, u32[]{:S(2)}) collective-permute-start(bf16[192,448]{1,0:T(8,128)(2,1)S(1)} %get-tuple-element.68), channel_id=1, source_target_pairs={{0,8},{4,12},{8,0},{12,4},{1,9},{5,13},{9,1},{13,5},{2,10},{6,14},... | collective-permute-start | bytes 516104 | tf_op jit(solution)/shard_map/ppermute | solution.py:243
  216.7 10.2 %collective-permute-start.39 = (bf16[24,4480]{1,0:T(8,128)(2,1)S(1)}, bf16[24,4480]{1,0:T(8,128)(2,1)S(1)}, u32[]{:S(2)}, u32[]{:S(2)}) collective-permute-start(bf16[24,4480]{1,0:T(8,128)(2,1)S(1)} %pad_maximum_fusion.rest_7_), channel_id=1, source_target_pairs={{0,4},{4,8},{8,12},{12,0},{1,5},{5,9},{9,13},{13,1},{2,6},{6,10},{... | collective-permute-start | bytes 645128 | tf_op jit(solution)/shard_map/ppermute | solution.py:251
  216.8 11.2 %collective-permute-start.41 = (bf16[24,4480]{1,0:T(8,128)(2,1)S(1)}, bf16[24,4480]{1,0:T(8,128)(2,1)S(1)}, u32[]{:S(2)}, u32[]{:S(2)}) collective-permute-start(bf16[24,4480]{1,0:T(8,128)(2,1)S(1)} %pad_maximum_fusion.rest_7_), channel_id=1, source_target_pairs={{0,16},{16,0},{1,17},{17,1},{2,18},{18,2},{3,19},{19,3},{4,20},{20... | collective-permute-start | bytes 645128 | tf_op jit(solution)/shard_map/ppermute | solution.py:272
  218.0 16.7 %collective-permute-start.37 = (bf16[24,4480]{1,0:T(8,128)(2,1)S(1)}, bf16[24,4480]{1,0:T(8,128)(2,1)S(1)}, u32[]{:S(2)}, u32[]{:S(2)}) collective-permute-start(bf16[24,4480]{1,0:T(8,128)(2,1)S(1)} %pad_maximum_fusion.rest_7_), channel_id=1, source_target_pairs={{0,8},{4,12},{8,0},{12,4},{1,9},{5,13},{9,1},{13,5},{2,10},{6,14},... | collective-permute-start | bytes 645128 | tf_op jit(solution)/shard_map/ppermute | solution.py:251
  218.6 17.6 %collective-permute-start.35 = (bf16[24,4480]{1,0:T(8,128)(2,1)S(1)}, bf16[24,4480]{1,0:T(8,128)(2,1)S(1)}, u32[]{:S(2)}, u32[]{:S(2)}) collective-permute-start(bf16[24,4480]{1,0:T(8,128)(2,1)S(1)} %pad_maximum_fusion.rest_7_), channel_id=1, source_target_pairs={{0,12},{4,0},{8,4},{12,8},{1,13},{5,1},{9,5},{13,9},{2,14},{6,2},{... | collective-permute-start | bytes 645128 | tf_op jit(solution)/shard_map/ppermute | solution.py:251
  221.8 14.9 %collective-permute-start.34 = (bf16[24,4480]{1,0:T(8,128)(2,1)S(1)}, bf16[24,4480]{1,0:T(8,128)(2,1)S(1)}, u32[]{:S(2)}, u32[]{:S(2)}) collective-permute-start(bf16[24,4480]{1,0:T(8,128)(2,1)S(1)} %pad_maximum_fusion.rest_7_), channel_id=1, source_target_pairs={{0,2},{1,3},{2,0},{3,1},{4,6},{5,7},{6,4},{7,5},{8,10},{9,11},{10,... | collective-permute-start | bytes 645128 | tf_op jit(solution)/shard_map/ppermute | solution.py:272
  227.0 11.0 %collective-permute-start.44 = (bf16[24,4480]{1,0:T(8,128)(2,1)S(1)}, bf16[24,4480]{1,0:T(8,128)(2,1)S(1)}, u32[]{:S(2)}, u32[]{:S(2)}) collective-permute-start(bf16[24,4480]{1,0:T(8,128)(2,1)S(1)} %collective-permute-done.39.rest_10_), channel_id=1, source_target_pairs={{0,16},{16,0},{1,17},{17,1},{2,18},{18,2},{3,19},{19,3},{4,20},{20... | collective-permute-start | bytes 645128 | tf_op jit(solution)/shard_map/ppermute | solution.py:272
  228.0 10.8 %collective-permute-start.40 = (bf16[24,4480]{1,0:T(8,128)(2,1)S(1)}, bf16[24,4480]{1,0:T(8,128)(2,1)S(1)}, u32[]{:S(2)}, u32[]{:S(2)}) collective-permute-start(bf16[24,4480]{1,0:T(8,128)(2,1)S(1)} %collective-permute-done.39.rest_10_), channel_id=1, source_target_pairs={{0,2},{1,3},{2,0},{3,1},{4,6},{5,7},{6,4},{7,5},{8,10},{9,11},{10,... | collective-permute-start | bytes 645128 | tf_op jit(solution)/shard_map/ppermute | solution.py:272
  236.7 9.8 %collective-permute-start.42 = (bf16[24,4480]{1,0:T(8,128)(2,1)S(1)}, bf16[24,4480]{1,0:T(8,128)(2,1)S(1)}, u32[]{:S(2)}, u32[]{:S(2)}) collective-permute-start(bf16[24,4480]{1,0:T(8,128)(2,1)S(1)} %collective-permute-done.35.rest_8_), channel_id=1, source_target_pairs={{0,16},{16,0},{1,17},{17,1},{2,18},{18,2},{3,19},{19,3},{4,20},{20... | collective-permute-start | bytes 645128 | tf_op jit(solution)/shard_map/ppermute | solution.py:272
  (57 other events, 562.7 us)

commit v5 on v4

--- a/solution.py
+++ b/solution.py
@@ -363,7 +363,7 @@
     )(*sources, *events)
 
 
-def update_cache(cache, numbers, packed, arrived, first_row, accept, event):
+def update_cache(cache, numbers, packed, arrived, first_row, accept, *events):
     slots, heads, size = cache.shape
     count = 1 + len(arrived)
     tail = pl.ds(packed.shape[1] - 16, 16)
@@ -371,8 +371,8 @@
     piece = 256
     parts = slots // piece
 
-    def kernel(numbers_ref, source, _, packed_ref, *rest):
-        arrived_refs, rest = rest[: count - 1], rest[count - 1 :]
+    def kernel(numbers_ref, source, packed_ref, *rest):
+        arrived_refs, rest = rest[: count - 1], rest[count - 1 + len(events) :]
         target, flag, held, tails, stage, ready, get, put, sem = rest
         flag[...] = jnp.zeros_like(flag)
 
@@ -426,7 +426,7 @@
             pl.BlockSpec(memory_space=pltpu.SMEM),
             pl.BlockSpec(memory_space=pltpu.HBM),
         ]
-        + [pl.BlockSpec(memory_space=pl.ANY)] * (1 + count),
+        + [pl.BlockSpec(memory_space=pl.ANY)] * (count + len(events)),
         out_specs=(
             pl.BlockSpec(memory_space=pltpu.HBM),
             pl.BlockSpec(memory_space=pltpu.VMEM),
@@ -442,9 +442,9 @@
         ],
         compiler_params=pltpu.CompilerParams(vmem_limit_bytes=56 * 2**20),
         cost_estimate=pl.CostEstimate(
-            flops=0, bytes_accessed=0, transcendentals=0
+            flops=0, bytes_accessed=4 * cache.size, transcendentals=0
         ),
-    )(numbers, cache, event, packed, *arrived)
+    )(numbers, cache, packed, *arrived, *events)
 
 
 def score_vocabulary(numbers, candidates, heads, vocab_blocks, half, lanes):
@@ -465,44 +465,53 @@
         candidate_refs, rest = rest[:groups], rest[groups:]
         vectors, rest = rest[: len(inputs)], rest[len(inputs) :]
         sources, rest = rest[: len(arrays)], rest[len(arrays) :]
-        *out_refs, held, arrived, wide, narrow, square, row_sems, sems = rest
+        out_ref, held, arrived, wide, narrow, square, row_sems, sems = rest
         arrivals = []
         for k, vector in enumerate(vectors):
             arrivals.append(pltpu.make_async_copy(vector, arrived.at[k], sems.at[k]))
-            arrivals[k].start(priority=k % 2)
-        for k, (array, first) in enumerate(parts):
-            source = sources[[array is known for known in arrays].index(True)]
-            for q, p in enumerate(range(0, half, unit)):
-                pltpu.make_async_copy(
-                    source.at[pl.ds(first + p, unit)],
-                    held.at[k // 2, pl.ds(k % 2 * half + p, unit)],
-                    row_sems.at[k // 2],
-                ).start(priority=q % 2)
+            arrivals[k].start(priority=0)
+        def fetch(b):
+            for k in (2 * b, 2 * b + 1):
+                array, first = parts[k]
+                source = sources[[array is known for known in arrays].index(True)]
+                for q, p in enumerate(range(0, half, unit)):
+                    pltpu.make_async_copy(
+                        source.at[pl.ds(first + p, unit)],
+                        held.at[b, pl.ds(k % 2 * half + p, unit)],
+                        row_sems.at[b],
+                    ).start(priority=1)
+
+        fetch(0)
+        fetch(1)
+        fetch(2)
+        fetch(3)
         spare = lanes - (count + 1) * tokens
         wanted = []
         for group, ref in enumerate(candidate_refs):
-            wide[pl.ds((group + 1) * lanes - spare, spare), :] = jnp.zeros(
-                (spare, width), jnp.float32
-            )
             square[...] = jnp.full((lanes, 128), -1, jnp.int32)
-            for head in range(count + 1):
-                square[head * tokens : (head + 1) * tokens, 0:CAND] = ref[head]
+            square[0:tokens, 0:CAND] = ref[0]
+            for j in range(count):
+                row_at = (j + 1) * tokens
+                square[row_at : row_at + tokens, 0:CAND] = ref[numbers_ref[2 * blocks + j] + 1]
             wanted.append(square[...].T[0:CAND])
-        for k, arrival in enumerate(arrivals):
-            arrival.wait()
-            group, j = k // count, k % count
-            place = numbers_ref[2 * blocks + j]
-            columns = pl.ds(pl.multiple_of(place * share, 128), share)
-            wide[pl.ds(group * lanes, tokens), columns] = arrived[k, :, width:].astype(
-                jnp.float32
-            )
-            first = pl.multiple_of(group * lanes + (place + 1) * tokens, 8)
-            wide[pl.ds(first, tokens), :] = arrived[k, :, :width].astype(jnp.float32)
-        narrow[...] = wide[...].astype(narrow.dtype)
+        def assemble(group):
+            for j in range(count):
+                arrivals[group * count + j].wait()
+                columns = pl.ds(pl.multiple_of(numbers_ref[2 * blocks + j] * share, 128), share)
+                wide[group * tokens : (group + 1) * tokens, columns] = arrived[
+                    group * count + j, :, width:
+                ].astype(jnp.float32)
+            pieces = [wide[group * tokens : (group + 1) * tokens, :]]
+            pieces += [arrived[group * count + j, :, :width].astype(jnp.float32) for j in range(count)]
+            pieces += [jnp.zeros((spare, width), jnp.float32)]
+            narrow[group * lanes : (group + 1) * lanes, :] = jnp.concatenate(
+                pieces, axis=0
+            ).astype(narrow.dtype)
+        assemble(0)
+        assemble(1)
         lane = lax.broadcasted_iota(jnp.int32, (half, lanes), 1)
         row = lax.broadcasted_iota(jnp.int32, (half, lanes), 0)
-        for out_ref in out_refs:
-            out_ref[...] = jnp.zeros_like(out_ref)
+        out_ref[...] = jnp.zeros_like(out_ref)
 
         def step(b, low):
             pltpu.make_async_copy(held.at[b], held.at[b], row_sems.at[b]).wait()
@@ -527,9 +536,11 @@
                         tally.append(
                             jnp.sum(jnp.where(match, logits, 0.0), axis=0, keepdims=True)
                         )
-                    out_refs[group][0 : CAND + 1, :] += jnp.concatenate(tally, axis=0)
+                    out_ref[16 * group : 16 * group + CAND + 1, :] += jnp.concatenate(tally, axis=0)
 
         for low in range(2):
+            if low == 1:
+                assemble(2)
 
             def run(b, carry, low=low):
                 step(b, low)
@@ -537,18 +548,25 @@
 
             middle = blocks // 2
             lax.fori_loop(low * middle, (low + 1) * middle, run, 0)
+        turn = numbers_ref[2 * blocks] * tokens
+        across = lax.broadcasted_iota(jnp.int32, out_ref.shape, 1)
+        values = out_ref[...]
+        ahead = pltpu.roll(values, turn, 1)
+        wrapped = pltpu.roll(values, turn + lanes - count * tokens, 1)
+        turned = jnp.where(across - turn >= tokens, ahead, wrapped)
+        out_ref[...] = jnp.where(across < tokens, values, turned)
 
     return pl.pallas_call(
         kernel,
-        out_shape=[jax.ShapeDtypeStruct((16, lanes), jnp.float32)] * groups,
+        out_shape=jax.ShapeDtypeStruct((16 * groups, lanes), jnp.float32),
         in_specs=[pl.BlockSpec(memory_space=pltpu.SMEM)]
         + [pl.BlockSpec(memory_space=pltpu.VMEM)] * groups
         + [pl.BlockSpec(memory_space=pl.ANY)] * (len(inputs) + len(arrays)),
-        out_specs=[pl.BlockSpec(memory_space=pltpu.VMEM)] * groups,
+        out_specs=pl.BlockSpec(memory_space=pltpu.VMEM),
         scratch_shapes=[
             pltpu.VMEM((blocks, extent, width), inputs[0].dtype),
             pltpu.VMEM((len(inputs),) + inputs[0].shape, inputs[0].dtype),
-            pltpu.VMEM((groups * lanes, width), jnp.float32),
+            pltpu.VMEM((groups * tokens, width), jnp.float32),
             pltpu.VMEM((groups * lanes, width), inputs[0].dtype),
             pltpu.VMEM((lanes, 128), jnp.int32),
             pltpu.SemaphoreType.DMA((blocks,)),
@@ -561,6 +579,37 @@
             transcendentals=4 * blocks * extent * lanes,
         ),
     )(numbers, *candidates, *inputs, *arrays)
+
+
+def activate_draft(parts, normed, kv_count, seq_count):
+    number, tokens, columns = parts.shape
+    tenants = number // (kv_count * seq_count)
+    width = kv_count * tenants * columns
+
+    def kernel(parts_ref, normed_ref, out_ref):
+        pair = []
+        for kv in range(kv_count):
+            for tenant in range(tenants):
+                total = 0.0
+                for seq in range(seq_count):
+                    block = parts_ref[(kv * seq_count + seq) * tenants + tenant]
+                    total = total + block.astype(jnp.float32)
+                pair.append(total / (1.0 + jnp.exp(-total)))
+                if len(pair) == 2:
+                    place = (kv * tenants + tenant - 1) * columns
+                    out_ref[:, place : place + 2 * columns] = jnp.concatenate(
+                        pair, axis=1
+                    ).astype(out_ref.dtype)
+                    pair = []
+        out_ref[:, width:] = normed_ref[...]
+
+    vmem = pl.BlockSpec(memory_space=pltpu.VMEM)
+    return pl.pallas_call(
+        kernel,
+        out_shape=jax.ShapeDtypeStruct((tokens, width + normed.shape[1]), normed.dtype),
+        in_specs=[vmem] * 2,
+        out_specs=vmem,
+    )(parts, normed)
 
 
 def project_out(places, attended, weight, own_rows):
@@ -725,10 +774,9 @@
     summed = add_up([lax.dynamic_index_in_dim(packed, seq_at, 0, False)] + arrived)
     denominator = (summed[rows, :rows] + summed[rows, rows : 2 * rows])[:, None] + tree_sums
     attended = ((summed[:rows] + tree_numerator) / denominator).astype(bf16)
-    core_rows = swap(vocab_weight, "vocab", 1)
     theirs, attention_out = project_out(
         jnp.stack(ahead).astype(jnp.int32),
-        list(hold([attended], core_rows)) + collect(attended)[1:],
+        collect(attended),
         output_projection,
         tok_block,
     )
@@ -770,13 +818,9 @@
         "td,dcf->ctf", scaled_ffn, gate_up_weight, preferred_element_type=f32
     ).astype(bf16)
 
-    first_part, second_part = hold([first_part, second_part], partial)
+    first_part, second_part = hold([first_part, second_part], scaled_ffn)
     first_part, second_part = swap(first_part, "kv", 1), swap(second_part, "vocab", 2)
     slot_numbers = jnp.stack([length - block_start, seq_at])
-    keys_updated, flag = update_cache(
-        cache_keys[0], slot_numbers, *head_blocks, rows + 1, accept_count, partial
-    )
-
     head_total = seq_count + 1
     lanes = 128
     starts = [
@@ -793,7 +837,7 @@
             (0, 3, half),
         )
     ]
-    later = (flag[0, 0] != 0.0).astype(jnp.int32)
+    later = (jnp.abs(partial[0, 0, 0].astype(f32)) > 3e38).astype(jnp.int32)
     candidates = [
         lax.dynamic_slice(
             candidate_tokens,
@@ -812,64 +856,67 @@
         return lax.dynamic_slice_in_dim(partial, place * share, share, 1)
 
     summed = add_up([rows_of(seq_at)] + send_ahead(lambda j: rows_of(ahead[j])))
+    keys_updated, key_flag = update_cache(
+        cache_keys[0], slot_numbers, *head_blocks, rows + 1, accept_count, *candidates
+    )
     activated = (jax.nn.gelu(summed[0], approximate=True) * summed[1]).astype(bf16)
-    (activated,) = hold([activated], flag)
+    (activated,) = hold([activated], key_flag, first_part, second_part)
+    ffn_out = in_order(
+        [
+            jnp.dot(block, down_weight, preferred_element_type=f32).astype(bf16)
+            for block in collect(activated)
+        ],
+        ahead,
+    ).reshape(groups, tok_block, width)
+    ffn_out, numbers, *candidates = hold(
+        [ffn_out, numbers, *candidates], first_part, second_part
+    )
+    ffn_out = add_up(list(lax.all_to_all(ffn_out, plane, 0, 0)))
+    second_sum, inverse = add_normed(first_sum, ffn_out, norm_post_feedforward)
+    normed = (second_sum * inverse * norm_final).astype(bf16)
+
+    gathered = lax.all_gather(normed, plane, axis=0, tiled=True)
+    lifted = jnp.einsum(
+        "td,ndc->ntc", gathered, draft_weight, preferred_element_type=f32
+    )
+    lifted = lifted + draft_bias[:, None, :] * (1.0 / seq_count)
+    lifted = lifted.astype(bf16).reshape(seq_count, kv_count, tenants, tok_block, -1)
+    lifted = lifted.transpose(1, 0, 2, 3, 4).reshape(seq_count * groups, tok_block, -1)
+    places = [("vocab", 2), (None, 0), ("kv", 1)]
+
+    def around(values):
+        return [values if axis is None else swap(values, axis, bit) for axis, bit in places]
+
+    first_part, second_part = hold([first_part, second_part], lifted)
+    core_first, core_second = swap(first_part, "vocab", 1), swap(second_part, "vocab", 1)
+    core_rows = swap(vocab_weight, "vocab", 1)
+    vocab_blocks = [
+        [(vocab_weight, 0), (core_rows, 0)],
+        [(first_part, 0), (core_first, 0)],
+        [(vocab_weight, half), (core_rows, half)],
+        [(second_part, 0), (core_second, 0)],
+    ]
     values_updated, value_flag = update_cache(
         cache_values[0],
         slot_numbers,
         *head_blocks,
         rows + 1 + accept_count,
         accept_count,
-        activated,
-    )
-    ffn_out = in_order(
-        [
-            jnp.dot(block, down_weight, preferred_element_type=f32).astype(bf16)
-            for block in collect(activated)
-        ],
-        ahead,
-    ).reshape(groups, tok_block, width)
-    ffn_out, numbers, *candidates = hold(
-        [ffn_out, numbers, *candidates], first_part, second_part, value_flag
-    )
-    ffn_out = add_up(list(lax.all_to_all(ffn_out, plane, 0, 0)))
-    second_sum, inverse = add_normed(first_sum, ffn_out, norm_post_feedforward)
-    normed = (second_sum * inverse * norm_final).astype(bf16)
-
-    gathered = lax.all_gather(normed, plane, axis=0, tiled=True)
-    lifted = jnp.einsum(
-        "td,ndc->ntc", gathered, draft_weight, preferred_element_type=f32
-    ).astype(bf16)
-    places = [("vocab", 2), (None, 0), ("kv", 1)]
-
-    def around(values):
-        return [values if axis is None else swap(values, axis, bit) for axis, bit in places]
-
-    first_part, second_part = hold([first_part, second_part], lifted)
-    core_first, core_second = swap(first_part, "vocab", 1), swap(second_part, "vocab", 1)
-    summed = add_up(
-        [lax.dynamic_index_in_dim(lifted, seq_at, 0, False)]
-        + send_ahead(lambda j: lax.dynamic_index_in_dim(lifted, ahead[j], 0, False))
-    )
-    bias = lax.dynamic_index_in_dim(draft_bias, seq_at, 0, True)
-    branch = jax.nn.silu(summed + bias).astype(bf16)
-    vocab_blocks = [
-        [(vocab_weight, 0), (core_rows, 0)],
-        [(first_part, 0), (core_first, 0)],
-        [(vocab_weight, half), (core_rows, half)],
-        [(second_part, 0), (core_second, 0)],
-    ]
-    (branch,) = hold([branch], core_first, core_second)
-    branch = lax.all_to_all(branch, plane, 0, 1, tiled=True)
-    heads = collect(jnp.concatenate([branch, normed], axis=1))
+        lifted,
+    )
+    everywhere = lax.all_to_all(lifted, ("kv", "seq", "vocab"), 0, 0, tiled=True)
+    branch = activate_draft(everywhere, normed, kv_count, seq_count)
+    (branch,) = hold([branch], core_first, core_second, core_rows, value_flag)
+    heads = collect(branch)
     heads = [list(group) for group in zip(*[around(head) for head in heads])]
     tally = score_vocabulary(
         numbers, candidates, heads, vocab_blocks, half, lanes
     )
-    tally = tally[1] + (swap(tally[0], "vocab", 2) + swap(tally[2], "kv", 1))
     tally = add_up(collect(tally))
     tally = lax.all_gather(tally, plane, axis=0)
-    tally = tally[:, : CAND + 1, : head_total * tok_block]
+    tally = tally.reshape(kv_count, tenants // 2, 2, 3, 16, lanes)
+    tally = tally[:, :, :, 1] + (tally[:, ::-1, :, 0] + tally[::-1, :, :, 2])
+    tally = tally[..., : CAND + 1, : head_total * tok_block]
     tally = tally.reshape(kv_count, tenants, CAND + 1, head_total, tok_block)
     log_normalizer = jnp.log(tally[:, :, 0].transpose(2, 0, 3, 1)).reshape(
         head_total, tree_size, tenants

time: 290 us -> 274 us (0.945)
  blocking collectives: 47.6 us -> 39.1 us
  Pallas kernels: 35.4 us -> 28.8 us
  local copies, waits for them, and re-layouts: 20.8 us -> 16.7 us
  waiting for transfers between devices: 76.9 us -> 80.2 us
    all_to_all x0 -> x1, waiting for transfers between devices: none -> 16.5 us  [local(): lax.all_to_all(lifted, ('kv', 'seq', 'vocab'), 0, 0, tiled=True)]
    ppermute x12 -> x9, waiting for transfers between devices: 38.4 us -> 23.6 us  [send_ahead(): lax.ppermute(pick(j), 'seq', [(i, (i + j) % count) for i in range(count)])]
    all_to_all x1 -> x0, blocking collectives: 8.96 us -> none  [local(): branch = lax.all_to_all(branch, plane, 0, 1, tiled=True)]
    ppermute x21, waiting for transfers between devices: 25.3 us -> 31.5 us  [collect(): lax.ppermute(block, 'seq', [(i, (i - j) % count) for i in range(count)])]
    pallas_call x2, Pallas kernels: 15.7 us -> 10.1 us  [update_cache(): pl.pallas_call(kernel, out_shape=(jax.ShapeDtypeStruct(cache.shape, cache...]
    ppermute x12 -> x9, starting transfers between devices: 18.2 us -> 13 us  [send_ahead(): lax.ppermute(pick(j), 'seq', [(i, (i + j) % count) for i in range(count)])]
    all_to_all x0 -> x1, starting transfers between devices: none -> 5.18 us  [local(): lax.all_to_all(lifted, ('kv', 'seq', 'vocab'), 0, 0, tiled=True)]
    ppermute x17 -> x15, waiting for transfers between devices: 13.3 us -> 8.57 us  [swap(): return lax.ppermute(values, axis, [(i, i ^ bit) for i in range(count)])]
  transfers between devices with their start and end apart: 50 -> 46, of which waited for: 29 -> 26; matrix products, arithmetic and copies ran while one was open for 11% -> 11% of each run, Pallas kernels for 7% -> 6%
where the time goes in v5:
time: 274 us; the launch traced here: 273 us
  waiting for transfers between devices  80.2 us (29%)
  starting transfers between devices  70.7 us (26%)
  blocking collectives  39.1 us (14%)
  Pallas kernels  28.8 us (11%)
  matrix products  21.8 us (8%)
  local copies, waits for them, and re-layouts  16.7 us (6%)
  other arithmetic  12.5 us (5%)
    ppermute x21, starting transfers between devices, collect(): lax.ppermute(block, 'seq', [(i, (i - j) % count) for i in range(count)])  34.6 us
    ppermute x21, waiting for transfers between devices, collect(): lax.ppermute(block, 'seq', [(i, (i - j) % count) for i in range(count)])  31.5 us
    ppermute x9, waiting for transfers between devices, send_ahead(): lax.ppermute(pick(j), 'seq', [(i, (i + j) % count) for i in range(count)])  23.6 us
    ppermute x15, starting transfers between devices, swap(): return lax.ppermute(values, axis, [(i, i ^ bit) for i in range(count)])  17.9 us
    all_to_all x1, waiting for transfers between devices, local(): lax.all_to_all(lifted, ('kv', 'seq', 'vocab'), 0, 0, tiled=True)  16.5 us
    ppermute x9, starting transfers between devices, send_ahead(): lax.ppermute(pick(j), 'seq', [(i, (i + j) % count) for i in range(count)])  13 us
    pallas_call x1, Pallas kernels, score_vocabulary(): pl.pallas_call(kernel, out_shape=jax.ShapeDtypeStruct((16 * groups, lanes...  12.1 us
    all_to_all x1, blocking collectives, local(): ffn_out = add_up(list(lax.all_to_all(ffn_out, plane, 0, 0)))  11 us
  transfers between devices with their start and end apart: 46, of which 26 were waited for; matrix products, arithmetic and copies ran while one was open for 11% of the time, Pallas kernels for 6%

profile of v5, /device:TPU:0, one launch (start us, length us, event | category | flops | bytes accessed | tf_op | source)
XLA Modules:
  0.0 272.6 jit_solution(5646933985067025682)
XLA Ops:
  0.6 3.0 %collective-permute-start = (bf16[24,896]{1,0:T(8,128)(2,1)}, bf16[24,896]{1,0:T(8,128)(2,1)S(1)}, u32[]{:S(2)}, u32[]{:S(2)}) collective-permute-start(bf16[24,896]{1,0:T(8,128)(2,1)} %bitcast.183), channel_id=1, source_target_pairs={{0,16},{16,0},{1,17},{17,1},{2,18},{18,2},{3,19},{19,3},{4,20},{20... | collective-permute-start | bytes 129032 | tf_op jit(solution)/shard_map/ppermute | solution.py:272
  7.0 7.5 %fusion.17 = bf16[4,48,1024]{2,1,0:T(8,128)(2,1)S(1)} fusion(bf16[896,4,1024]{2,1,0:T(4,128)(2,1)} %param.20, f32[896]{0:T(1024)} %param.22, bf16[24,896]{1,0:T(8,128)(2,1)S(1)} %collective-permute-done, bf16[24,896]{1,0:T(8,128)(2,1)} %bitcast.185), kind=kOutput, calls=%fused_computation.13 | convolution fusion | flops 352776192 | bytes 7822848 | tf_op jit(solution)/shard_map/td,dhc->htc/dot_general | solution.py:691
  22.7 2.9 %collective-permute-done.2 = bf16[48,1152]{1,0:T(8,128)(2,1)S(1)} collective-permute-done((bf16[48,1152]{1,0:T(8,128)(2,1)S(1)}, bf16[48,1152]{1,0:T(8,128)(2,1)S(1)}, u32[]{:S(2)}, u32[]{:S(2)}) %collective-permute-start.2) | collective-permute-done | bytes 110624 | tf_op jit(solution)/shard_map/ppermute | solution.py:243
  42.5 3.6 %collective-permute-done.8.rest_1_ = bf16[112,256]{1,0:T(8,128)(2,1)S(1)} collective-permute-done((bf16[112,256]{1,0:T(8,128)(2,1)S(1)}, bf16[112,256]{1,0:T(8,128)(2,1)S(1)}, u32[]{:S(2)}, u32[]{:S(2)}) %collective-permute-start.8) | collective-permute-done | bytes 57376 | tf_op jit(solution)/shard_map/ppermute | solution.py:243
  56.5 3.4 %shard_map.211 = (bf16[256,3584]{1,0:T(8,128)(2,1)}, bf16[256,3584]{1,0:T(8,128)(2,1)}) custom-call(bf16[512,3584]{1,0:T(8,128)(2,1)} %rest_15_.1, bf16[24,896]{1,0:T(8,128)(2,1)} %copy-done.2), custom_call_target="tpu_custom_call" | custom-call | bytes 7340032 | tf_op jit(solution)/shard_map/pallas_call | solution.py:347
  71.2 10.7 %all_gather.12.refs_2_ = bf16[192,896]{1,0:T(8,128)(2,1)} all-gather(bf16[24,896]{1,0:T(8,128)(2,1)S(1)} %get-tuple-element.51), channel_id=1, replica_groups=mesh['kv'=2,'seq'=4,'vocab'=4] {'kv','vocab'}, dimensions={0}, use_global_device_ids=true | all-gather | bytes 387072 | tf_op jit(solution)/shard_map/all_gather | solution.py:814
  83.9 4.4 %fusion.10 = bf16[192,2,1792]{2,0,1:T(8,128)(2,1)S(1)} fusion(bf16[896,2,1792]{2,1,0:T(2,128)(2,1)} %param.32, bf16[192,896]{1,0:T(8,128)(2,1)S(1)} %copy-done.8), kind=kOutput, calls=%fused_computation.9 | convolution fusion | flops 1233813504 | bytes 8142848 | tf_op jit(solution)/shard_map/td,dcf->ctf/dot_general | solution.py:817
  90.4 3.8 %collective-permute-start.19 = (bf16[2,48,1792]{2,1,0:T(8,128)(2,1)}, bf16[2,48,1792]{2,1,0:T(8,128)(2,1)}, u32[]{:S(2)}, u32[]{:S(2)}) collective-permute-start(bf16[2,48,1792]{2,1,0:T(8,128)(2,1)} %get-tuple-element.58), channel_id=1, source_target_pairs={{0,12},{4,0},{8,4},{12,8},{1,13},{5,1},{9,5},{13,9},{2,14},{6,2},{... | collective-permute-start | bytes 1032200 | tf_op jit(solution)/shard_map/ppermute | solution.py:243
  103.0 5.1 %shard_map.213 = (bf16[2048,4,256]{2,1,0:T(4,128)(2,1)}, f32[8,128]{1,0:T(8,128)}) custom-call(s32[2]{0:T(128)} %pad_add_fusion.1.numbers_ref, bf16[2048,4,256]{2,1,0:T(4,128)(2,1)} %bitcast.169, bf16[4,112,256]{2,1,0:T(8,128)(2,1)} %copy-done.5, bf16[112,256]{1,0:T(8,128)(2,1)} %copy-done.11, bf16[112,256]{1,0:T(8,128)(2,1)} %copy-done.10, ...), custom_call_target="tpu_custom_call" | custom-call | bytes 8388608 | tf_op jit(solution)/shard_map/pallas_call | solution.py:419
  110.9 13.2 %collective-permute-done.18 = bf16[2,48,1792]{2,1,0:T(8,128)(2,1)} collective-permute-done((bf16[2,48,1792]{2,1,0:T(8,128)(2,1)S(1)}, bf16[2,48,1792]{2,1,0:T(8,128)(2,1)}, u32[]{:S(2)}, u32[]{:S(2)}) %collective-permute-start.18) | collective-permute-done | bytes 344096 | tf_op jit(solution)/shard_map/ppermute | solution.py:243
  131.8 7.5 %collective-permute-done.22 = bf16[48,1792]{1,0:T(8,128)(2,1)S(1)} collective-permute-done((bf16[48,1792]{1,0:T(8,128)(2,1)}, bf16[48,1792]{1,0:T(8,128)(2,1)S(1)}, u32[]{:S(2)}, u32[]{:S(2)}) %collective-permute-start.22) | collective-permute-done | bytes 172064 | tf_op jit(solution)/shard_map/ppermute | solution.py:251
  143.9 11.0 %all_to_all.10 = bf16[8,24,896]{2,1,0:T(8,128)(2,1)S(1)} all-to-all(bf16[8,24,896]{2,1,0:T(8,128)(2,1)} %get-tuple-element.29), channel_id=1, replica_groups=mesh['kv'=2,'seq'=4,'vocab'=4] {'kv','vocab'}, dimensions={0} | all-to-all | bytes 688128 | tf_op jit(solution)/shard_map/all_to_all | solution.py:874
  156.4 3.1 %collective-permute-start.26 = (f32[24,128]{1,0:T(8,128)S(1)}, f32[24,128]{1,0:T(8,128)S(1)}, u32[]{:S(2)}, u32[]{:S(2)}) collective-permute-start(f32[24,128]{1,0:T(8,128)S(1)} %pad_maximum_fusion.8), channel_id=1, source_target_pairs={{0,8},{4,12},{8,0},{12,4},{1,9},{5,13},{9,1},{13,5},{2,10},{6,14},... | collective-permute-start | bytes 36872 | tf_op jit(solution)/shard_map/ppermute | solution.py:251
  166.2 8.8 %all_gather.13 = bf16[192,896]{1,0:T(8,128)(2,1)S(1)} all-gather(bf16[24,896]{1,0:T(8,128)(2,1)S(1)} %multiply_convert_fusion.normed_ref), channel_id=1, replica_groups=mesh['kv'=2,'seq'=4,'vocab'=4] {'kv','vocab'}, dimensions={0}, use_global_device_ids=true | all-gather | bytes 387072 | tf_op jit(solution)/shard_map/all_gather | solution.py:878
  175.0 3.0 %add_convert_fusion = bf16[192,4,448]{2,0,1:T(8,128)(2,1)S(1)} fusion(bf16[4,896,448]{1,2,0:T(8,128)(2,1)} %param.34, f32[4,448]{1,0:T(4,128)S(1)} %broadcast_multiply_fusion, bf16[192,896]{1,0:T(8,128)(2,1)S(1)} %all_gather.13), kind=kOutput, calls=%fused_computation.10 | convolution fusion | flops 617250816 | bytes 4250624 | tf_op jit(solution)/shard_map/td,ndc->ntc/dot_general | solution.py:879
  179.6 5.2 %all-to-all-start.1 = ((bf16[32,24,448]{2,1,0:T(8,128)(2,1)}), bf16[32,24,448]{2,1,0:T(8,128)(2,1)}, u32[]{:S(2)}, u32[]{:S(2)}) async-start(bf16[32,24,448]{2,1,0:T(8,128)(2,1)} %bitcast.167), calls=%async_computation.1 | async-start | bytes 1572864 | tf_op jit(solution)/shard_map/all_to_all | solution.py:907
  184.8 5.0 %shard_map.217 = (bf16[2048,4,256]{2,1,0:T(4,128)(2,1)}, f32[8,128]{1,0:T(8,128)}) custom-call(s32[2]{0:T(128)} %pad_add_fusion.1.numbers_ref, bf16[2048,4,256]{2,1,0:T(4,128)(2,1)} %bitcast.171, bf16[4,112,256]{2,1,0:T(8,128)(2,1)} %copy-done.5, bf16[112,256]{1,0:T(8,128)(2,1)} %copy-done.11, bf16[112,256]{1,0:T(8,128)(2,1)} %copy-done.10, ...), custom_call_target="tpu_custom_call" | custom-call | bytes 8388608 | tf_op jit(solution)/shard_map/pallas_call | solution.py:419
  189.8 16.5 %all-to-all-done.1.parts_ref = bf16[32,24,448]{2,1,0:T(8,128)(2,1)} async-done(((bf16[32,24,448]{2,1,0:T(8,128)(2,1)}), bf16[32,24,448]{2,1,0:T(8,128)(2,1)}, u32[]{:S(2)}, u32[]{:S(2)}) %all-to-all-start.1) | async-done | bytes 688160 | tf_op jit(solution)/shard_map/all_to_all | solution.py:907
  214.3 4.5 %collective-permute-done.36.rest_10_ = bf16[24,4480]{1,0:T(8,128)(2,1)S(1)} collective-permute-done((bf16[24,4480]{1,0:T(8,128)(2,1)}, bf16[24,4480]{1,0:T(8,128)(2,1)S(1)}, u32[]{:S(2)}, u32[]{:S(2)}) %collective-permute-start.36) | collective-permute-done | bytes 215072 | tf_op jit(solution)/shard_map/ppermute | solution.py:251
  220.8 5.8 %collective-permute-done.34.rest_9_ = bf16[24,4480]{1,0:T(8,128)(2,1)S(1)} collective-permute-done((bf16[24,4480]{1,0:T(8,128)(2,1)}, bf16[24,4480]{1,0:T(8,128)(2,1)S(1)}, u32[]{:S(2)}, u32[]{:S(2)}) %collective-permute-start.34) | collective-permute-done | bytes 215072 | tf_op jit(solution)/shard_map/ppermute | solution.py:251
  230.7 4.2 %collective-permute-done.40.rest_13_ = bf16[24,4480]{1,0:T(8,128)(2,1)S(1)} collective-permute-done((bf16[24,4480]{1,0:T(8,128)(2,1)S(1)}, bf16[24,4480]{1,0:T(8,128)(2,1)S(1)}, u32[]{:S(2)}, u32[]{:S(2)}) %collective-permute-start.40) | collective-permute-done | bytes 215072 | tf_op jit(solution)/shard_map/ppermute | solution.py:272
  239.6 12.1 %shard_map.221 = f32[48,128]{1,0:T(8,128)} custom-call(s32[12]{0:T(128)} %get-tuple-element.31.numbers_ref, s32[5,24,8]{2,1,0:T(8,128)} %get-tuple-element.32.rest_0_, s32[5,24,8]{2,1,0:T(8,128)} %get-tuple-element.33.rest_1_, s32[5,24,8]{2,1,0:T(8,128)} %get-tuple-element.34.rest_2_, bf16[24,4480]{1,0:T(8,128)(2,1)} %copy-done.19, ...), custom_call_target="tpu_custom_call" | custom-call | flops 3758096384 | bytes 14680064 | tf_op jit(solution)/shard_map/pallas_call | solution.py:559
  251.7 4.2 %collective-permute-start.44 = (f32[48,128]{1,0:T(8,128)}, f32[48,128]{1,0:T(8,128)S(1)}, u32[]{:S(2)}, u32[]{:S(2)}) collective-permute-start(f32[48,128]{1,0:T(8,128)} %shard_map.221), channel_id=1, source_target_pairs={{0,4},{4,8},{8,12},{12,0},{1,5},{5,9},{9,13},{13,1},{2,6},{6,10},{... | collective-permute-start | bytes 73736 | tf_op jit(solution)/shard_map/ppermute | solution.py:251
  261.9 8.7 %all-gather = f32[384,128]{1,0:T(8,128)S(1)} all-gather(f32[48,128]{1,0:T(8,128)S(1)} %add_add_fusion.1), channel_id=2, replica_groups=mesh['kv'=2,'seq'=4,'vocab'=4] {'kv','vocab'}, dimensions={0}, use_global_device_ids=true | all-gather | bytes 221184 | tf_op jit(solution)/shard_map/all_gather | solution.py:916
  (243 shorter events, 112.9 us)
Async XLA Ops:
  16.8 8.9 %collective-permute-start.2 = (bf16[48,1152]{1,0:T(8,128)(2,1)S(1)}, bf16[48,1152]{1,0:T(8,128)(2,1)S(1)}, u32[]{:S(2)}, u32[]{:S(2)}) collective-permute-start(bf16[48,1152]{1,0:T(8,128)(2,1)S(1)} %get-tuple-element.61), channel_id=1, source_target_pairs={{0,8},{4,12},{8,0},{12,4},{1,9},{5,13},{9,1},{13,5},{2,10},{6,14},... | collective-permute-start | bytes 331784 | tf_op jit(solution)/shard_map/ppermute | solution.py:243
  26.5 8.6 %collective-permute-start.6 = (bf16[96,256]{1,0:T(8,128)(2,1)S(1)}, bf16[96,256]{1,0:T(8,128)(2,1)S(1)}, u32[]{:S(2)}, u32[]{:S(2)}) collective-permute-start(bf16[96,256]{1,0:T(8,128)(2,1)S(1)} %pad_maximum_fusion.2), channel_id=1, source_target_pairs={{0,4},{4,8},{8,12},{12,0},{1,5},{5,9},{9,13},{13,1},{2,6},{6,10},{... | collective-permute-start | bytes 147464 | tf_op jit(solution)/shard_map/ppermute | solution.py:251
  81.9 44.4 %collective-permute-start.20 = (bf16[256,3584]{1,0:T(8,128)(2,1)}, bf16[256,3584]{1,0:T(8,128)(2,1)}, u32[]{:S(2)}, u32[]{:S(2)}) collective-permute-start(bf16[256,3584]{1,0:T(8,128)(2,1)} %get-tuple-element.27), channel_id=1, source_target_pairs={{0,16},{16,0},{1,17},{17,1},{2,18},{18,2},{3,19},{19,3},{4,20},{20... | collective-permute-start | bytes 5505032 | tf_op jit(solution)/shard_map/ppermute | solution.py:272
  82.5 43.8 %collective-permute-start.21 = (bf16[256,3584]{1,0:T(8,128)(2,1)}, bf16[256,3584]{1,0:T(8,128)(2,1)}, u32[]{:S(2)}, u32[]{:S(2)}) collective-permute-start(bf16[256,3584]{1,0:T(8,128)(2,1)} %get-tuple-element.28), channel_id=1, source_target_pairs={{0,2},{1,3},{2,0},{3,1},{4,6},{5,7},{6,4},{7,5},{8,10},{9,11},{10,... | collective-permute-start | bytes 5505032 | tf_op jit(solution)/shard_map/ppermute | solution.py:272
  90.4 18.4 %collective-permute-start.17 = (bf16[2,48,1792]{2,1,0:T(8,128)(2,1)}, bf16[2,48,1792]{2,1,0:T(8,128)(2,1)}, u32[]{:S(2)}, u32[]{:S(2)}) collective-permute-start(bf16[2,48,1792]{2,1,0:T(8,128)(2,1)} %get-tuple-element.57), channel_id=1, source_target_pairs={{0,4},{4,8},{8,12},{12,0},{1,5},{5,9},{9,13},{13,1},{2,6},{6,10},{... | collective-permute-start | bytes 1032200 | tf_op jit(solution)/shard_map/ppermute | solution.py:243
  90.4 20.6 %collective-permute-start.19 = (bf16[2,48,1792]{2,1,0:T(8,128)(2,1)}, bf16[2,48,1792]{2,1,0:T(8,128)(2,1)}, u32[]{:S(2)}, u32[]{:S(2)}) collective-permute-start(bf16[2,48,1792]{2,1,0:T(8,128)(2,1)} %get-tuple-element.58), channel_id=1, source_target_pairs={{0,12},{4,0},{8,4},{12,8},{1,13},{5,1},{9,5},{13,9},{2,14},{6,2},{... | collective-permute-start | bytes 1032200 | tf_op jit(solution)/shard_map/ppermute | solution.py:243
  94.2 29.9 %collective-permute-start.18 = (bf16[2,48,1792]{2,1,0:T(8,128)(2,1)S(1)}, bf16[2,48,1792]{2,1,0:T(8,128)(2,1)}, u32[]{:S(2)}, u32[]{:S(2)}) collective-permute-start(bf16[2,48,1792]{2,1,0:T(8,128)(2,1)S(1)} %get-tuple-element.59), channel_id=1, source_target_pairs={{0,8},{4,12},{8,0},{12,4},{1,9},{5,13},{9,1},{13,5},{2,10},{6,14},... | collective-permute-start | bytes 1032200 | tf_op jit(solution)/shard_map/ppermute | solution.py:243
  108.8 99.6 %collective-permute-start.30 = (bf16[512,3584]{1,0:T(8,128)(2,1)}, bf16[512,3584]{1,0:T(8,128)(2,1)}, u32[]{:S(2)}, u32[]{:S(2)}) collective-permute-start(bf16[512,3584]{1,0:T(8,128)(2,1)} %rest_15_.1), channel_id=1, source_target_pairs={{0,1},{1,0},{2,3},{3,2},{4,5},{5,4},{6,7},{7,6},{8,9},{9,8},{10,11... | collective-permute-start | bytes 11010056 | tf_op jit(solution)/shard_map/ppermute | solution.py:272
  126.3 16.2 %collective-permute-start.24 = (bf16[48,1792]{1,0:T(8,128)(2,1)}, bf16[48,1792]{1,0:T(8,128)(2,1)S(1)}, u32[]{:S(2)}, u32[]{:S(2)}) collective-permute-start(bf16[48,1792]{1,0:T(8,128)(2,1)} %shard_map.215), channel_id=1, source_target_pairs={{0,4},{4,8},{8,12},{12,0},{1,5},{5,9},{9,13},{13,1},{2,6},{6,10},{... | collective-permute-start | bytes 516104 | tf_op jit(solution)/shard_map/ppermute | solution.py:251
  126.4 15.5 %collective-permute-start.23 = (bf16[48,1792]{1,0:T(8,128)(2,1)}, bf16[48,1792]{1,0:T(8,128)(2,1)S(1)}, u32[]{:S(2)}, u32[]{:S(2)}) collective-permute-start(bf16[48,1792]{1,0:T(8,128)(2,1)} %shard_map.215), channel_id=1, source_target_pairs={{0,8},{4,12},{8,0},{12,4},{1,9},{5,13},{9,1},{13,5},{2,10},{6,14},... | collective-permute-start | bytes 516104 | tf_op jit(solution)/shard_map/ppermute | solution.py:251
  128.4 10.9 %collective-permute-start.22 = (bf16[48,1792]{1,0:T(8,128)(2,1)}, bf16[48,1792]{1,0:T(8,128)(2,1)S(1)}, u32[]{:S(2)}, u32[]{:S(2)}) collective-permute-start(bf16[48,1792]{1,0:T(8,128)(2,1)} %shard_map.215), channel_id=1, source_target_pairs={{0,12},{4,0},{8,4},{12,8},{1,13},{5,1},{9,5},{13,9},{2,14},{6,2},{... | collective-permute-start | bytes 516104 | tf_op jit(solution)/shard_map/ppermute | solution.py:251
  179.1 29.2 %collective-permute-start.28 = (bf16[256,3584]{1,0:T(8,128)(2,1)}, bf16[256,3584]{1,0:T(8,128)(2,1)}, u32[]{:S(2)}, u32[]{:S(2)}) collective-permute-start(bf16[256,3584]{1,0:T(8,128)(2,1)} %get-tuple-element.35.rest_17_), channel_id=1, source_target_pairs={{0,1},{1,0},{2,3},{3,2},{4,5},{5,4},{6,7},{7,6},{8,9},{9,8},{10,11... | collective-permute-start | bytes 5505032 | tf_op jit(solution)/shard_map/ppermute | solution.py:272
  179.4 28.9 %collective-permute-start.29 = (bf16[256,3584]{1,0:T(8,128)(2,1)}, bf16[256,3584]{1,0:T(8,128)(2,1)}, u32[]{:S(2)}, u32[]{:S(2)}) collective-permute-start(bf16[256,3584]{1,0:T(8,128)(2,1)} %get-tuple-element.36.rest_19_), channel_id=1, source_target_pairs={{0,1},{1,0},{2,3},{3,2},{4,5},{5,4},{6,7},{7,6},{8,9},{9,8},{10,11... | collective-permute-start | bytes 5505032 | tf_op jit(solution)/shard_map/ppermute | solution.py:272
  179.6 26.7 %all-to-all-start.1 = ((bf16[32,24,448]{2,1,0:T(8,128)(2,1)}), bf16[32,24,448]{2,1,0:T(8,128)(2,1)}, u32[]{:S(2)}, u32[]{:S(2)}) async-start(bf16[32,24,448]{2,1,0:T(8,128)(2,1)} %bitcast.167), calls=%async_computation.1 | async-start | bytes 1572864 | tf_op jit(solution)/shard_map/all_to_all | solution.py:907
  208.4 10.4 %collective-permute-start.36 = (bf16[24,4480]{1,0:T(8,128)(2,1)}, bf16[24,4480]{1,0:T(8,128)(2,1)S(1)}, u32[]{:S(2)}, u32[]{:S(2)}) collective-permute-start(bf16[24,4480]{1,0:T(8,128)(2,1)} %shard_map.220.rest_7_), channel_id=1, source_target_pairs={{0,4},{4,8},{8,12},{12,0},{1,5},{5,9},{9,13},{13,1},{2,6},{6,10},{... | collective-permute-start | bytes 645128 | tf_op jit(solution)/shard_map/ppermute | solution.py:251
  208.7 11.1 %collective-permute-start.38 = (bf16[24,4480]{1,0:T(8,128)(2,1)}, bf16[24,4480]{1,0:T(8,128)(2,1)S(1)}, u32[]{:S(2)}, u32[]{:S(2)}) collective-permute-start(bf16[24,4480]{1,0:T(8,128)(2,1)} %shard_map.220.rest_7_), channel_id=1, source_target_pairs={{0,16},{16,0},{1,17},{17,1},{2,18},{18,2},{3,19},{19,3},{4,20},{20... | collective-permute-start | bytes 645128 | tf_op jit(solution)/shard_map/ppermute | solution.py:272
  210.2 16.4 %collective-permute-start.34 = (bf16[24,4480]{1,0:T(8,128)(2,1)}, bf16[24,4480]{1,0:T(8,128)(2,1)S(1)}, u32[]{:S(2)}, u32[]{:S(2)}) collective-permute-start(bf16[24,4480]{1,0:T(8,128)(2,1)} %shard_map.220.rest_7_), channel_id=1, source_target_pairs={{0,8},{4,12},{8,0},{12,4},{1,9},{5,13},{9,1},{13,5},{2,10},{6,14},... | collective-permute-start | bytes 645128 | tf_op jit(solution)/shard_map/ppermute | solution.py:251
  211.3 16.2 %collective-permute-start.32 = (bf16[24,4480]{1,0:T(8,128)(2,1)}, bf16[24,4480]{1,0:T(8,128)(2,1)S(1)}, u32[]{:S(2)}, u32[]{:S(2)}) collective-permute-start(bf16[24,4480]{1,0:T(8,128)(2,1)} %shard_map.220.rest_7_), channel_id=1, source_target_pairs={{0,12},{4,0},{8,4},{12,8},{1,13},{5,1},{9,5},{13,9},{2,14},{6,2},{... | collective-permute-start | bytes 645128 | tf_op jit(solution)/shard_map/ppermute | solution.py:251
  213.2 14.5 %collective-permute-start.31 = (bf16[24,4480]{1,0:T(8,128)(2,1)}, bf16[24,4480]{1,0:T(8,128)(2,1)S(1)}, u32[]{:S(2)}, u32[]{:S(2)}) collective-permute-start(bf16[24,4480]{1,0:T(8,128)(2,1)} %shard_map.220.rest_7_), channel_id=1, source_target_pairs={{0,2},{1,3},{2,0},{3,1},{4,6},{5,7},{6,4},{7,5},{8,10},{9,11},{10,... | collective-permute-start | bytes 645128 | tf_op jit(solution)/shard_map/ppermute | solution.py:272
  218.7 10.7 %collective-permute-start.41 = (bf16[24,4480]{1,0:T(8,128)(2,1)S(1)}, bf16[24,4480]{1,0:T(8,128)(2,1)S(1)}, u32[]{:S(2)}, u32[]{:S(2)}) collective-permute-start(bf16[24,4480]{1,0:T(8,128)(2,1)S(1)} %collective-permute-done.36.rest_10_), channel_id=1, source_target_pairs={{0,16},{16,0},{1,17},{17,1},{2,18},{18,2},{3,19},{19,3},{4,20},{20... | collective-permute-start | bytes 645128 | tf_op jit(solution)/shard_map/ppermute | solution.py:272
  219.8 10.9 %collective-permute-start.37 = (bf16[24,4480]{1,0:T(8,128)(2,1)S(1)}, bf16[24,4480]{1,0:T(8,128)(2,1)S(1)}, u32[]{:S(2)}, u32[]{:S(2)}) collective-permute-start(bf16[24,4480]{1,0:T(8,128)(2,1)S(1)} %collective-permute-done.36.rest_10_), channel_id=1, source_target_pairs={{0,2},{1,3},{2,0},{3,1},{4,6},{5,7},{6,4},{7,5},{8,10},{9,11},{10,... | collective-permute-start | bytes 645128 | tf_op jit(solution)/shard_map/ppermute | solution.py:272
  226.6 8.2 %collective-permute-start.40 = (bf16[24,4480]{1,0:T(8,128)(2,1)S(1)}, bf16[24,4480]{1,0:T(8,128)(2,1)S(1)}, u32[]{:S(2)}, u32[]{:S(2)}) collective-permute-start(bf16[24,4480]{1,0:T(8,128)(2,1)S(1)} %collective-permute-done.34.rest_9_), channel_id=1, source_target_pairs={{0,16},{16,0},{1,17},{17,1},{2,18},{18,2},{3,19},{19,3},{4,20},{20... | collective-permute-start | bytes 645128 | tf_op jit(solution)/shard_map/ppermute | solution.py:272
  227.8 10.1 %collective-permute-start.39 = (bf16[24,4480]{1,0:T(8,128)(2,1)S(1)}, bf16[24,4480]{1,0:T(8,128)(2,1)S(1)}, u32[]{:S(2)}, u32[]{:S(2)}) collective-permute-start(bf16[24,4480]{1,0:T(8,128)(2,1)S(1)} %collective-permute-done.32.rest_8_), channel_id=1, source_target_pairs={{0,16},{16,0},{1,17},{17,1},{2,18},{18,2},{3,19},{19,3},{4,20},{20... | collective-permute-start | bytes 645128 | tf_op jit(solution)/shard_map/ppermute | solution.py:272
  229.4 9.5 %collective-permute-start.33 = (bf16[24,4480]{1,0:T(8,128)(2,1)S(1)}, bf16[24,4480]{1,0:T(8,128)(2,1)S(1)}, u32[]{:S(2)}, u32[]{:S(2)}) collective-permute-start(bf16[24,4480]{1,0:T(8,128)(2,1)S(1)} %collective-permute-done.32.rest_8_), channel_id=1, source_target_pairs={{0,2},{1,3},{2,0},{3,1},{4,6},{5,7},{6,4},{7,5},{8,10},{9,11},{10,... | collective-permute-start | bytes 645128 | tf_op jit(solution)/shard_map/ppermute | solution.py:272
  (52 other events, 526.6 us)

commit v6 on v5

--- a/solution.py
+++ b/solution.py
@@ -610,6 +610,53 @@
         in_specs=[vmem] * 2,
         out_specs=vmem,
     )(parts, normed)
+
+
+def project_in(rows, weight):
+    tokens, depth = rows.shape
+    _, heads, columns = weight.shape
+    unit = 128
+
+    def kernel(rows_ref, weight_ref, out_ref, spread, total):
+        source = lax.broadcasted_iota(jnp.int32, (unit, unit * heads), 0)
+        place = lax.broadcasted_iota(jnp.int32, (unit, unit * heads), 1)
+        for h in range(heads):
+            spread[h] = jnp.where(place == source * heads + h, 1.0, 0.0).astype(rows.dtype)
+        total[...] = jnp.zeros_like(total)
+        for k in range(depth // unit):
+            block = rows_ref[:, k * unit : (k + 1) * unit]
+            wide = jnp.concatenate(
+                [
+                    jnp.dot(block, spread[h], preferred_element_type=jnp.float32)
+                    for h in range(heads)
+                ],
+                axis=0,
+            ).astype(rows.dtype)
+            total[...] += jnp.dot(
+                wide,
+                weight_ref[k * unit : (k + 1) * unit].reshape(unit * heads, columns),
+                preferred_element_type=jnp.float32,
+            )
+        for h in range(heads):
+            out_ref[h] = total[h * tokens : (h + 1) * tokens, :].astype(out_ref.dtype)
+
+    vmem = pl.BlockSpec(memory_space=pltpu.VMEM)
+    return pl.pallas_call(
+        kernel,
+        out_shape=jax.ShapeDtypeStruct((heads, tokens, columns), rows.dtype),
+        in_specs=[vmem] * 2,
+        out_specs=vmem,
+        scratch_shapes=[
+            pltpu.VMEM((heads, unit, unit * heads), rows.dtype),
+            pltpu.VMEM((heads * tokens, columns), jnp.float32),
+        ],
+        compiler_params=pltpu.CompilerParams(vmem_limit_bytes=24 * 2**20),
+        cost_estimate=pl.CostEstimate(
+            flops=2 * heads * tokens * weight.size,
+            bytes_accessed=2 * weight.size,
+            transcendentals=0,
+        ),
+    )(rows, weight)
 
 
 def project_out(places, attended, weight, own_rows):
@@ -688,9 +735,7 @@
 
     tenant_float = tenant_state.astype(f32)
     scaled_input = (tenant_float * norm_pre_attention).astype(bf16)
-    projected = jnp.einsum(
-        "td,dhc->htc", scaled_input, input_projection, preferred_element_type=f32
-    ).astype(bf16)
+    projected = project_in(scaled_input, input_projection)
     square_lanes = split_lanes(jnp.sum(tenant_float * tenant_float, axis=-1, keepdims=True))
     head_count = projected.shape[0]
     pair = 2 * HEAD_SIZE

time: 274 us -> 272 us (level)
  Pallas kernels: 28.8 us -> 37.2 us
  matrix products: 21.8 us -> 14.3 us
  waiting for transfers between devices: 80.2 us -> 76.8 us
  local copies, waits for them, and re-layouts: 16.7 us -> 19.8 us
    dot_general x1 -> x0, matrix products: 7.53 us -> none  [local(): jnp.einsum('td,dhc->htc', scaled_input, input_projection, preferred_eleme...]
    pallas_call x2, Pallas kernels: 10.1 us -> 15.8 us  [update_cache(): pl.pallas_call(kernel, out_shape=(jax.ShapeDtypeStruct(cache.shape, cache...]
    unnamed x63 -> x65, local copies, waits for them, and re-layouts: 4.38 us -> 7.47 us
    all_to_all x1, waiting for transfers between devices: 16.5 us -> 13.7 us  [local(): lax.all_to_all(lifted, ('kv', 'seq', 'vocab'), 0, 0, tiled=True)]
  transfers between devices with their start and end apart: 46 -> 46, of which waited for: 26 -> 26; matrix products, arithmetic and copies ran while one was open for 11% -> 11% of each run, Pallas kernels for 6% -> 8%
where the time goes in v6:
time: 272 us; the launch traced here: 271 us
  waiting for transfers between devices  76.8 us (28%)
  starting transfers between devices  68.5 us (25%)
  blocking collectives  38.9 us (14%)
  Pallas kernels  37.2 us (14%)
  local copies, waits for them, and re-layouts  19.8 us (7%)
  matrix products  14.3 us (5%)
  other arithmetic  12.4 us (5%)
  between operations  2.72 us (1%)
    ppermute x21, starting transfers between devices, collect(): lax.ppermute(block, 'seq', [(i, (i - j) % count) for i in range(count)])  34.6 us
    ppermute x21, waiting for transfers between devices, collect(): lax.ppermute(block, 'seq', [(i, (i - j) % count) for i in range(count)])  31.6 us
    ppermute x9, waiting for transfers between devices, send_ahead(): lax.ppermute(pick(j), 'seq', [(i, (i + j) % count) for i in range(count)])  23 us
    pallas_call x2, Pallas kernels, update_cache(): pl.pallas_call(kernel, out_shape=(jax.ShapeDtypeStruct(cache.shape, cache...  15.8 us
    ppermute x15, starting transfers between devices, swap(): return lax.ppermute(values, axis, [(i, i ^ bit) for i in range(count)])  15.7 us
    all_to_all x1, waiting for transfers between devices, local(): lax.all_to_all(lifted, ('kv', 'seq', 'vocab'), 0, 0, tiled=True)  13.7 us
    ppermute x9, starting transfers between devices, send_ahead(): lax.ppermute(pick(j), 'seq', [(i, (i + j) % count) for i in range(count)])  13 us
    pallas_call x1, Pallas kernels, score_vocabulary(): pl.pallas_call(kernel, out_shape=jax.ShapeDtypeStruct((16 * groups, lanes...  12 us
  transfers between devices with their start and end apart: 46, of which 26 were waited for; matrix products, arithmetic and copies ran while one was open for 11% of the time, Pallas kernels for 8%

profile of v6, /device:TPU:0, one launch (start us, length us, event | category | flops | bytes accessed | tf_op | source)
XLA Modules:
  0.0 270.7 jit_solution(13894114702458433257)
XLA Ops:
  0.6 3.0 %collective-permute-start = (bf16[24,896]{1,0:T(8,128)(2,1)}, bf16[24,896]{1,0:T(8,128)(2,1)S(1)}, u32[]{:S(2)}, u32[]{:S(2)}) collective-permute-start(bf16[24,896]{1,0:T(8,128)(2,1)} %bitcast.178), channel_id=1, source_target_pairs={{0,16},{16,0},{1,17},{17,1},{2,18},{18,2},{3,19},{19,3},{4,20},{20... | collective-permute-start | bytes 129032 | tf_op jit(solution)/shard_map/ppermute | solution.py:272
  7.0 3.1 %copy-done.1 = bf16[896,4,1024]{2,1,0:T(4,128)(2,1)S(1)} copy-done((bf16[896,4,1024]{2,1,0:T(4,128)(2,1)S(1)}, bf16[896,4,1024]{2,1,0:T(4,128)(2,1)}, u32[]{:S(2)}) %copy-start.1) | copy-done | bytes 7340056
  21.0 2.9 %collective-permute-done.2 = bf16[48,1152]{1,0:T(8,128)(2,1)S(1)} collective-permute-done((bf16[48,1152]{1,0:T(8,128)(2,1)S(1)}, bf16[48,1152]{1,0:T(8,128)(2,1)S(1)}, u32[]{:S(2)}, u32[]{:S(2)}) %collective-permute-start.2) | collective-permute-done | bytes 110624 | tf_op jit(solution)/shard_map/ppermute | solution.py:243
  40.8 3.6 %collective-permute-done.8.rest_1_ = bf16[112,256]{1,0:T(8,128)(2,1)S(1)} collective-permute-done((bf16[112,256]{1,0:T(8,128)(2,1)S(1)}, bf16[112,256]{1,0:T(8,128)(2,1)S(1)}, u32[]{:S(2)}, u32[]{:S(2)}) %collective-permute-start.8) | collective-permute-done | bytes 57376 | tf_op jit(solution)/shard_map/ppermute | solution.py:243
  54.8 3.4 %shard_map.212 = (bf16[256,3584]{1,0:T(8,128)(2,1)}, bf16[256,3584]{1,0:T(8,128)(2,1)}) custom-call(bf16[512,3584]{1,0:T(8,128)(2,1)} %rest_15_.1, bf16[24,896]{1,0:T(8,128)(2,1)} %copy-done.3), custom_call_target="tpu_custom_call" | custom-call | bytes 7340032 | tf_op jit(solution)/shard_map/pallas_call | solution.py:347
  69.5 10.5 %all_gather.12.refs_2_ = bf16[192,896]{1,0:T(8,128)(2,1)} all-gather(bf16[24,896]{1,0:T(8,128)(2,1)S(1)} %get-tuple-element.51), channel_id=1, replica_groups=mesh['kv'=2,'seq'=4,'vocab'=4] {'kv','vocab'}, dimensions={0}, use_global_device_ids=true | all-gather | bytes 387072 | tf_op jit(solution)/shard_map/all_gather | solution.py:859
  82.0 4.4 %fusion.8 = bf16[192,2,1792]{2,0,1:T(8,128)(2,1)S(1)} fusion(bf16[896,2,1792]{2,1,0:T(2,128)(2,1)} %param.32, bf16[192,896]{1,0:T(8,128)(2,1)S(1)} %copy-done.9), kind=kOutput, calls=%fused_computation.7 | convolution fusion | flops 1233813504 | bytes 8142848 | tf_op jit(solution)/shard_map/td,dcf->ctf/dot_general | solution.py:862
  88.5 3.8 %collective-permute-start.19 = (bf16[2,48,1792]{2,1,0:T(8,128)(2,1)}, bf16[2,48,1792]{2,1,0:T(8,128)(2,1)}, u32[]{:S(2)}, u32[]{:S(2)}) collective-permute-start(bf16[2,48,1792]{2,1,0:T(8,128)(2,1)} %get-tuple-element.58), channel_id=1, source_target_pairs={{0,12},{4,0},{8,4},{12,8},{1,13},{5,1},{9,5},{13,9},{2,14},{6,2},{... | collective-permute-start | bytes 1032200 | tf_op jit(solution)/shard_map/ppermute | solution.py:243
  101.2 8.0 %shard_map.214 = (bf16[2048,4,256]{2,1,0:T(4,128)(2,1)}, f32[8,128]{1,0:T(8,128)}) custom-call(s32[2]{0:T(128)} %pad_add_fusion.1.numbers_ref, bf16[2048,4,256]{2,1,0:T(4,128)(2,1)} %bitcast.164, bf16[4,112,256]{2,1,0:T(8,128)(2,1)} %copy-done.6, bf16[112,256]{1,0:T(8,128)(2,1)} %copy-done.12, bf16[112,256]{1,0:T(8,128)(2,1)} %copy-done.11, ...), custom_call_target="tpu_custom_call" | custom-call | bytes 8388608 | tf_op jit(solution)/shard_map/pallas_call | solution.py:419
  109.7 12.5 %collective-permute-done.18 = bf16[2,48,1792]{2,1,0:T(8,128)(2,1)} collective-permute-done((bf16[2,48,1792]{2,1,0:T(8,128)(2,1)S(1)}, bf16[2,48,1792]{2,1,0:T(8,128)(2,1)}, u32[]{:S(2)}, u32[]{:S(2)}) %collective-permute-start.18) | collective-permute-done | bytes 344096 | tf_op jit(solution)/shard_map/ppermute | solution.py:243
  130.0 7.5 %collective-permute-done.22 = bf16[48,1792]{1,0:T(8,128)(2,1)S(1)} collective-permute-done((bf16[48,1792]{1,0:T(8,128)(2,1)}, bf16[48,1792]{1,0:T(8,128)(2,1)S(1)}, u32[]{:S(2)}, u32[]{:S(2)}) %collective-permute-start.22) | collective-permute-done | bytes 172064 | tf_op jit(solution)/shard_map/ppermute | solution.py:251
  142.1 11.0 %all_to_all.10 = bf16[8,24,896]{2,1,0:T(8,128)(2,1)S(1)} all-to-all(bf16[8,24,896]{2,1,0:T(8,128)(2,1)} %get-tuple-element.29), channel_id=1, replica_groups=mesh['kv'=2,'seq'=4,'vocab'=4] {'kv','vocab'}, dimensions={0} | all-to-all | bytes 688128 | tf_op jit(solution)/shard_map/all_to_all | solution.py:919
  154.5 3.1 %collective-permute-start.26 = (f32[24,128]{1,0:T(8,128)S(1)}, f32[24,128]{1,0:T(8,128)S(1)}, u32[]{:S(2)}, u32[]{:S(2)}) collective-permute-start(f32[24,128]{1,0:T(8,128)S(1)} %pad_maximum_fusion.7), channel_id=1, source_target_pairs={{0,8},{4,12},{8,0},{12,4},{1,9},{5,13},{9,1},{13,5},{2,10},{6,14},... | collective-permute-start | bytes 36872 | tf_op jit(solution)/shard_map/ppermute | solution.py:251
  164.4 8.8 %all_gather.13 = bf16[192,896]{1,0:T(8,128)(2,1)S(1)} all-gather(bf16[24,896]{1,0:T(8,128)(2,1)S(1)} %multiply_convert_fusion.normed_ref), channel_id=1, replica_groups=mesh['kv'=2,'seq'=4,'vocab'=4] {'kv','vocab'}, dimensions={0}, use_global_device_ids=true | all-gather | bytes 387072 | tf_op jit(solution)/shard_map/all_gather | solution.py:923
  173.2 3.0 %add_convert_fusion = bf16[192,4,448]{2,0,1:T(8,128)(2,1)S(1)} fusion(bf16[4,896,448]{1,2,0:T(8,128)(2,1)} %param.34, f32[4,448]{1,0:T(4,128)S(1)} %broadcast_multiply_fusion, bf16[192,896]{1,0:T(8,128)(2,1)S(1)} %all_gather.13), kind=kOutput, calls=%fused_computation.8 | convolution fusion | flops 617250816 | bytes 4250624 | tf_op jit(solution)/shard_map/td,ndc->ntc/dot_general | solution.py:924
  177.7 5.2 %all-to-all-start.1 = ((bf16[32,24,448]{2,1,0:T(8,128)(2,1)}), bf16[32,24,448]{2,1,0:T(8,128)(2,1)}, u32[]{:S(2)}, u32[]{:S(2)}) async-start(bf16[32,24,448]{2,1,0:T(8,128)(2,1)} %bitcast.162), calls=%async_computation.1 | async-start | bytes 1572864 | tf_op jit(solution)/shard_map/all_to_all | solution.py:952
  182.9 7.8 %shard_map.218 = (bf16[2048,4,256]{2,1,0:T(4,128)(2,1)}, f32[8,128]{1,0:T(8,128)}) custom-call(s32[2]{0:T(128)} %pad_add_fusion.1.numbers_ref, bf16[2048,4,256]{2,1,0:T(4,128)(2,1)} %bitcast.166, bf16[4,112,256]{2,1,0:T(8,128)(2,1)} %copy-done.6, bf16[112,256]{1,0:T(8,128)(2,1)} %copy-done.12, bf16[112,256]{1,0:T(8,128)(2,1)} %copy-done.11, ...), custom_call_target="tpu_custom_call" | custom-call | bytes 8388608 | tf_op jit(solution)/shard_map/pallas_call | solution.py:419
  190.8 13.7 %all-to-all-done.1.parts_ref = bf16[32,24,448]{2,1,0:T(8,128)(2,1)} async-done(((bf16[32,24,448]{2,1,0:T(8,128)(2,1)}), bf16[32,24,448]{2,1,0:T(8,128)(2,1)}, u32[]{:S(2)}, u32[]{:S(2)}) %all-to-all-start.1) | async-done | bytes 688160 | tf_op jit(solution)/shard_map/all_to_all | solution.py:952
  212.4 4.5 %collective-permute-done.36.rest_10_ = bf16[24,4480]{1,0:T(8,128)(2,1)S(1)} collective-permute-done((bf16[24,4480]{1,0:T(8,128)(2,1)}, bf16[24,4480]{1,0:T(8,128)(2,1)S(1)}, u32[]{:S(2)}, u32[]{:S(2)}) %collective-permute-start.36) | collective-permute-done | bytes 215072 | tf_op jit(solution)/shard_map/ppermute | solution.py:251
  218.9 5.8 %collective-permute-done.34.rest_9_ = bf16[24,4480]{1,0:T(8,128)(2,1)S(1)} collective-permute-done((bf16[24,4480]{1,0:T(8,128)(2,1)}, bf16[24,4480]{1,0:T(8,128)(2,1)S(1)}, u32[]{:S(2)}, u32[]{:S(2)}) %collective-permute-start.34) | collective-permute-done | bytes 215072 | tf_op jit(solution)/shard_map/ppermute | solution.py:251
  228.8 4.2 %collective-permute-done.40.rest_13_ = bf16[24,4480]{1,0:T(8,128)(2,1)S(1)} collective-permute-done((bf16[24,4480]{1,0:T(8,128)(2,1)S(1)}, bf16[24,4480]{1,0:T(8,128)(2,1)S(1)}, u32[]{:S(2)}, u32[]{:S(2)}) %collective-permute-start.40) | collective-permute-done | bytes 215072 | tf_op jit(solution)/shard_map/ppermute | solution.py:272
  237.7 12.0 %shard_map.222 = f32[48,128]{1,0:T(8,128)} custom-call(s32[12]{0:T(128)} %get-tuple-element.31.numbers_ref, s32[5,24,8]{2,1,0:T(8,128)} %get-tuple-element.32.rest_0_, s32[5,24,8]{2,1,0:T(8,128)} %get-tuple-element.33.rest_1_, s32[5,24,8]{2,1,0:T(8,128)} %get-tuple-element.34.rest_2_, bf16[24,4480]{1,0:T(8,128)(2,1)} %copy-done.20, ...), custom_call_target="tpu_custom_call" | custom-call | flops 3758096384 | bytes 14680064 | tf_op jit(solution)/shard_map/pallas_call | solution.py:559
  249.7 4.2 %collective-permute-start.44 = (f32[48,128]{1,0:T(8,128)}, f32[48,128]{1,0:T(8,128)S(1)}, u32[]{:S(2)}, u32[]{:S(2)}) collective-permute-start(f32[48,128]{1,0:T(8,128)} %shard_map.222), channel_id=1, source_target_pairs={{0,4},{4,8},{8,12},{12,0},{1,5},{5,9},{9,13},{13,1},{2,6},{6,10},{... | collective-permute-start | bytes 73736 | tf_op jit(solution)/shard_map/ppermute | solution.py:251
  260.0 8.7 %all-gather = f32[384,128]{1,0:T(8,128)S(1)} all-gather(f32[48,128]{1,0:T(8,128)S(1)} %add_add_fusion.1), channel_id=2, replica_groups=mesh['kv'=2,'seq'=4,'vocab'=4] {'kv','vocab'}, dimensions={0}, use_global_device_ids=true | all-gather | bytes 221184 | tf_op jit(solution)/shard_map/all_gather | solution.py:961
  (245 shorter events, 113.5 us)
Async XLA Ops:
  15.1 8.9 %collective-permute-start.2 = (bf16[48,1152]{1,0:T(8,128)(2,1)S(1)}, bf16[48,1152]{1,0:T(8,128)(2,1)S(1)}, u32[]{:S(2)}, u32[]{:S(2)}) collective-permute-start(bf16[48,1152]{1,0:T(8,128)(2,1)S(1)} %get-tuple-element.61), channel_id=1, source_target_pairs={{0,8},{4,12},{8,0},{12,4},{1,9},{5,13},{9,1},{13,5},{2,10},{6,14},... | collective-permute-start | bytes 331784 | tf_op jit(solution)/shard_map/ppermute | solution.py:243
  24.8 8.6 %collective-permute-start.6 = (bf16[96,256]{1,0:T(8,128)(2,1)S(1)}, bf16[96,256]{1,0:T(8,128)(2,1)S(1)}, u32[]{:S(2)}, u32[]{:S(2)}) collective-permute-start(bf16[96,256]{1,0:T(8,128)(2,1)S(1)} %pad_maximum_fusion.1), channel_id=1, source_target_pairs={{0,4},{4,8},{8,12},{12,0},{1,5},{5,9},{9,13},{13,1},{2,6},{6,10},{... | collective-permute-start | bytes 147464 | tf_op jit(solution)/shard_map/ppermute | solution.py:251
  80.0 44.4 %collective-permute-start.20 = (bf16[256,3584]{1,0:T(8,128)(2,1)}, bf16[256,3584]{1,0:T(8,128)(2,1)}, u32[]{:S(2)}, u32[]{:S(2)}) collective-permute-start(bf16[256,3584]{1,0:T(8,128)(2,1)} %get-tuple-element.27), channel_id=1, source_target_pairs={{0,16},{16,0},{1,17},{17,1},{2,18},{18,2},{3,19},{19,3},{4,20},{20... | collective-permute-start | bytes 5505032 | tf_op jit(solution)/shard_map/ppermute | solution.py:272
  80.6 43.8 %collective-permute-start.21 = (bf16[256,3584]{1,0:T(8,128)(2,1)}, bf16[256,3584]{1,0:T(8,128)(2,1)}, u32[]{:S(2)}, u32[]{:S(2)}) collective-permute-start(bf16[256,3584]{1,0:T(8,128)(2,1)} %get-tuple-element.28), channel_id=1, source_target_pairs={{0,2},{1,3},{2,0},{3,1},{4,6},{5,7},{6,4},{7,5},{8,10},{9,11},{10,... | collective-permute-start | bytes 5505032 | tf_op jit(solution)/shard_map/ppermute | solution.py:272
  88.5 21.2 %collective-permute-start.17 = (bf16[2,48,1792]{2,1,0:T(8,128)(2,1)}, bf16[2,48,1792]{2,1,0:T(8,128)(2,1)}, u32[]{:S(2)}, u32[]{:S(2)}) collective-permute-start(bf16[2,48,1792]{2,1,0:T(8,128)(2,1)} %get-tuple-element.57), channel_id=1, source_target_pairs={{0,4},{4,8},{8,12},{12,0},{1,5},{5,9},{9,13},{13,1},{2,6},{6,10},{... | collective-permute-start | bytes 1032200 | tf_op jit(solution)/shard_map/ppermute | solution.py:243
  88.5 21.2 %collective-permute-start.19 = (bf16[2,48,1792]{2,1,0:T(8,128)(2,1)}, bf16[2,48,1792]{2,1,0:T(8,128)(2,1)}, u32[]{:S(2)}, u32[]{:S(2)}) collective-permute-start(bf16[2,48,1792]{2,1,0:T(8,128)(2,1)} %get-tuple-element.58), channel_id=1, source_target_pairs={{0,12},{4,0},{8,4},{12,8},{1,13},{5,1},{9,5},{13,9},{2,14},{6,2},{... | collective-permute-start | bytes 1032200 | tf_op jit(solution)/shard_map/ppermute | solution.py:243
  92.3 29.9 %collective-permute-start.18 = (bf16[2,48,1792]{2,1,0:T(8,128)(2,1)S(1)}, bf16[2,48,1792]{2,1,0:T(8,128)(2,1)}, u32[]{:S(2)}, u32[]{:S(2)}) collective-permute-start(bf16[2,48,1792]{2,1,0:T(8,128)(2,1)S(1)} %get-tuple-element.59), channel_id=1, source_target_pairs={{0,8},{4,12},{8,0},{12,4},{1,9},{5,13},{9,1},{13,5},{2,10},{6,14},... | collective-permute-start | bytes 1032200 | tf_op jit(solution)/shard_map/ppermute | solution.py:243
  109.7 96.8 %collective-permute-start.30 = (bf16[512,3584]{1,0:T(8,128)(2,1)}, bf16[512,3584]{1,0:T(8,128)(2,1)}, u32[]{:S(2)}, u32[]{:S(2)}) collective-permute-start(bf16[512,3584]{1,0:T(8,128)(2,1)} %rest_15_.1), channel_id=1, source_target_pairs={{0,1},{1,0},{2,3},{3,2},{4,5},{5,4},{6,7},{7,6},{8,9},{9,8},{10,11... | collective-permute-start | bytes 11010056 | tf_op jit(solution)/shard_map/ppermute | solution.py:272
  124.5 16.2 %collective-permute-start.24 = (bf16[48,1792]{1,0:T(8,128)(2,1)}, bf16[48,1792]{1,0:T(8,128)(2,1)S(1)}, u32[]{:S(2)}, u32[]{:S(2)}) collective-permute-start(bf16[48,1792]{1,0:T(8,128)(2,1)} %shard_map.216), channel_id=1, source_target_pairs={{0,4},{4,8},{8,12},{12,0},{1,5},{5,9},{9,13},{13,1},{2,6},{6,10},{... | collective-permute-start | bytes 516104 | tf_op jit(solution)/shard_map/ppermute | solution.py:251
  124.5 15.5 %collective-permute-start.23 = (bf16[48,1792]{1,0:T(8,128)(2,1)}, bf16[48,1792]{1,0:T(8,128)(2,1)S(1)}, u32[]{:S(2)}, u32[]{:S(2)}) collective-permute-start(bf16[48,1792]{1,0:T(8,128)(2,1)} %shard_map.216), channel_id=1, source_target_pairs={{0,8},{4,12},{8,0},{12,4},{1,9},{5,13},{9,1},{13,5},{2,10},{6,14},... | collective-permute-start | bytes 516104 | tf_op jit(solution)/shard_map/ppermute | solution.py:251
  126.5 10.9 %collective-permute-start.22 = (bf16[48,1792]{1,0:T(8,128)(2,1)}, bf16[48,1792]{1,0:T(8,128)(2,1)S(1)}, u32[]{:S(2)}, u32[]{:S(2)}) collective-permute-start(bf16[48,1792]{1,0:T(8,128)(2,1)} %shard_map.216), channel_id=1, source_target_pairs={{0,12},{4,0},{8,4},{12,8},{1,13},{5,1},{9,5},{13,9},{2,14},{6,2},{... | collective-permute-start | bytes 516104 | tf_op jit(solution)/shard_map/ppermute | solution.py:251
  177.2 29.2 %collective-permute-start.28 = (bf16[256,3584]{1,0:T(8,128)(2,1)}, bf16[256,3584]{1,0:T(8,128)(2,1)}, u32[]{:S(2)}, u32[]{:S(2)}) collective-permute-start(bf16[256,3584]{1,0:T(8,128)(2,1)} %get-tuple-element.35.rest_17_), channel_id=1, source_target_pairs={{0,1},{1,0},{2,3},{3,2},{4,5},{5,4},{6,7},{7,6},{8,9},{9,8},{10,11... | collective-permute-start | bytes 5505032 | tf_op jit(solution)/shard_map/ppermute | solution.py:272
  177.6 28.9 %collective-permute-start.29 = (bf16[256,3584]{1,0:T(8,128)(2,1)}, bf16[256,3584]{1,0:T(8,128)(2,1)}, u32[]{:S(2)}, u32[]{:S(2)}) collective-permute-start(bf16[256,3584]{1,0:T(8,128)(2,1)} %get-tuple-element.36.rest_19_), channel_id=1, source_target_pairs={{0,1},{1,0},{2,3},{3,2},{4,5},{5,4},{6,7},{7,6},{8,9},{9,8},{10,11... | collective-permute-start | bytes 5505032 | tf_op jit(solution)/shard_map/ppermute | solution.py:272
  177.7 26.7 %all-to-all-start.1 = ((bf16[32,24,448]{2,1,0:T(8,128)(2,1)}), bf16[32,24,448]{2,1,0:T(8,128)(2,1)}, u32[]{:S(2)}, u32[]{:S(2)}) async-start(bf16[32,24,448]{2,1,0:T(8,128)(2,1)} %bitcast.162), calls=%async_computation.1 | async-start | bytes 1572864 | tf_op jit(solution)/shard_map/all_to_all | solution.py:952
  206.5 10.4 %collective-permute-start.36 = (bf16[24,4480]{1,0:T(8,128)(2,1)}, bf16[24,4480]{1,0:T(8,128)(2,1)S(1)}, u32[]{:S(2)}, u32[]{:S(2)}) collective-permute-start(bf16[24,4480]{1,0:T(8,128)(2,1)} %shard_map.221.rest_7_), channel_id=1, source_target_pairs={{0,4},{4,8},{8,12},{12,0},{1,5},{5,9},{9,13},{13,1},{2,6},{6,10},{... | collective-permute-start | bytes 645128 | tf_op jit(solution)/shard_map/ppermute | solution.py:251
  206.8 11.1 %collective-permute-start.38 = (bf16[24,4480]{1,0:T(8,128)(2,1)}, bf16[24,4480]{1,0:T(8,128)(2,1)S(1)}, u32[]{:S(2)}, u32[]{:S(2)}) collective-permute-start(bf16[24,4480]{1,0:T(8,128)(2,1)} %shard_map.221.rest_7_), channel_id=1, source_target_pairs={{0,16},{16,0},{1,17},{17,1},{2,18},{18,2},{3,19},{19,3},{4,20},{20... | collective-permute-start | bytes 645128 | tf_op jit(solution)/shard_map/ppermute | solution.py:272
  208.3 16.4 %collective-permute-start.34 = (bf16[24,4480]{1,0:T(8,128)(2,1)}, bf16[24,4480]{1,0:T(8,128)(2,1)S(1)}, u32[]{:S(2)}, u32[]{:S(2)}) collective-permute-start(bf16[24,4480]{1,0:T(8,128)(2,1)} %shard_map.221.rest_7_), channel_id=1, source_target_pairs={{0,8},{4,12},{8,0},{12,4},{1,9},{5,13},{9,1},{13,5},{2,10},{6,14},... | collective-permute-start | bytes 645128 | tf_op jit(solution)/shard_map/ppermute | solution.py:251
  209.4 16.2 %collective-permute-start.32 = (bf16[24,4480]{1,0:T(8,128)(2,1)}, bf16[24,4480]{1,0:T(8,128)(2,1)S(1)}, u32[]{:S(2)}, u32[]{:S(2)}) collective-permute-start(bf16[24,4480]{1,0:T(8,128)(2,1)} %shard_map.221.rest_7_), channel_id=1, source_target_pairs={{0,12},{4,0},{8,4},{12,8},{1,13},{5,1},{9,5},{13,9},{2,14},{6,2},{... | collective-permute-start | bytes 645128 | tf_op jit(solution)/shard_map/ppermute | solution.py:251
  211.4 14.5 %collective-permute-start.31 = (bf16[24,4480]{1,0:T(8,128)(2,1)}, bf16[24,4480]{1,0:T(8,128)(2,1)S(1)}, u32[]{:S(2)}, u32[]{:S(2)}) collective-permute-start(bf16[24,4480]{1,0:T(8,128)(2,1)} %shard_map.221.rest_7_), channel_id=1, source_target_pairs={{0,2},{1,3},{2,0},{3,1},{4,6},{5,7},{6,4},{7,5},{8,10},{9,11},{10,... | collective-permute-start | bytes 645128 | tf_op jit(solution)/shard_map/ppermute | solution.py:272
  216.8 10.7 %collective-permute-start.41 = (bf16[24,4480]{1,0:T(8,128)(2,1)S(1)}, bf16[24,4480]{1,0:T(8,128)(2,1)S(1)}, u32[]{:S(2)}, u32[]{:S(2)}) collective-permute-start(bf16[24,4480]{1,0:T(8,128)(2,1)S(1)} %collective-permute-done.36.rest_10_), channel_id=1, source_target_pairs={{0,16},{16,0},{1,17},{17,1},{2,18},{18,2},{3,19},{19,3},{4,20},{20... | collective-permute-start | bytes 645128 | tf_op jit(solution)/shard_map/ppermute | solution.py:272
  217.9 10.9 %collective-permute-start.37 = (bf16[24,4480]{1,0:T(8,128)(2,1)S(1)}, bf16[24,4480]{1,0:T(8,128)(2,1)S(1)}, u32[]{:S(2)}, u32[]{:S(2)}) collective-permute-start(bf16[24,4480]{1,0:T(8,128)(2,1)S(1)} %collective-permute-done.36.rest_10_), channel_id=1, source_target_pairs={{0,2},{1,3},{2,0},{3,1},{4,6},{5,7},{6,4},{7,5},{8,10},{9,11},{10,... | collective-permute-start | bytes 645128 | tf_op jit(solution)/shard_map/ppermute | solution.py:272
  224.7 8.2 %collective-permute-start.40 = (bf16[24,4480]{1,0:T(8,128)(2,1)S(1)}, bf16[24,4480]{1,0:T(8,128)(2,1)S(1)}, u32[]{:S(2)}, u32[]{:S(2)}) collective-permute-start(bf16[24,4480]{1,0:T(8,128)(2,1)S(1)} %collective-permute-done.34.rest_9_), channel_id=1, source_target_pairs={{0,16},{16,0},{1,17},{17,1},{2,18},{18,2},{3,19},{19,3},{4,20},{20... | collective-permute-start | bytes 645128 | tf_op jit(solution)/shard_map/ppermute | solution.py:272
  225.9 10.1 %collective-permute-start.39 = (bf16[24,4480]{1,0:T(8,128)(2,1)S(1)}, bf16[24,4480]{1,0:T(8,128)(2,1)S(1)}, u32[]{:S(2)}, u32[]{:S(2)}) collective-permute-start(bf16[24,4480]{1,0:T(8,128)(2,1)S(1)} %collective-permute-done.32.rest_8_), channel_id=1, source_target_pairs={{0,16},{16,0},{1,17},{17,1},{2,18},{18,2},{3,19},{19,3},{4,20},{20... | collective-permute-start | bytes 645128 | tf_op jit(solution)/shard_map/ppermute | solution.py:272
  227.5 9.5 %collective-permute-start.33 = (bf16[24,4480]{1,0:T(8,128)(2,1)S(1)}, bf16[24,4480]{1,0:T(8,128)(2,1)S(1)}, u32[]{:S(2)}, u32[]{:S(2)}) collective-permute-start(bf16[24,4480]{1,0:T(8,128)(2,1)S(1)} %collective-permute-done.32.rest_8_), channel_id=1, source_target_pairs={{0,2},{1,3},{2,0},{3,1},{4,6},{5,7},{6,4},{7,5},{8,10},{9,11},{10,... | collective-permute-start | bytes 645128 | tf_op jit(solution)/shard_map/ppermute | solution.py:272
  (53 other events, 521.1 us)

commit v7 on v6

--- a/solution.py
+++ b/solution.py
@@ -592,7 +592,7 @@
             for tenant in range(tenants):
                 total = 0.0
                 for seq in range(seq_count):
-                    block = parts_ref[(kv * seq_count + seq) * tenants + tenant]
+                    block = parts_ref[(seq * kv_count + kv) * tenants + tenant]
                     total = total + block.astype(jnp.float32)
                 pair.append(total / (1.0 + jnp.exp(-total)))
                 if len(pair) == 2:
@@ -925,8 +925,7 @@
         "td,ndc->ntc", gathered, draft_weight, preferred_element_type=f32
     )
     lifted = lifted + draft_bias[:, None, :] * (1.0 / seq_count)
-    lifted = lifted.astype(bf16).reshape(seq_count, kv_count, tenants, tok_block, -1)
-    lifted = lifted.transpose(1, 0, 2, 3, 4).reshape(seq_count * groups, tok_block, -1)
+    lifted = lifted.astype(bf16).reshape(seq_count * groups, tok_block, -1)
     places = [("vocab", 2), (None, 0), ("kv", 1)]
 
     def around(values):
@@ -949,7 +948,7 @@
         accept_count,
         lifted,
     )
-    everywhere = lax.all_to_all(lifted, ("kv", "seq", "vocab"), 0, 0, tiled=True)
+    everywhere = lax.all_to_all(lifted, ("seq", "kv", "vocab"), 0, 0, tiled=True)
     branch = activate_draft(everywhere, normed, kv_count, seq_count)
     (branch,) = hold([branch], core_first, core_second, core_rows, value_flag)
     heads = collect(branch)

time: 272 us -> 272 us (level)
  Pallas kernels: 37.2 us -> 31.5 us
  waiting for transfers between devices: 76.8 us -> 80.5 us
    pallas_call x2, Pallas kernels: 15.8 us -> 10.1 us  [update_cache(): pl.pallas_call(kernel, out_shape=(jax.ShapeDtypeStruct(cache.shape, cache...]
    ppermute x9, waiting for transfers between devices: 23 us -> 25.9 us  [send_ahead(): lax.ppermute(pick(j), 'seq', [(i, (i + j) % count) for i in range(count)])]
  transfers between devices with their start and end apart: 46 -> 46, of which waited for: 26 -> 26; matrix products, arithmetic and copies ran while one was open for 11% -> 11% of each run, Pallas kernels for 8% -> 6%
where the time goes in v7:
time: 272 us; the launch traced here: 271 us
  waiting for transfers between devices  80.5 us (30%)
  starting transfers between devices  70.2 us (26%)
  blocking collectives  39.5 us (15%)
  Pallas kernels  31.5 us (12%)
  local copies, waits for them, and re-layouts  18.9 us (7%)
  matrix products  15.2 us (6%)
  other arithmetic  12.4 us (5%)
    ppermute x21, starting transfers between devices, collect(): lax.ppermute(block, 'seq', [(i, (i - j) % count) for i in range(count)])  35.3 us
    ppermute x21, waiting for transfers between devices, collect(): lax.ppermute(block, 'seq', [(i, (i - j) % count) for i in range(count)])  29.7 us
    ppermute x9, waiting for transfers between devices, send_ahead(): lax.ppermute(pick(j), 'seq', [(i, (i + j) % count) for i in range(count)])  25.9 us
    ppermute x15, starting transfers between devices, swap(): return lax.ppermute(values, axis, [(i, i ^ bit) for i in range(count)])  16.6 us
    all_to_all x1, waiting for transfers between devices, local(): lax.all_to_all(lifted, ('seq', 'kv', 'vocab'), 0, 0, tiled=True)  15.6 us
    ppermute x9, starting transfers between devices, send_ahead(): lax.ppermute(pick(j), 'seq', [(i, (i + j) % count) for i in range(count)])  13 us
    pallas_call x1, Pallas kernels, score_vocabulary(): pl.pallas_call(kernel, out_shape=jax.ShapeDtypeStruct((16 * groups, lanes...  12 us
    all_to_all x1, blocking collectives, local(): ffn_out = add_up(list(lax.all_to_all(ffn_out, plane, 0, 0)))  11 us
  transfers between devices with their start and end apart: 46, of which 26 were waited for; matrix products, arithmetic and copies ran while one was open for 11% of the time, Pallas kernels for 6%

profile of v7, /device:TPU:0, one launch (start us, length us, event | category | flops | bytes accessed | tf_op | source)
XLA Modules:
  0.0 270.8 jit_solution(18094736047555955798)
XLA Ops:
  0.6 3.0 %collective-permute-start = (bf16[24,896]{1,0:T(8,128)(2,1)}, bf16[24,896]{1,0:T(8,128)(2,1)S(1)}, u32[]{:S(2)}, u32[]{:S(2)}) collective-permute-start(bf16[24,896]{1,0:T(8,128)(2,1)} %bitcast.174), channel_id=1, source_target_pairs={{0,16},{16,0},{1,17},{17,1},{2,18},{18,2},{3,19},{19,3},{4,20},{20... | collective-permute-start | bytes 129032 | tf_op jit(solution)/shard_map/ppermute | solution.py:272
  7.0 3.1 %copy-done.1 = bf16[896,4,1024]{2,1,0:T(4,128)(2,1)S(1)} copy-done((bf16[896,4,1024]{2,1,0:T(4,128)(2,1)S(1)}, bf16[896,4,1024]{2,1,0:T(4,128)(2,1)}, u32[]{:S(2)}) %copy-start.1) | copy-done | bytes 7340056
  21.0 2.9 %collective-permute-done.2 = bf16[48,1152]{1,0:T(8,128)(2,1)S(1)} collective-permute-done((bf16[48,1152]{1,0:T(8,128)(2,1)S(1)}, bf16[48,1152]{1,0:T(8,128)(2,1)S(1)}, u32[]{:S(2)}, u32[]{:S(2)}) %collective-permute-start.2) | collective-permute-done | bytes 110624 | tf_op jit(solution)/shard_map/ppermute | solution.py:243
  40.8 3.6 %collective-permute-done.8.rest_1_ = bf16[112,256]{1,0:T(8,128)(2,1)S(1)} collective-permute-done((bf16[112,256]{1,0:T(8,128)(2,1)S(1)}, bf16[112,256]{1,0:T(8,128)(2,1)S(1)}, u32[]{:S(2)}, u32[]{:S(2)}) %collective-permute-start.8) | collective-permute-done | bytes 57376 | tf_op jit(solution)/shard_map/ppermute | solution.py:243
  54.8 3.4 %shard_map.212 = (bf16[256,3584]{1,0:T(8,128)(2,1)}, bf16[256,3584]{1,0:T(8,128)(2,1)}) custom-call(bf16[512,3584]{1,0:T(8,128)(2,1)} %rest_15_.1, bf16[24,896]{1,0:T(8,128)(2,1)} %copy-done.3), custom_call_target="tpu_custom_call" | custom-call | bytes 7340032 | tf_op jit(solution)/shard_map/pallas_call | solution.py:347
  69.5 10.5 %all_gather.12.refs_2_ = bf16[192,896]{1,0:T(8,128)(2,1)} all-gather(bf16[24,896]{1,0:T(8,128)(2,1)S(1)} %get-tuple-element.51), channel_id=1, replica_groups=mesh['kv'=2,'seq'=4,'vocab'=4] {'kv','vocab'}, dimensions={0}, use_global_device_ids=true | all-gather | bytes 387072 | tf_op jit(solution)/shard_map/all_gather | solution.py:859
  82.0 4.4 %fusion.8 = bf16[192,2,1792]{2,0,1:T(8,128)(2,1)S(1)} fusion(bf16[896,2,1792]{2,1,0:T(2,128)(2,1)} %param.32, bf16[192,896]{1,0:T(8,128)(2,1)S(1)} %copy-done.9), kind=kOutput, calls=%fused_computation.7 | convolution fusion | flops 1233813504 | bytes 8142848 | tf_op jit(solution)/shard_map/td,dcf->ctf/dot_general | solution.py:862
  88.5 3.8 %collective-permute-start.19 = (bf16[2,48,1792]{2,1,0:T(8,128)(2,1)}, bf16[2,48,1792]{2,1,0:T(8,128)(2,1)}, u32[]{:S(2)}, u32[]{:S(2)}) collective-permute-start(bf16[2,48,1792]{2,1,0:T(8,128)(2,1)} %get-tuple-element.58), channel_id=1, source_target_pairs={{0,12},{4,0},{8,4},{12,8},{1,13},{5,1},{9,5},{13,9},{2,14},{6,2},{... | collective-permute-start | bytes 1032200 | tf_op jit(solution)/shard_map/ppermute | solution.py:243
  101.2 5.1 %shard_map.214 = (bf16[2048,4,256]{2,1,0:T(4,128)(2,1)}, f32[8,128]{1,0:T(8,128)}) custom-call(s32[2]{0:T(128)} %pad_add_fusion.1.numbers_ref, bf16[2048,4,256]{2,1,0:T(4,128)(2,1)} %bitcast.161, bf16[4,112,256]{2,1,0:T(8,128)(2,1)} %copy-done.6, bf16[112,256]{1,0:T(8,128)(2,1)} %copy-done.12, bf16[112,256]{1,0:T(8,128)(2,1)} %copy-done.11, ...), custom_call_target="tpu_custom_call" | custom-call | bytes 8388608 | tf_op jit(solution)/shard_map/pallas_call | solution.py:419
  106.8 15.4 %collective-permute-done.18 = bf16[2,48,1792]{2,1,0:T(8,128)(2,1)} collective-permute-done((bf16[2,48,1792]{2,1,0:T(8,128)(2,1)S(1)}, bf16[2,48,1792]{2,1,0:T(8,128)(2,1)}, u32[]{:S(2)}, u32[]{:S(2)}) %collective-permute-start.18) | collective-permute-done | bytes 344096 | tf_op jit(solution)/shard_map/ppermute | solution.py:243
  130.0 7.5 %collective-permute-done.22 = bf16[48,1792]{1,0:T(8,128)(2,1)S(1)} collective-permute-done((bf16[48,1792]{1,0:T(8,128)(2,1)}, bf16[48,1792]{1,0:T(8,128)(2,1)S(1)}, u32[]{:S(2)}, u32[]{:S(2)}) %collective-permute-start.22) | collective-permute-done | bytes 172064 | tf_op jit(solution)/shard_map/ppermute | solution.py:251
  142.1 11.0 %all_to_all.10 = bf16[8,24,896]{2,1,0:T(8,128)(2,1)S(1)} all-to-all(bf16[8,24,896]{2,1,0:T(8,128)(2,1)} %get-tuple-element.29), channel_id=1, replica_groups=mesh['kv'=2,'seq'=4,'vocab'=4] {'kv','vocab'}, dimensions={0} | all-to-all | bytes 688128 | tf_op jit(solution)/shard_map/all_to_all | solution.py:919
  154.5 3.1 %collective-permute-start.26 = (f32[24,128]{1,0:T(8,128)S(1)}, f32[24,128]{1,0:T(8,128)S(1)}, u32[]{:S(2)}, u32[]{:S(2)}) collective-permute-start(f32[24,128]{1,0:T(8,128)S(1)} %pad_maximum_fusion.7), channel_id=1, source_target_pairs={{0,8},{4,12},{8,0},{12,4},{1,9},{5,13},{9,1},{13,5},{2,10},{6,14},... | collective-permute-start | bytes 36872 | tf_op jit(solution)/shard_map/ppermute | solution.py:251
  164.4 8.8 %all_gather.13 = bf16[192,896]{1,0:T(8,128)(2,1)S(1)} all-gather(bf16[24,896]{1,0:T(8,128)(2,1)S(1)} %multiply_convert_fusion.normed_ref), channel_id=1, replica_groups=mesh['kv'=2,'seq'=4,'vocab'=4] {'kv','vocab'}, dimensions={0}, use_global_device_ids=true | all-gather | bytes 387072 | tf_op jit(solution)/shard_map/all_gather | solution.py:923
  173.2 3.9 %add_convert_fusion = bf16[192,4,448]{2,0,1:T(8,128)(2,1)} fusion(bf16[4,896,448]{1,2,0:T(8,128)(2,1)} %param.34, f32[4,448]{1,0:T(4,128)S(1)} %broadcast_multiply_fusion, bf16[192,896]{1,0:T(8,128)(2,1)S(1)} %all_gather.13), kind=kOutput, calls=%fused_computation.8 | convolution fusion | flops 617250816 | bytes 4250624 | tf_op jit(solution)/shard_map/td,ndc->ntc/dot_general | solution.py:924
  177.6 5.2 %all-to-all-start.1 = ((bf16[32,24,448]{2,1,0:T(8,128)(2,1)}), bf16[32,24,448]{2,1,0:T(8,128)(2,1)}, u32[]{:S(2)}, u32[]{:S(2)}) async-start(bf16[32,24,448]{2,1,0:T(8,128)(2,1)} %bitcast.159), calls=%async_computation.1 | async-start | bytes 1572864 | tf_op jit(solution)/shard_map/all_to_all | solution.py:951
  182.8 5.0 %shard_map.218 = (bf16[2048,4,256]{2,1,0:T(4,128)(2,1)}, f32[8,128]{1,0:T(8,128)}) custom-call(s32[2]{0:T(128)} %pad_add_fusion.1.numbers_ref, bf16[2048,4,256]{2,1,0:T(4,128)(2,1)} %bitcast.163, bf16[4,112,256]{2,1,0:T(8,128)(2,1)} %copy-done.6, bf16[112,256]{1,0:T(8,128)(2,1)} %copy-done.12, bf16[112,256]{1,0:T(8,128)(2,1)} %copy-done.11, ...), custom_call_target="tpu_custom_call" | custom-call | bytes 8388608 | tf_op jit(solution)/shard_map/pallas_call | solution.py:419
  187.8 15.6 %all-to-all-done.1.parts_ref = bf16[32,24,448]{2,1,0:T(8,128)(2,1)} async-done(((bf16[32,24,448]{2,1,0:T(8,128)(2,1)}), bf16[32,24,448]{2,1,0:T(8,128)(2,1)}, u32[]{:S(2)}, u32[]{:S(2)}) %all-to-all-start.1) | async-done | bytes 688160 | tf_op jit(solution)/shard_map/all_to_all | solution.py:951
  212.3 3.6 %collective-permute-done.36.rest_10_ = bf16[24,4480]{1,0:T(8,128)(2,1)S(1)} collective-permute-done((bf16[24,4480]{1,0:T(8,128)(2,1)}, bf16[24,4480]{1,0:T(8,128)(2,1)S(1)}, u32[]{:S(2)}, u32[]{:S(2)}) %collective-permute-start.36) | collective-permute-done | bytes 215072 | tf_op jit(solution)/shard_map/ppermute | solution.py:251
  218.9 5.0 %collective-permute-done.34.rest_9_ = bf16[24,4480]{1,0:T(8,128)(2,1)S(1)} collective-permute-done((bf16[24,4480]{1,0:T(8,128)(2,1)}, bf16[24,4480]{1,0:T(8,128)(2,1)S(1)}, u32[]{:S(2)}, u32[]{:S(2)}) %collective-permute-start.34) | collective-permute-done | bytes 215072 | tf_op jit(solution)/shard_map/ppermute | solution.py:251
  228.0 4.1 %collective-permute-done.40.rest_13_ = bf16[24,4480]{1,0:T(8,128)(2,1)S(1)} collective-permute-done((bf16[24,4480]{1,0:T(8,128)(2,1)S(1)}, bf16[24,4480]{1,0:T(8,128)(2,1)S(1)}, u32[]{:S(2)}, u32[]{:S(2)}) %collective-permute-start.40) | collective-permute-done | bytes 215072 | tf_op jit(solution)/shard_map/ppermute | solution.py:272
  237.6 12.0 %shard_map.222 = f32[48,128]{1,0:T(8,128)} custom-call(s32[12]{0:T(128)} %get-tuple-element.31.numbers_ref, s32[5,24,8]{2,1,0:T(8,128)} %get-tuple-element.32.rest_0_, s32[5,24,8]{2,1,0:T(8,128)} %get-tuple-element.33.rest_1_, s32[5,24,8]{2,1,0:T(8,128)} %get-tuple-element.34.rest_2_, bf16[24,4480]{1,0:T(8,128)(2,1)} %copy-done.20, ...), custom_call_target="tpu_custom_call" | custom-call | flops 3758096384 | bytes 14680064 | tf_op jit(solution)/shard_map/pallas_call | solution.py:559
  249.6 3.9 %collective-permute-start.44 = (f32[48,128]{1,0:T(8,128)}, f32[48,128]{1,0:T(8,128)S(1)}, u32[]{:S(2)}, u32[]{:S(2)}) collective-permute-start(f32[48,128]{1,0:T(8,128)} %shard_map.222), channel_id=1, source_target_pairs={{0,4},{4,8},{8,12},{12,0},{1,5},{5,9},{9,13},{13,1},{2,6},{6,10},{... | collective-permute-start | bytes 73736 | tf_op jit(solution)/shard_map/ppermute | solution.py:251
  259.5 9.3 %all-gather = f32[384,128]{1,0:T(8,128)S(1)} all-gather(f32[48,128]{1,0:T(8,128)S(1)} %add_add_fusion.1), channel_id=2, replica_groups=mesh['kv'=2,'seq'=4,'vocab'=4] {'kv','vocab'}, dimensions={0}, use_global_device_ids=true | all-gather | bytes 221184 | tf_op jit(solution)/shard_map/all_gather | solution.py:960
  (244 shorter events, 114.9 us)
Async XLA Ops:
  15.1 8.9 %collective-permute-start.2 = (bf16[48,1152]{1,0:T(8,128)(2,1)S(1)}, bf16[48,1152]{1,0:T(8,128)(2,1)S(1)}, u32[]{:S(2)}, u32[]{:S(2)}) collective-permute-start(bf16[48,1152]{1,0:T(8,128)(2,1)S(1)} %get-tuple-element.61), channel_id=1, source_target_pairs={{0,8},{4,12},{8,0},{12,4},{1,9},{5,13},{9,1},{13,5},{2,10},{6,14},... | collective-permute-start | bytes 331784 | tf_op jit(solution)/shard_map/ppermute | solution.py:243
  24.8 8.6 %collective-permute-start.6 = (bf16[96,256]{1,0:T(8,128)(2,1)S(1)}, bf16[96,256]{1,0:T(8,128)(2,1)S(1)}, u32[]{:S(2)}, u32[]{:S(2)}) collective-permute-start(bf16[96,256]{1,0:T(8,128)(2,1)S(1)} %pad_maximum_fusion.1), channel_id=1, source_target_pairs={{0,4},{4,8},{8,12},{12,0},{1,5},{5,9},{9,13},{13,1},{2,6},{6,10},{... | collective-permute-start | bytes 147464 | tf_op jit(solution)/shard_map/ppermute | solution.py:251
  80.0 44.4 %collective-permute-start.20 = (bf16[256,3584]{1,0:T(8,128)(2,1)}, bf16[256,3584]{1,0:T(8,128)(2,1)}, u32[]{:S(2)}, u32[]{:S(2)}) collective-permute-start(bf16[256,3584]{1,0:T(8,128)(2,1)} %get-tuple-element.27), channel_id=1, source_target_pairs={{0,16},{16,0},{1,17},{17,1},{2,18},{18,2},{3,19},{19,3},{4,20},{20... | collective-permute-start | bytes 5505032 | tf_op jit(solution)/shard_map/ppermute | solution.py:272
  80.6 43.8 %collective-permute-start.21 = (bf16[256,3584]{1,0:T(8,128)(2,1)}, bf16[256,3584]{1,0:T(8,128)(2,1)}, u32[]{:S(2)}, u32[]{:S(2)}) collective-permute-start(bf16[256,3584]{1,0:T(8,128)(2,1)} %get-tuple-element.28), channel_id=1, source_target_pairs={{0,2},{1,3},{2,0},{3,1},{4,6},{5,7},{6,4},{7,5},{8,10},{9,11},{10,... | collective-permute-start | bytes 5505032 | tf_op jit(solution)/shard_map/ppermute | solution.py:272
  88.5 18.3 %collective-permute-start.17 = (bf16[2,48,1792]{2,1,0:T(8,128)(2,1)}, bf16[2,48,1792]{2,1,0:T(8,128)(2,1)}, u32[]{:S(2)}, u32[]{:S(2)}) collective-permute-start(bf16[2,48,1792]{2,1,0:T(8,128)(2,1)} %get-tuple-element.57), channel_id=1, source_target_pairs={{0,4},{4,8},{8,12},{12,0},{1,5},{5,9},{9,13},{13,1},{2,6},{6,10},{... | collective-permute-start | bytes 1032200 | tf_op jit(solution)/shard_map/ppermute | solution.py:243
  88.5 18.3 %collective-permute-start.19 = (bf16[2,48,1792]{2,1,0:T(8,128)(2,1)}, bf16[2,48,1792]{2,1,0:T(8,128)(2,1)}, u32[]{:S(2)}, u32[]{:S(2)}) collective-permute-start(bf16[2,48,1792]{2,1,0:T(8,128)(2,1)} %get-tuple-element.58), channel_id=1, source_target_pairs={{0,12},{4,0},{8,4},{12,8},{1,13},{5,1},{9,5},{13,9},{2,14},{6,2},{... | collective-permute-start | bytes 1032200 | tf_op jit(solution)/shard_map/ppermute | solution.py:243
  92.3 29.9 %collective-permute-start.18 = (bf16[2,48,1792]{2,1,0:T(8,128)(2,1)S(1)}, bf16[2,48,1792]{2,1,0:T(8,128)(2,1)}, u32[]{:S(2)}, u32[]{:S(2)}) collective-permute-start(bf16[2,48,1792]{2,1,0:T(8,128)(2,1)S(1)} %get-tuple-element.59), channel_id=1, source_target_pairs={{0,8},{4,12},{8,0},{12,4},{1,9},{5,13},{9,1},{13,5},{2,10},{6,14},... | collective-permute-start | bytes 1032200 | tf_op jit(solution)/shard_map/ppermute | solution.py:243
  106.8 98.7 %collective-permute-start.30 = (bf16[512,3584]{1,0:T(8,128)(2,1)}, bf16[512,3584]{1,0:T(8,128)(2,1)}, u32[]{:S(2)}, u32[]{:S(2)}) collective-permute-start(bf16[512,3584]{1,0:T(8,128)(2,1)} %rest_15_.1), channel_id=1, source_target_pairs={{0,1},{1,0},{2,3},{3,2},{4,5},{5,4},{6,7},{7,6},{8,9},{9,8},{10,11... | collective-permute-start | bytes 11010056 | tf_op jit(solution)/shard_map/ppermute | solution.py:272
  124.5 16.2 %collective-permute-start.24 = (bf16[48,1792]{1,0:T(8,128)(2,1)}, bf16[48,1792]{1,0:T(8,128)(2,1)S(1)}, u32[]{:S(2)}, u32[]{:S(2)}) collective-permute-start(bf16[48,1792]{1,0:T(8,128)(2,1)} %shard_map.216), channel_id=1, source_target_pairs={{0,4},{4,8},{8,12},{12,0},{1,5},{5,9},{9,13},{13,1},{2,6},{6,10},{... | collective-permute-start | bytes 516104 | tf_op jit(solution)/shard_map/ppermute | solution.py:251
  124.5 15.5 %collective-permute-start.23 = (bf16[48,1792]{1,0:T(8,128)(2,1)}, bf16[48,1792]{1,0:T(8,128)(2,1)S(1)}, u32[]{:S(2)}, u32[]{:S(2)}) collective-permute-start(bf16[48,1792]{1,0:T(8,128)(2,1)} %shard_map.216), channel_id=1, source_target_pairs={{0,8},{4,12},{8,0},{12,4},{1,9},{5,13},{9,1},{13,5},{2,10},{6,14},... | collective-permute-start | bytes 516104 | tf_op jit(solution)/shard_map/ppermute | solution.py:251
  126.5 10.9 %collective-permute-start.22 = (bf16[48,1792]{1,0:T(8,128)(2,1)}, bf16[48,1792]{1,0:T(8,128)(2,1)S(1)}, u32[]{:S(2)}, u32[]{:S(2)}) collective-permute-start(bf16[48,1792]{1,0:T(8,128)(2,1)} %shard_map.216), channel_id=1, source_target_pairs={{0,12},{4,0},{8,4},{12,8},{1,13},{5,1},{9,5},{13,9},{2,14},{6,2},{... | collective-permute-start | bytes 516104 | tf_op jit(solution)/shard_map/ppermute | solution.py:251
  177.1 28.3 %collective-permute-start.28 = (bf16[256,3584]{1,0:T(8,128)(2,1)}, bf16[256,3584]{1,0:T(8,128)(2,1)}, u32[]{:S(2)}, u32[]{:S(2)}) collective-permute-start(bf16[256,3584]{1,0:T(8,128)(2,1)} %get-tuple-element.35.rest_17_), channel_id=1, source_target_pairs={{0,1},{1,0},{2,3},{3,2},{4,5},{5,4},{6,7},{7,6},{8,9},{9,8},{10,11... | collective-permute-start | bytes 5505032 | tf_op jit(solution)/shard_map/ppermute | solution.py:272
  177.5 28.0 %collective-permute-start.29 = (bf16[256,3584]{1,0:T(8,128)(2,1)}, bf16[256,3584]{1,0:T(8,128)(2,1)}, u32[]{:S(2)}, u32[]{:S(2)}) collective-permute-start(bf16[256,3584]{1,0:T(8,128)(2,1)} %get-tuple-element.36.rest_19_), channel_id=1, source_target_pairs={{0,1},{1,0},{2,3},{3,2},{4,5},{5,4},{6,7},{7,6},{8,9},{9,8},{10,11... | collective-permute-start | bytes 5505032 | tf_op jit(solution)/shard_map/ppermute | solution.py:272
  177.6 25.8 %all-to-all-start.1 = ((bf16[32,24,448]{2,1,0:T(8,128)(2,1)}), bf16[32,24,448]{2,1,0:T(8,128)(2,1)}, u32[]{:S(2)}, u32[]{:S(2)}) async-start(bf16[32,24,448]{2,1,0:T(8,128)(2,1)} %bitcast.159), calls=%async_computation.1 | async-start | bytes 1572864 | tf_op jit(solution)/shard_map/all_to_all | solution.py:951
  205.5 10.4 %collective-permute-start.36 = (bf16[24,4480]{1,0:T(8,128)(2,1)}, bf16[24,4480]{1,0:T(8,128)(2,1)S(1)}, u32[]{:S(2)}, u32[]{:S(2)}) collective-permute-start(bf16[24,4480]{1,0:T(8,128)(2,1)} %shard_map.221.rest_7_), channel_id=1, source_target_pairs={{0,4},{4,8},{8,12},{12,0},{1,5},{5,9},{9,13},{13,1},{2,6},{6,10},{... | collective-permute-start | bytes 645128 | tf_op jit(solution)/shard_map/ppermute | solution.py:251
  206.8 10.6 %collective-permute-start.38 = (bf16[24,4480]{1,0:T(8,128)(2,1)}, bf16[24,4480]{1,0:T(8,128)(2,1)S(1)}, u32[]{:S(2)}, u32[]{:S(2)}) collective-permute-start(bf16[24,4480]{1,0:T(8,128)(2,1)} %shard_map.221.rest_7_), channel_id=1, source_target_pairs={{0,16},{16,0},{1,17},{17,1},{2,18},{18,2},{3,19},{19,3},{4,20},{20... | collective-permute-start | bytes 645128 | tf_op jit(solution)/shard_map/ppermute | solution.py:272
  207.9 16.0 %collective-permute-start.34 = (bf16[24,4480]{1,0:T(8,128)(2,1)}, bf16[24,4480]{1,0:T(8,128)(2,1)S(1)}, u32[]{:S(2)}, u32[]{:S(2)}) collective-permute-start(bf16[24,4480]{1,0:T(8,128)(2,1)} %shard_map.221.rest_7_), channel_id=1, source_target_pairs={{0,8},{4,12},{8,0},{12,4},{1,9},{5,13},{9,1},{13,5},{2,10},{6,14},... | collective-permute-start | bytes 645128 | tf_op jit(solution)/shard_map/ppermute | solution.py:251
  209.0 16.4 %collective-permute-start.32 = (bf16[24,4480]{1,0:T(8,128)(2,1)}, bf16[24,4480]{1,0:T(8,128)(2,1)S(1)}, u32[]{:S(2)}, u32[]{:S(2)}) collective-permute-start(bf16[24,4480]{1,0:T(8,128)(2,1)} %shard_map.221.rest_7_), channel_id=1, source_target_pairs={{0,12},{4,0},{8,4},{12,8},{1,13},{5,1},{9,5},{13,9},{2,14},{6,2},{... | collective-permute-start | bytes 645128 | tf_op jit(solution)/shard_map/ppermute | solution.py:251
  210.9 15.7 %collective-permute-start.31 = (bf16[24,4480]{1,0:T(8,128)(2,1)}, bf16[24,4480]{1,0:T(8,128)(2,1)S(1)}, u32[]{:S(2)}, u32[]{:S(2)}) collective-permute-start(bf16[24,4480]{1,0:T(8,128)(2,1)} %shard_map.221.rest_7_), channel_id=1, source_target_pairs={{0,2},{1,3},{2,0},{3,1},{4,6},{5,7},{6,4},{7,5},{8,10},{9,11},{10,... | collective-permute-start | bytes 645128 | tf_op jit(solution)/shard_map/ppermute | solution.py:272
  215.9 11.9 %collective-permute-start.41 = (bf16[24,4480]{1,0:T(8,128)(2,1)S(1)}, bf16[24,4480]{1,0:T(8,128)(2,1)S(1)}, u32[]{:S(2)}, u32[]{:S(2)}) collective-permute-start(bf16[24,4480]{1,0:T(8,128)(2,1)S(1)} %collective-permute-done.36.rest_10_), channel_id=1, source_target_pairs={{0,16},{16,0},{1,17},{17,1},{2,18},{18,2},{3,19},{19,3},{4,20},{20... | collective-permute-start | bytes 645128 | tf_op jit(solution)/shard_map/ppermute | solution.py:272
  217.4 10.6 %collective-permute-start.37 = (bf16[24,4480]{1,0:T(8,128)(2,1)S(1)}, bf16[24,4480]{1,0:T(8,128)(2,1)S(1)}, u32[]{:S(2)}, u32[]{:S(2)}) collective-permute-start(bf16[24,4480]{1,0:T(8,128)(2,1)S(1)} %collective-permute-done.36.rest_10_), channel_id=1, source_target_pairs={{0,2},{1,3},{2,0},{3,1},{4,6},{5,7},{6,4},{7,5},{8,10},{9,11},{10,... | collective-permute-start | bytes 645128 | tf_op jit(solution)/shard_map/ppermute | solution.py:272
  225.4 8.2 %collective-permute-start.35 = (bf16[24,4480]{1,0:T(8,128)(2,1)S(1)}, bf16[24,4480]{1,0:T(8,128)(2,1)S(1)}, u32[]{:S(2)}, u32[]{:S(2)}) collective-permute-start(bf16[24,4480]{1,0:T(8,128)(2,1)S(1)} %collective-permute-done.34.rest_9_), channel_id=1, source_target_pairs={{0,2},{1,3},{2,0},{3,1},{4,6},{5,7},{6,4},{7,5},{8,10},{9,11},{10,... | collective-permute-start | bytes 645128 | tf_op jit(solution)/shard_map/ppermute | solution.py:272
  226.6 9.0 %collective-permute-start.39 = (bf16[24,4480]{1,0:T(8,128)(2,1)S(1)}, bf16[24,4480]{1,0:T(8,128)(2,1)S(1)}, u32[]{:S(2)}, u32[]{:S(2)}) collective-permute-start(bf16[24,4480]{1,0:T(8,128)(2,1)S(1)} %collective-permute-done.32.rest_8_), channel_id=1, source_target_pairs={{0,16},{16,0},{1,17},{17,1},{2,18},{18,2},{3,19},{19,3},{4,20},{20... | collective-permute-start | bytes 645128 | tf_op jit(solution)/shard_map/ppermute | solution.py:272
  227.8 9.1 %collective-permute-start.33 = (bf16[24,4480]{1,0:T(8,128)(2,1)S(1)}, bf16[24,4480]{1,0:T(8,128)(2,1)S(1)}, u32[]{:S(2)}, u32[]{:S(2)}) collective-permute-start(bf16[24,4480]{1,0:T(8,128)(2,1)S(1)} %collective-permute-done.32.rest_8_), channel_id=1, source_target_pairs={{0,2},{1,3},{2,0},{3,1},{4,6},{5,7},{6,4},{7,5},{8,10},{9,11},{10,... | collective-permute-start | bytes 645128 | tf_op jit(solution)/shard_map/ppermute | solution.py:272
  (53 other events, 519.9 us)
